TPU v7x, 32 devices: a whole 2x2x4 slice. The times are simulated.
32 devices in a mesh: seq: 8 (over y, x, core), mp: 4 (over z).
Axes of the slice: x: 2, y: 2, z: 4, core: 2. Of those that a mesh axis runs over, the one named last changes fastest.
Arguments:
- tokens: bfloat16 [8192, 2048], P(('seq', 'mp'))
- gain_mix: float32 [2048], replicated, may hold values from 0.25 to 1.75
- w_query: bfloat16 [2048, 2048], P(None, 'mp')
- w_key: bfloat16 [2048, 2048], P(None, 'mp')
- w_value: bfloat16 [2048, 4096], P(None, 'mp')
- w_gate: bfloat16 [2048, 4096], P(None, 'mp')
- w_out: bfloat16 [4096, 2048], P('mp')
- gain_ffn: float32 [2048], replicated, may hold values from 0.25 to 1.75
- w_up: bfloat16 [2048, 4096], P(None, 'mp')
- w_down: bfloat16 [4096, 2048], P('mp')
- cotangent: bfloat16 [8192, 2048], P(('seq', 'mp'))
Outputs:
- output: bfloat16 [8192, 2048], P(('seq', 'mp'))
- grad_tokens: bfloat16 [8192, 2048], P(('seq', 'mp'))
- grad_gain_mix: float32 [2048], replicated
- grad_w_query: float32 [2048, 2048], P('seq', 'mp')
- grad_w_key: float32 [2048, 2048], P('seq', 'mp')
- grad_w_value: float32 [2048, 4096], P('seq', 'mp')
- grad_w_gate: float32 [2048, 4096], P('seq', 'mp')
- grad_w_out: float32 [4096, 2048], P(('mp', 'seq'))
- grad_gain_ffn: float32 [2048], replicated
- grad_w_up: float32 [2048, 4096], P('seq', 'mp')
- grad_w_down: float32 [4096, 2048], P(('mp', 'seq'))
All inputs are finite; a program needn't handle non-finite values.
Results may differ from a plain program's by a relative error of at most 0.02.
Values may be sent and summed in bfloat16 or wider, within the bound.
A program may use at most 320 MiB of HBM per device.

v0:
```python
import math

import jax
import jax.numpy as jnp
from jax import lax
from jax.sharding import PartitionSpec as P

DK = 256
DV = 512
STRETCH = 256
SEQ_DEVS = 4


eps = 1e-05


def carried_in(value, axis, join, neutral, backward):
    count = lax.axis_size(axis)
    place = lax.axis_index(axis)
    ahead = count - 1 - place if backward else place
    gathered = jax.tree.map(
        lambda a, kind: lax.all_gather(a.astype(kind), axis), value, (jnp.bfloat16, jnp.bfloat16)
    )
    state = jax.tree.map(lambda a, e: jnp.zeros_like(a) + jnp.asarray(e, a.dtype), value, neutral)

    def one(turn, state):
        source = count - 1 - turn if backward else turn
        return join(
            state,
            jax.tree.map(
                lambda a, own: lax.dynamic_index_in_dim(a, source, 0, False).astype(own.dtype),
                gathered,
                value,
            ),
        )

    return lax.fori_loop(0, ahead, one, state)


def normalize(rows):
    centre = rows - jnp.mean(rows, axis=-1, keepdims=True)
    inverse = lax.rsqrt(jnp.mean(centre * centre, axis=-1, keepdims=True) + eps)
    return (centre * inverse, inverse)


def norm_back(grad_hat, unit, inverse):
    first = jnp.mean(grad_hat, axis=-1, keepdims=True)
    second = jnp.mean(grad_hat * unit, axis=-1, keepdims=True)
    return inverse * (grad_hat - first - unit * second)


def angles(positions):
    half = DK // 2
    freq = jnp.exp(-math.log(10000.0) * jnp.arange(half, dtype=jnp.float32) / (half - 1))
    phase = positions.astype(jnp.float32)[:, None] * freq[None, :]
    return (jnp.cos(phase)[:, None, :], jnp.sin(phase)[:, None, :])


def rotate(values, cosine, sine):
    half = DK // 2
    first = values[..., :half]
    second = values[..., half:]
    return jnp.concatenate(
        [first * cosine - second * sine, second * cosine + first * sine], axis=-1
    )


def to_blocks(rows, heads, width):
    count = rows.shape[0] // STRETCH
    return rows.reshape(count, STRETCH, heads, width).transpose(2, 0, 1, 3)


def from_blocks(blocks):
    heads, count, size, width = blocks.shape
    return blocks.transpose(1, 2, 0, 3).reshape(count * size, heads * width)


def product_t(left, right):
    return lax.dot_general(
        left, right, (((0,), (0,)), ((), ())), preferred_element_type=jnp.float32
    )


def product_rt(left, right):
    return lax.dot_general(
        left, right, (((1,), (1,)), ((), ())), preferred_element_type=jnp.float32
    )


def combine(earlier, later):
    return (earlier[0] * later[0], earlier[1] * later[0][:, None, None] + later[1])


def shards(
    tokens, gain_mix, w_query, w_key, w_value, w_gate, w_out, gain_ffn, w_up, w_down, cotangent
):
    bf16 = jnp.bfloat16
    f32 = jnp.float32
    span_rows = lax.axis_size("mp") * tokens.shape[0]
    local_heads = w_query.shape[1] // DK
    blocks = span_rows // STRETCH
    place = lax.axis_index("seq") % SEQ_DEVS
    resid = tokens.astype(f32)
    unit_mix, inv_mix = normalize(resid)
    normed_mix = (unit_mix * gain_mix).astype(bf16)
    gathered_mix = lax.all_gather(normed_mix, "mp", axis=0, tiled=True)
    query_pre = jnp.dot(gathered_mix, w_query, preferred_element_type=f32)
    key_pre = jnp.dot(gathered_mix, w_key, preferred_element_type=f32)
    value_pre = jnp.dot(gathered_mix, w_value, preferred_element_type=f32)
    gate_pre = jnp.dot(gathered_mix, w_gate, preferred_element_type=f32)
    positions = place * span_rows + jnp.arange(span_rows, dtype=jnp.int32)
    cosine, sine = angles(positions)
    query = rotate(query_pre.reshape(span_rows, local_heads, DK), cosine, sine).astype(bf16)
    keys = rotate(key_pre.reshape(span_rows, local_heads, DK), cosine, sine).astype(bf16)
    q_blk = to_blocks(query.reshape(span_rows, local_heads * DK), local_heads, DK)
    k_blk = to_blocks(keys.reshape(span_rows, local_heads * DK), local_heads, DK)
    v_blk = to_blocks(value_pre.astype(bf16), local_heads, DV)
    heads = (lax.axis_index("mp") * local_heads).astype(f32) + jnp.arange(local_heads, dtype=f32)
    logs = jnp.log1p(-jnp.exp2(-5.0 - heads))
    steps = jnp.arange(STRETCH, dtype=f32)
    gaps = steps[:, None] - steps[None, :]
    mask = jnp.where(gaps >= 0, jnp.exp(logs[:, None, None] * jnp.maximum(gaps, 0.0)), 0.0)
    q_scale = jnp.exp(logs[:, None] * (steps + 1.0))[:, None, :, None]
    k_scale = jnp.exp(logs[:, None] * (STRETCH - 1.0 - steps))[:, None, :, None]
    stretch_decay = jnp.exp(logs * STRETCH)[:, None, None]
    span_decay = jnp.exp(logs * span_rows)
    scores = jnp.einsum("hcik,hcjk->hcij", q_blk, k_blk, preferred_element_type=f32)
    weights = (scores * mask[:, None]).astype(bf16)
    intra = jnp.einsum("hcij,hcjv->hciv", weights, v_blk, preferred_element_type=f32)
    value_dec = (v_blk.astype(f32) * k_scale).astype(bf16)
    query_dec = (q_blk.astype(f32) * q_scale).astype(bf16)
    local_states = jnp.einsum("hcjk,hcjv->hckv", k_blk, value_dec, preferred_element_type=f32)
    span_state = jnp.zeros_like(local_states[:, 0])
    for index in range(blocks):
        span_state = stretch_decay * span_state + local_states[:, index]
    passes = (place < SEQ_DEVS - 1).astype(f32)
    start = (jnp.ones_like(span_decay), jnp.zeros_like(span_state))
    incoming = carried_in((span_decay * passes, span_state * passes), "seq", combine, start, False)[
        1
    ]
    carried_state = incoming
    entering = []
    for index in range(blocks):
        entering.append(carried_state)
        carried_state = stretch_decay * carried_state + local_states[:, index]
    entering = jnp.stack(entering, axis=1).astype(bf16)
    cross = jnp.einsum("hcik,hckv->hciv", query_dec, entering, preferred_element_type=f32)
    mixed = intra + cross
    unit_grp, inv_grp = normalize(mixed)
    unit_rows = from_blocks(unit_grp)
    swish = jax.nn.silu(gate_pre)
    gated = (swish * unit_rows).astype(bf16)
    mixer = lax.psum_scatter(
        jnp.dot(gated, w_out, preferred_element_type=f32).astype(jnp.bfloat16),
        "mp",
        scatter_dimension=0,
        tiled=True,
    ).astype(jnp.float32)
    hidden = resid + mixer
    unit_ffn, inv_ffn = normalize(hidden)
    normed_ffn = (unit_ffn * gain_ffn).astype(bf16)
    gathered_ffn = lax.all_gather(normed_ffn, "mp", axis=0, tiled=True)
    up = jnp.dot(gathered_ffn, w_up, preferred_element_type=f32)
    act = jax.nn.gelu(up, approximate=False).astype(bf16)
    ffn = lax.psum_scatter(
        jnp.dot(act, w_down, preferred_element_type=f32).astype(jnp.bfloat16),
        "mp",
        scatter_dimension=0,
        tiled=True,
    ).astype(jnp.float32)
    output = (hidden + ffn).astype(bf16)
    cot_rows = lax.all_gather(cotangent, "mp", axis=0, tiled=True)
    grad_down = product_t(act, cot_rows)
    grad_act = product_rt(cot_rows, w_down)
    gelu_value, gelu_back = jax.vjp(lambda v: jax.nn.gelu(v, approximate=False), up)
    grad_up = gelu_back(grad_act)[0].astype(bf16)
    grad_up_w = product_t(gathered_ffn, grad_up)
    grad_normed_ffn = lax.psum_scatter(
        product_rt(grad_up, w_up).astype(jnp.bfloat16), "mp", scatter_dimension=0, tiled=True
    ).astype(jnp.float32)
    gain_ffn_part = jnp.sum(grad_normed_ffn * unit_ffn, axis=0)
    grad_hidden = cotangent.astype(f32) + norm_back(grad_normed_ffn * gain_ffn, unit_ffn, inv_ffn)
    hidden_rows = lax.all_gather(grad_hidden.astype(bf16), "mp", axis=0, tiled=True)
    grad_out_w = product_t(gated, hidden_rows)
    grad_gated = product_rt(hidden_rows, w_out)
    silu_value, silu_back = jax.vjp(jax.nn.silu, gate_pre)
    grad_gate = silu_back(grad_gated * unit_rows)[0].astype(bf16)
    grad_unit = to_blocks(grad_gated * swish, local_heads, DV)
    grad_mixed = norm_back(grad_unit, unit_grp, inv_grp).astype(bf16)
    grad_raw = jnp.einsum("hciv,hcjv->hcij", grad_mixed, v_blk, preferred_element_type=f32)
    grad_scores = (grad_raw * mask[:, None]).astype(bf16)
    grad_q = jnp.einsum("hcij,hcjk->hcik", grad_scores, k_blk, preferred_element_type=f32)
    grad_k = jnp.einsum("hcij,hcik->hcjk", grad_scores, q_blk, preferred_element_type=f32)
    grad_v = jnp.einsum("hcij,hciv->hcjv", weights, grad_mixed, preferred_element_type=f32)
    grad_q = grad_q + q_scale * jnp.einsum(
        "hciv,hckv->hcik", grad_mixed, entering, preferred_element_type=f32
    )
    grad_enter = jnp.einsum("hcik,hciv->hckv", query_dec, grad_mixed, preferred_element_type=f32)
    local_grad = jnp.zeros_like(span_state)
    for index in reversed(range(blocks)):
        local_grad = stretch_decay * local_grad + grad_enter[:, index]
    takes = (place > 0).astype(f32)
    leaving = carried_in((span_decay * takes, local_grad * takes), "seq", combine, start, True)[1]
    carried = leaving
    grad_local = [None] * blocks
    for index in reversed(range(blocks)):
        grad_local[index] = carried
        carried = grad_enter[:, index] + stretch_decay * carried
    grad_local = jnp.stack(grad_local, axis=1).astype(bf16)
    grad_k = grad_k + jnp.einsum(
        "hcjv,hckv->hcjk", value_dec, grad_local, preferred_element_type=f32
    )
    grad_v = grad_v + k_scale * jnp.einsum(
        "hcjk,hckv->hcjv", k_blk, grad_local, preferred_element_type=f32
    )
    back_sine = -sine
    grad_query = rotate(from_blocks(grad_q).reshape(span_rows, local_heads, DK), cosine, back_sine)
    grad_query = grad_query.reshape(span_rows, local_heads * DK).astype(bf16)
    grad_key = rotate(from_blocks(grad_k).reshape(span_rows, local_heads, DK), cosine, back_sine)
    grad_key = grad_key.reshape(span_rows, local_heads * DK).astype(bf16)
    grad_value = from_blocks(grad_v).astype(bf16)
    grad_query_w = product_t(gathered_mix, grad_query)
    grad_key_w = product_t(gathered_mix, grad_key)
    grad_value_w = product_t(gathered_mix, grad_value)
    grad_gate_w = product_t(gathered_mix, grad_gate)
    part_mix = product_rt(grad_query, w_query) + product_rt(grad_key, w_key)
    part_mix = part_mix + product_rt(grad_value, w_value) + product_rt(grad_gate, w_gate)
    grad_normed_mix = lax.psum_scatter(
        part_mix.astype(jnp.bfloat16), "mp", scatter_dimension=0, tiled=True
    ).astype(jnp.float32)
    gain_mix_part = jnp.sum(grad_normed_mix * unit_mix, axis=0)
    grad_tokens = (grad_hidden + norm_back(grad_normed_mix * gain_mix, unit_mix, inv_mix)).astype(
        bf16
    )
    gain_mix_sum, gain_ffn_sum = lax.psum((gain_mix_part, gain_ffn_part), ("seq", "mp"))
    summed = (
        lax.psum_scatter(
            grad_query_w.astype(jnp.bfloat16), "seq", scatter_dimension=0, tiled=True
        ).astype(jnp.float32),
        lax.psum_scatter(
            grad_key_w.astype(jnp.bfloat16), "seq", scatter_dimension=0, tiled=True
        ).astype(jnp.float32),
        lax.psum_scatter(
            grad_value_w.astype(jnp.bfloat16), "seq", scatter_dimension=0, tiled=True
        ).astype(jnp.float32),
        lax.psum_scatter(
            grad_gate_w.astype(jnp.bfloat16), "seq", scatter_dimension=0, tiled=True
        ).astype(jnp.float32),
        lax.psum_scatter(
            grad_out_w.astype(jnp.bfloat16), "seq", scatter_dimension=0, tiled=True
        ).astype(jnp.float32),
        lax.psum_scatter(
            grad_up_w.astype(jnp.bfloat16), "seq", scatter_dimension=0, tiled=True
        ).astype(jnp.float32),
        lax.psum_scatter(
            grad_down.astype(jnp.bfloat16), "seq", scatter_dimension=0, tiled=True
        ).astype(jnp.float32),
    )
    final_query, final_key, final_value, final_gate, final_out, final_up, final_down = summed
    return (
        output,
        grad_tokens,
        gain_mix_sum,
        final_query,
        final_key,
        final_value,
        final_gate,
        final_out,
        gain_ffn_sum,
        final_up,
        final_down,
    )


def solution(mesh):
    return jax.shard_map(
        shards,
        mesh=mesh,
        in_specs=(
            P(("seq", "mp"), None),
            P(),
            P(None, "mp"),
            P(None, "mp"),
            P(None, "mp"),
            P(None, "mp"),
            P("mp", None),
            P(),
            P(None, "mp"),
            P("mp", None),
            P(("seq", "mp"), None),
        ),
        out_specs=(
            P(("seq", "mp"), None),
            P(("seq", "mp"), None),
            P(),
            P("seq", "mp"),
            P("seq", "mp"),
            P("seq", "mp"),
            P("seq", "mp"),
            P(("mp", "seq"), None),
            P(),
            P("seq", "mp"),
            P(("mp", "seq"), None),
        ),
        check_vma=False,
    )
```

profile of v0, /device:TPU:0, one launch (start us, length us, event | category | flops | bytes accessed | tf_op | source)
XLA Modules:
  0.0 1246.4 jit_solution(14603131687070515165)
XLA Ops:
  11.1 2.6 fusion.27
  13.9 3.0 fusion.83
  16.9 80.4 %all-gather.9.cloned.1.call-done = bf16[1024,2048]{1,0:T(8,128)(2,1)} async-done(((bf16[256,2048]{1,0:T(8,128)(2,1)}), bf16[1024,2048]{1,0:T(8,128)(2,1)}) %all-gather.9.cloned.1.call-update) | async-done | bytes 4194320 | tf_op jit(solution)/shard_map/all_gather | solution.py:106
  97.3 9.3 convolution_convert_fusion.10
  106.6 4.5 reshape.468
  111.1 5.4 fusion.95
  116.5 2.4 fusion.94
  118.9 2.2 subtract_convert_fusion.2
  124.0 2.7 fusion.53
  130.2 9.2 all-gather
  147.5 2.8 fusion.43
  150.3 15.2 %all-gather.11.cloned.1.call-done = bf16[8,2,256,512]{3,2,1,0:T(8,128)(2,1)} async-done(((bf16[1,2,256,512]{3,2,1,0:T(8,128)(2,1)}), bf16[8,2,256,512]{3,2,1,0:T(8,128)(2,1)}) %all-gather.11.cloned.1.call-update) | async-done | bytes 4194320 | tf_op jit(solution)/shard_map/all_gather | solution.py:22
  165.7 2.2 convert_bitcast_fusion.3
  174.0 3.2 copy.95
  179.9 2.3 copy-done.86
  182.3 6.6 multiply_convert_fusion.1
  190.2 6.0 convolution_convert_fusion.7
  196.4 87.7 %reduce-scatter.12.cloned.1.call-done = bf16[256,2048]{1,0:T(8,128)(2,1)} async-done(((bf16[1024,2048]{1,0:T(8,128)(2,1)}), bf16[256,2048]{1,0:T(8,128)(2,1)}) %reduce-scatter.12.cloned.1.call-update) | async-done | bytes 1048592 | tf_op jit(solution)/shard_map/reduce_scatter | solution.py:153
  289.8 80.6 %all-gather.13.cloned.1.call-done = bf16[1024,2048]{1,0:T(8,128)(2,1)} async-done(((bf16[256,2048]{1,0:T(8,128)(2,1)}), bf16[1024,2048]{1,0:T(8,128)(2,1)}) %all-gather.13.cloned.1.call-update) | async-done | bytes 4194320 | tf_op jit(solution)/shard_map/all_gather | solution.py:162
  370.5 10.1 fusion.96
  380.5 70.8 %all-gather.15.cloned.1.call-done = bf16[1024,2048]{1,0:T(8,128)(2,1)} async-done(((bf16[256,2048]{1,0:T(8,128)(2,1)}), bf16[1024,2048]{1,0:T(8,128)(2,1)}) %all-gather.15.cloned.1.call-update) | async-done | bytes 4194320 | tf_op jit(solution)/shard_map/all_gather | solution.py:172
  451.3 18.7 %add_convert_fusion.1 = (bf16[1024,1024]{1,0:T(8,128)(2,1)S(1)}, f32[1024,1024]{1,0:T(8,128)}) fusion(f32[1024,1024]{1,0:T(8,128)} %fusion.96, bf16[1024,2048]{1,0:T(8,128)(2,1)} %all-gather.15.cloned.1.call-done, bf16[1024,2048]{1,0:T(8,128)(2,1)} %param.24), kind=kOutput, calls=%fused_computation.25 | convolution fusion | flops 4370464768 | bytes 18874368 | tf_op jit(solution)/shard_map/dot_general | solution.py:85
  471.3 6.2 convolution_convert_fusion.5
  477.8 75.2 %reduce-scatter.16.cloned.1.call-done = bf16[256,2048]{1,0:T(8,128)(2,1)} async-done(((bf16[1024,2048]{1,0:T(8,128)(2,1)}), bf16[256,2048]{1,0:T(8,128)(2,1)}) %reduce-scatter.16.cloned.1.call-update) | async-done | bytes 1048592 | tf_op jit(solution)/shard_map/reduce_scatter | solution.py:178
  553.0 3.2 fusion.37
  557.3 4.0 fusion.89
  561.4 81.4 %all-gather.17.cloned.1.call-done = bf16[1024,2048]{1,0:T(8,128)(2,1)} async-done(((bf16[256,2048]{1,0:T(8,128)(2,1)}), bf16[1024,2048]{1,0:T(8,128)(2,1)}) %all-gather.17.cloned.1.call-update) | async-done | bytes 4194320 | tf_op jit(solution)/shard_map/all_gather | solution.py:183
  642.7 14.2 %fusion.78 = (f32[1024,1024]{1,0:T(8,128)}, bf16[1024,1024]{1,0:T(8,128)(2,1)}) fusion(f32[1024,1024]{1,0:T(8,128)} %get-tuple-element.245, f32[1024,1024]{1,0:T(8,128)} %bitcast.283, bf16[1024,2048]{1,0:T(8,128)(2,1)} %all-gather.17.cloned.1.call-done, bf16[1024,2048]{1,0:T(8,128)(2,1)} %param.21), kind=kOutput, calls=%fused_computation.160 | convolution fusion | flops 4308598784 | bytes 23068672 | tf_op jit(solution)/shard_map/dot_general | solution.py:85
  656.9 6.6 reshape.470
  663.6 5.1 bitcast_reduce_fusion
  677.0 4.7 multiply_convert_fusion
  683.0 6.3 convolution_convert_fusion
  689.3 9.5 convolution_convert_fusion.1
  699.0 9.5 convolution_convert_fusion.2
  708.7 8.8 all-gather.1
  717.6 9.4 convolution_convert_fusion.3
  727.1 3.5 multiply_convert_fusion.3
  733.4 2.5 copy.127
  737.4 11.3 while.27
  748.7 2.7 fusion.79
  755.7 2.5 copy.129
  758.2 2.5 copy.128
  760.8 4.1 subtract_convert_fusion
  765.9 3.7 convolution_convert_fusion.9
  770.8 5.9 convolution_convert_fusion.8
  776.8 3.2 fusion.98
  781.1 2.2 copy.113
  785.2 6.2 convolution_convert_fusion.4
  791.9 7.6 fusion.100
  799.5 5.8 fusion.97
  805.3 6.7 fusion.99
  812.0 12.0 add_convert_fusion
  824.3 9.4 convolution_convert_fusion.6
  835.9 2.2 convert_element_type.291
  838.1 38.2 %reduce-scatter.28.cloned.1.call-done = bf16[128,2048]{1,0:T(8,128)(2,1)} async-done(((bf16[1024,2048]{1,0:T(8,128)(2,1)}), bf16[128,2048]{1,0:T(8,128)(2,1)}) %reduce-scatter.28.cloned.1.call-update) | async-done | bytes 524304 | tf_op jit(solution)/shard_map/reduce_scatter | solution.py:249
  878.4 52.8 %reduce-scatter.26.cloned.1.call-done = bf16[256,1024]{1,0:T(8,128)(2,1)} async-done(((bf16[2048,1024]{1,0:T(8,128)(2,1)}), bf16[256,1024]{1,0:T(8,128)(2,1)}) %reduce-scatter.26.cloned.1.call-update) | async-done | bytes 524304 | tf_op jit(solution)/shard_map/reduce_scatter | solution.py:246
  933.4 42.4 %reduce-scatter.20.cloned.1.call-done = bf16[256,512]{1,0:T(8,128)(2,1)} async-done(((bf16[2048,512]{1,0:T(8,128)(2,1)}), bf16[256,512]{1,0:T(8,128)(2,1)}) %reduce-scatter.20.cloned.1.call-update) | async-done | bytes 262160 | tf_op jit(solution)/shard_map/reduce_scatter | solution.py:237
  977.6 42.9 %reduce-scatter.22.cloned.1.call-done = bf16[256,512]{1,0:T(8,128)(2,1)} async-done(((bf16[2048,512]{1,0:T(8,128)(2,1)}), bf16[256,512]{1,0:T(8,128)(2,1)}) %reduce-scatter.22.cloned.1.call-update) | async-done | bytes 262160 | tf_op jit(solution)/shard_map/reduce_scatter | solution.py:240
  1022.3 52.8 %reduce-scatter.24.cloned.1.call-done = bf16[256,1024]{1,0:T(8,128)(2,1)} async-done(((bf16[2048,1024]{1,0:T(8,128)(2,1)}), bf16[256,1024]{1,0:T(8,128)(2,1)}) %reduce-scatter.24.cloned.1.call-update) | async-done | bytes 524304 | tf_op jit(solution)/shard_map/reduce_scatter | solution.py:243
  1077.2 76.9 %reduce-scatter.18.cloned.1.call-done = bf16[256,2048]{1,0:T(8,128)(2,1)} async-done(((bf16[1024,2048]{1,0:T(8,128)(2,1)}), bf16[256,2048]{1,0:T(8,128)(2,1)}) %reduce-scatter.18.cloned.1.call-update) | async-done | bytes 1048592 | tf_op jit(solution)/shard_map/reduce_scatter | solution.py:228
  1154.1 2.2 fusion.39
  1156.3 46.2 %all-reduce = (f32[2048]{0:T(1024)}, f32[2048]{0:T(1024)}) all-reduce(f32[2048]{0:T(1024)S(1)} %get-tuple-element.175, f32[2048]{0:T(1024)S(1)} %copy-done.62), channel_id=1, replica_groups=mesh['seq'=8,'mp'=4] {'seq','mp'}, use_global_device_ids=true, to_apply=%region_21.22 | all-reduce | flops 4096 | bytes 32768 | tf_op jit(solution)/shard_map/psum | solution.py:235
  1202.5 32.1 %reduce-scatter.14.cloned.1.call-done = bf16[256,2048]{1,0:T(8,128)(2,1)} async-done(((bf16[1024,2048]{1,0:T(8,128)(2,1)}), bf16[256,2048]{1,0:T(8,128)(2,1)}) %reduce-scatter.14.cloned.1.call-update) | async-done | bytes 1048592 | tf_op jit(solution)/shard_map/reduce_scatter | solution.py:165
  1234.6 5.1 fusion.31
  (314 shorter events, 84.4 us)
Async XLA Ops:
  7.2 109.3 %copy-start = (bf16[2048,512]{1,0:T(8,128)(2,1)S(1)}, bf16[2048,512]{1,0:T(8,128)(2,1)}, u32[]{:S(2)}) copy-start(bf16[2048,512]{1,0:T(8,128)(2,1)} %param.17) | copy-start | bytes 6291460
  7.2 90.1 %all-gather.9.cloned.1.call-start = ((), (), s32[]{:S(2)}) async-start(), calls=%async_computation.11 | async-start | bytes 5242880 | tf_op jit(solution)/shard_map/all_gather | solution.py:106
  13.7 151.9 %all-gather.11.cloned.1.call-start = ((), (), s32[]{:S(2)}) async-start(), calls=%async_computation.12 | async-start | bytes 4718592 | tf_op jit(solution)/shard_map/all_gather | solution.py:22
  13.8 125.9 %copy-start.79 = (f32[2]{0:T(128)}, f32[2]{0:T(128)S(1)}, u32[]{:S(2)}) copy-start(f32[2]{0:T(128)S(1)} %negate_log-plus-one_fusion) | copy-start | bytes 28
  13.8 92.8 %copy-start.75 = (f32[256]{0:T(256)}, f32[256]{0:T(256)S(1)}, u32[]{:S(2)}) copy-start(f32[256]{0:T(256)S(1)} %get-tuple-element.248) | copy-start | bytes 3076
  13.8 92.7 %copy-start.77 = (f32[256]{0:T(256)}, f32[256]{0:T(256)S(1)}, u32[]{:S(2)}) copy-start(f32[256]{0:T(256)S(1)} %get-tuple-element.249) | copy-start | bytes 3076
  13.9 110.1 %copy-start.67 = (f32[2,256]{1,0:T(2,128)}, f32[2,256]{1,0:T(2,128)S(1)}, u32[]{:S(2)}) copy-start(f32[2,256]{1,0:T(2,128)S(1)} %get-tuple-element.240) | copy-start | bytes 6148
  16.9 102.0 %copy-start.13 = (f32[1024,128]{0,1:T(8,128)}, f32[1024,128]{0,1:T(8,128)S(1)}, u32[]{:S(2)}) copy-start(f32[1024,128]{0,1:T(8,128)S(1)} %get-tuple-element.237) | copy-start | bytes 1572868
  111.1 5.4 copy-start.85
  122.5 4.2 copy-start.19
  124.0 6.1 copy-start.22
  130.1 153.9 %reduce-scatter.12.cloned.1.call-start = ((), (), s32[]{:S(2)}) async-start(), calls=%async_computation.13 | async-start | bytes 5242880 | tf_op jit(solution)/shard_map/reduce_scatter | solution.py:153
  142.0 8.4 copy-start.15
  143.5 6.9 copy-start.17
  143.5 4.0 copy-start.11
  165.7 4.3 copy-start.26
  165.7 4.3 copy-start.28
  177.3 5.0 copy-start.86
  178.3 10.6 copy-start.30
  182.3 8.0 copy-start.82
  196.3 87.8 %copy-start.1 = (bf16[256,2048]{1,0:T(8,128)(2,1)S(1)}, bf16[256,2048]{1,0:T(8,128)(2,1)}, u32[]{:S(2)}) copy-start(bf16[256,2048]{1,0:T(8,128)(2,1)} %param.15) | copy-start | bytes 3145732
  196.3 91.2 %copy-start.57 = (f32[2048]{0:T(1024)S(1)}, f32[2048]{0:T(1024)}, u32[]{:S(2)}) copy-start(f32[2048]{0:T(1024)} %param.22) | copy-start | bytes 24580
  196.3 174.2 %all-gather.13.cloned.1.call-start = ((), (), s32[]{:S(2)}) async-start(), calls=%async_computation.14 | async-start | bytes 5242880 | tf_op jit(solution)/shard_map/all_gather | solution.py:162
  285.8 270.4 %copy-start.60 = (f32[256]{0:T(256)}, f32[256]{0:T(256)S(1)}, u32[]{:S(2)}) copy-start(f32[256]{0:T(256)S(1)} %broadcast_multiply_fusion.7) | copy-start | bytes 3076
  287.5 268.6 %copy-start.65 = (f32[256]{0:T(256)}, f32[256]{0:T(256)S(1)}, u32[]{:S(2)}) copy-start(f32[256]{0:T(256)S(1)} %add_rsqrt_fusion.1) | copy-start | bytes 3076
  289.0 162.3 %all-gather.15.cloned.1.call-start = ((), (), s32[]{:S(2)}) async-start(), calls=%async_computation.16 | async-start | bytes 5242880 | tf_op jit(solution)/shard_map/all_gather | solution.py:172
  289.6 263.4 %reduce-scatter.16.cloned.1.call-start = ((), (), s32[]{:S(2)}) async-start(), calls=%async_computation.17 | async-start | bytes 5242880 | tf_op jit(solution)/shard_map/reduce_scatter | solution.py:178
  451.3 20.0 %copy-start.81 = (bf16[2048,1024]{1,0:T(8,128)(2,1)S(1)}, bf16[2048,1024]{1,0:T(8,128)(2,1)}, u32[]{:S(2)}) copy-start(bf16[2048,1024]{1,0:T(8,128)(2,1)} %param.23) | copy-start | bytes 12582916
  477.5 165.2 %all-gather.17.cloned.1.call-start = ((), (), s32[]{:S(2)}) async-start(), calls=%async_computation.18 | async-start | bytes 5242880 | tf_op jit(solution)/shard_map/all_gather | solution.py:183
  561.3 176.0 %all-gather.19.cloned.1.call-start = ((), (), s32[]{:S(2)}) async-start(), calls=%async_computation.19 | async-start | bytes 4718592 | tf_op jit(solution)/shard_map/all_gather | solution.py:22
  663.6 5.2 copy-start.4
  663.6 5.9 copy-start.5
  676.5 157.2 %reduce-scatter.32.cloned.1.call-start = ((), (), s32[]{:S(2)}) async-start(), calls=%async_computation.27 | async-start | bytes 4718592 | tf_op jit(solution)/shard_map/reduce_scatter | solution.py:255
  677.0 6.0 copy-start.89
  689.3 146.6 %reduce-scatter.30.cloned.1.call-start = ((), (), s32[]{:S(2)}) async-start(), calls=%async_computation.26 | async-start | bytes 4718592 | tf_op jit(solution)/shard_map/reduce_scatter | solution.py:252
  698.8 177.5 %reduce-scatter.28.cloned.1.call-start = ((), (), s32[]{:S(2)}) async-start(), calls=%async_computation.25 | async-start | bytes 4718592 | tf_op jit(solution)/shard_map/reduce_scatter | solution.py:249
  708.6 9.0 copy-start.76
  708.6 9.0 copy-start.78
  708.6 9.0 copy-start.80
  708.6 222.7 %reduce-scatter.26.cloned.1.call-start = ((), (), s32[]{:S(2)}) async-start(), calls=%async_computation.24 | async-start | bytes 4718592 | tf_op jit(solution)/shard_map/reduce_scatter | solution.py:246
  727.0 248.7 %reduce-scatter.20.cloned.1.call-start = ((), (), s32[]{:S(2)}) async-start(), calls=%async_computation.21 | async-start | bytes 2359296 | tf_op jit(solution)/shard_map/reduce_scatter | solution.py:237
  727.1 4.0 copy-start.46
  727.1 4.2 copy-start.56
  754.2 6.5 copy-start.14
  754.2 6.5 copy-start.33
  760.8 5.1 copy-start.87
  769.6 250.9 %reduce-scatter.22.cloned.1.call-start = ((), (), s32[]{:S(2)}) async-start(), calls=%async_computation.22 | async-start | bytes 2359296 | tf_op jit(solution)/shard_map/reduce_scatter | solution.py:240
  776.7 298.3 %reduce-scatter.24.cloned.1.call-start = ((), (), s32[]{:S(2)}) async-start(), calls=%async_computation.23 | async-start | bytes 4718592 | tf_op jit(solution)/shard_map/reduce_scatter | solution.py:243
  781.1 4.1 copy-start.88
  791.4 362.7 %reduce-scatter.18.cloned.1.call-start = ((), (), s32[]{:S(2)}) async-start(), calls=%async_computation.20 | async-start | bytes 5242880 | tf_op jit(solution)/shard_map/reduce_scatter | solution.py:228
  791.9 7.6 copy-start.40
  799.5 5.8 copy-start.38
  799.5 5.8 copy-start.84
  824.0 410.6 %reduce-scatter.14.cloned.1.call-start = ((), (), s32[]{:S(2)}) async-start(), calls=%async_computation.15 | async-start | bytes 5242880 | tf_op jit(solution)/shard_map/reduce_scatter | solution.py:165
  835.8 318.3 %copy-start.2 = (bf16[256,2048]{1,0:T(8,128)(2,1)S(1)}, bf16[256,2048]{1,0:T(8,128)(2,1)}, u32[]{:S(2)}) copy-start(bf16[256,2048]{1,0:T(8,128)(2,1)} %param.15) | copy-start | bytes 3145732
  835.8 318.3 %copy-start.59 = (f32[2048]{0:T(1024)S(1)}, f32[2048]{0:T(1024)}, u32[]{:S(2)}) copy-start(f32[2048]{0:T(1024)} %param.16) | copy-start | bytes 24580
  835.8 318.3 %copy-start.64 = (f32[256]{0:T(256)S(1)}, f32[256]{0:T(256)}, u32[]{:S(2)}) copy-start(f32[256]{0:T(256)} %copy-done.63) | copy-start | bytes 3076
  835.8 318.3 %copy-start.70 = (f32[256]{0:T(256)S(1)}, f32[256]{0:T(256)}, u32[]{:S(2)}) copy-start(f32[256]{0:T(256)} %copy-done.69) | copy-start | bytes 3076
  838.1 318.2 %copy-start.62 = (f32[2048]{0:T(1024)S(1)}, f32[2048]{0:T(1024)}, u32[]{:S(2)}) copy-start(f32[2048]{0:T(1024)} %get-tuple-element.173) | copy-start | bytes 24580
  838.1 396.5 %copy-start.58 = (f32[2048]{0:T(1024)S(1)}, f32[2048]{0:T(1024)}, u32[]{:S(2)}) copy-start(f32[2048]{0:T(1024)} %param.22) | copy-start | bytes 24580
  838.1 396.5 %copy-start.61 = (f32[256]{0:T(256)S(1)}, f32[256]{0:T(256)}, u32[]{:S(2)}) copy-start(f32[256]{0:T(256)} %copy-done.60) | copy-start | bytes 3076
  838.1 396.5 %copy-start.66 = (f32[256]{0:T(256)S(1)}, f32[256]{0:T(256)}, u32[]{:S(2)}) copy-start(f32[256]{0:T(256)} %copy-done.65) | copy-start | bytes 3076
  838.1 396.5 %copy-start.72 = (f32[256]{0:T(256)S(1)}, f32[256]{0:T(256)}, u32[]{:S(2)}) copy-start(f32[256]{0:T(256)} %copy-done.71) | copy-start | bytes 3076
  838.1 396.5 %copy-start.74 = (f32[256]{0:T(256)S(1)}, f32[256]{0:T(256)}, u32[]{:S(2)}) copy-start(f32[256]{0:T(256)} %copy-done.73) | copy-start | bytes 3076
  (45 other events, 103.4 us)
Sparse Core Ops, SparseCore 0:
  13.8 83.4 all-gather.8
  130.3 35.2 all-gather.10
  196.4 87.6 reduce-scatter.11
  289.1 81.2 all-gather.12
  371.9 79.2 all-gather.14
  477.6 75.2 reduce-scatter.15
  561.4 81.2 all-gather.16
  676.6 35.2 all-gather.18
  715.3 51.3 reduce-scatter.31
  770.2 51.3 reduce-scatter.29
  824.9 51.3 reduce-scatter.27
  879.9 51.3 reduce-scatter.25
  934.5 41.1 reduce-scatter.19
  979.3 41.2 reduce-scatter.21
  1023.7 51.3 reduce-scatter.23
  1077.3 76.7 reduce-scatter.17
  1156.3 78.2 reduce-scatter.13
where the time goes:
time: 1260 us; the launch traced here: 1250 us
  waiting for transfers between devices  830 us (66%)
  matrix products  191 us (15%)
  other arithmetic  83.5 us (7%)
  blocking collectives  64.2 us (5%)
  local copies, waits for them, and re-layouts  59.9 us (5%)
  between operations  15.4 us (1%)
    reduce_scatter x1, waiting for transfers between devices, shards(): lax.psum_scatter(jnp.dot(gated, w_out, preferred_element_type=f32).astype...  87.7 us
    all_gather x1, waiting for transfers between devices, shards(): lax.all_gather(grad_hidden.astype(bf16), 'mp', axis=0, tiled=True)  81.4 us
    all_gather x1, waiting for transfers between devices, shards(): gathered_ffn = lax.all_gather(normed_ffn, 'mp', axis=0, tiled=True)  80.6 us
    all_gather x1, waiting for transfers between devices, shards(): gathered_mix = lax.all_gather(normed_mix, 'mp', axis=0, tiled=True)  80.4 us
    reduce_scatter x1, waiting for transfers between devices, shards(): lax.psum_scatter(part_mix.astype(jnp.bfloat16), 'mp', scatter_dimension=0...  76.9 us
    reduce_scatter x1, waiting for transfers between devices, shards(): lax.psum_scatter(product_rt(grad_up, w_up).astype(jnp.bfloat16), 'mp', sc...  75.2 us
    dot_general x7, matrix products, product_rt(): lax.dot_general(left, right, (((1,), (1,)), ((), ())), preferred_element_...  71.2 us
    all_gather x1, waiting for transfers between devices, shards(): cot_rows = lax.all_gather(cotangent, 'mp', axis=0, tiled=True)  70.8 us
  transfers between devices with their start and end apart: 17, of which 14 were waited for; matrix products, arithmetic and copies ran while one was open for 14% of the time, Pallas kernels for 0%

commit v1 on v0

--- a/solution.py
+++ b/solution.py
@@ -14,27 +14,86 @@
 eps = 1e-05
 
 
-def carried_in(value, axis, join, neutral, backward):
-    count = lax.axis_size(axis)
-    place = lax.axis_index(axis)
-    ahead = count - 1 - place if backward else place
-    gathered = jax.tree.map(
-        lambda a, kind: lax.all_gather(a.astype(kind), axis), value, (jnp.bfloat16, jnp.bfloat16)
-    )
-    state = jax.tree.map(lambda a, e: jnp.zeros_like(a) + jnp.asarray(e, a.dtype), value, neutral)
-
-    def one(turn, state):
-        source = count - 1 - turn if backward else turn
-        return join(
-            state,
-            jax.tree.map(
-                lambda a, own: lax.dynamic_index_in_dim(a, source, 0, False).astype(own.dtype),
-                gathered,
-                value,
-            ),
-        )
-
-    return lax.fori_loop(0, ahead, one, state)
+def carried_in(state, decay, place, backward):
+    count = lax.axis_size("seq")
+    groups = [list(range(i, i + SEQ_DEVS)) for i in range(0, count, SEQ_DEVS)]
+    gathered = lax.all_gather(state.astype(jnp.bfloat16), "seq", axis_index_groups=groups)
+    total = jnp.zeros_like(state)
+    for other in range(SEQ_DEVS):
+        hops = other - place - 1 if backward else place - other - 1
+        weight = jnp.where(hops >= 0, decay ** jnp.maximum(hops, 0).astype(jnp.float32), 0.0)
+        total = total + weight[:, None, None] * gathered[other].astype(jnp.float32)
+    return total
+
+
+def core_swap(value):
+    count = lax.axis_size("seq")
+    return lax.ppermute(value, "seq", [(i, i ^ 1) for i in range(count)])
+
+
+def mp_swap(value, bit):
+    count = lax.axis_size("mp")
+    return lax.ppermute(value, "mp", [(i, i ^ bit) for i in range(count)])
+
+
+def same_core():
+    count = lax.axis_size("seq")
+    return [list(range(core, count, 2)) for core in range(2)]
+
+
+def group_rows(own):
+    chip = jnp.concatenate([own, mp_swap(own, 1)], axis=0)
+    return jnp.concatenate([chip, core_swap(chip)], axis=0)
+
+
+def group_sum(part):
+    f32, bf16 = jnp.float32, jnp.bfloat16
+    rows = part.shape[0] // 4
+    keep = part[: 2 * rows] + core_swap(part[2 * rows :].astype(bf16)).astype(f32)
+    return keep[:rows] + mp_swap(keep[rows:].astype(bf16), 1).astype(f32)
+
+
+def far_shard(weight):
+    rows = weight.shape[0] // lax.axis_size("seq")
+    piece = lax.dynamic_slice_in_dim(weight, lax.axis_index("seq") * rows, rows, 0)
+    return lax.all_gather(mp_swap(piece, 2), "seq", axis=0, tiled=True)
+
+
+def scatter_pair(grad):
+    f32, bf16 = jnp.float32, jnp.bfloat16
+    count = lax.axis_size("seq")
+    core = lax.axis_index("seq") % 2
+    parts = grad.astype(bf16).reshape(count // 2, 2, grad.shape[0] // count, grad.shape[1])
+    away = lax.dynamic_index_in_dim(parts, 1 - core, 1, False)
+    kept = lax.dynamic_index_in_dim(parts, core, 1, False)
+    total = (kept.astype(f32) + core_swap(away).astype(f32)).astype(bf16)
+    total = total.reshape(grad.shape[0] // 2, grad.shape[1])
+    return lax.psum_scatter(
+        total, "seq", scatter_dimension=0, tiled=True, axis_index_groups=same_core()
+    ).astype(f32)
+
+
+def scatter_far(grad):
+    f32, bf16 = jnp.float32, jnp.bfloat16
+    count, depth = lax.axis_size("seq"), lax.axis_size("mp")
+    core = lax.axis_index("seq") % 2
+    part = lax.psum_scatter(
+        grad.astype(bf16), "seq", scatter_dimension=0, tiled=True, axis_index_groups=same_core()
+    )
+    half = part.shape[0] // 2
+    first, second = part[:half], part[half:]
+    crossed, straight = [], []
+    for s in range(count):
+        for z in range(depth):
+            here = s * depth + z
+            if s % 2 == 0:
+                crossed.append((here, (s + 1) * depth + z))
+            else:
+                crossed.append((here, (s - 1) * depth + (z ^ 2)))
+                straight.append((here, s * depth + (z ^ 2)))
+    one = lax.ppermute(jnp.where(core == 0, second, first), ("seq", "mp"), crossed)
+    two = lax.ppermute(second, ("seq", "mp"), straight)
+    return one.astype(f32) + jnp.where(core == 0, first, two).astype(f32)
 
 
 def normalize(rows):
@@ -85,10 +144,6 @@
     return lax.dot_general(
         left, right, (((1,), (1,)), ((), ())), preferred_element_type=jnp.float32
     )
-
-
-def combine(earlier, later):
-    return (earlier[0] * later[0], earlier[1] * later[0][:, None, None] + later[1])
 
 
 def shards(
@@ -100,10 +155,14 @@
     local_heads = w_query.shape[1] // DK
     blocks = span_rows // STRETCH
     place = lax.axis_index("seq") % SEQ_DEVS
+    core = lax.axis_index("seq") % 2
     resid = tokens.astype(f32)
     unit_mix, inv_mix = normalize(resid)
     normed_mix = (unit_mix * gain_mix).astype(bf16)
     gathered_mix = lax.all_gather(normed_mix, "mp", axis=0, tiled=True)
+    w_up = jnp.where(core == 0, w_up, far_shard(w_up))
+    w_down = jnp.where(core == 0, w_down, far_shard(w_down))
+    cot_rows = group_rows(cotangent)
     query_pre = jnp.dot(gathered_mix, w_query, preferred_element_type=f32)
     key_pre = jnp.dot(gathered_mix, w_key, preferred_element_type=f32)
     value_pre = jnp.dot(gathered_mix, w_value, preferred_element_type=f32)
@@ -133,11 +192,7 @@
     span_state = jnp.zeros_like(local_states[:, 0])
     for index in range(blocks):
         span_state = stretch_decay * span_state + local_states[:, index]
-    passes = (place < SEQ_DEVS - 1).astype(f32)
-    start = (jnp.ones_like(span_decay), jnp.zeros_like(span_state))
-    incoming = carried_in((span_decay * passes, span_state * passes), "seq", combine, start, False)[
-        1
-    ]
+    incoming = carried_in(span_state, span_decay, place, False)
     carried_state = incoming
     entering = []
     for index in range(blocks):
@@ -159,25 +214,16 @@
     hidden = resid + mixer
     unit_ffn, inv_ffn = normalize(hidden)
     normed_ffn = (unit_ffn * gain_ffn).astype(bf16)
-    gathered_ffn = lax.all_gather(normed_ffn, "mp", axis=0, tiled=True)
+    gathered_ffn = group_rows(normed_ffn)
     up = jnp.dot(gathered_ffn, w_up, preferred_element_type=f32)
     act = jax.nn.gelu(up, approximate=False).astype(bf16)
-    ffn = lax.psum_scatter(
-        jnp.dot(act, w_down, preferred_element_type=f32).astype(jnp.bfloat16),
-        "mp",
-        scatter_dimension=0,
-        tiled=True,
-    ).astype(jnp.float32)
-    output = (hidden + ffn).astype(bf16)
-    cot_rows = lax.all_gather(cotangent, "mp", axis=0, tiled=True)
+    output = (hidden + group_sum(jnp.dot(act, w_down, preferred_element_type=f32))).astype(bf16)
     grad_down = product_t(act, cot_rows)
     grad_act = product_rt(cot_rows, w_down)
     gelu_value, gelu_back = jax.vjp(lambda v: jax.nn.gelu(v, approximate=False), up)
     grad_up = gelu_back(grad_act)[0].astype(bf16)
     grad_up_w = product_t(gathered_ffn, grad_up)
-    grad_normed_ffn = lax.psum_scatter(
-        product_rt(grad_up, w_up).astype(jnp.bfloat16), "mp", scatter_dimension=0, tiled=True
-    ).astype(jnp.float32)
+    grad_normed_ffn = group_sum(product_rt(grad_up, w_up))
     gain_ffn_part = jnp.sum(grad_normed_ffn * unit_ffn, axis=0)
     grad_hidden = cotangent.astype(f32) + norm_back(grad_normed_ffn * gain_ffn, unit_ffn, inv_ffn)
     hidden_rows = lax.all_gather(grad_hidden.astype(bf16), "mp", axis=0, tiled=True)
@@ -199,8 +245,7 @@
     local_grad = jnp.zeros_like(span_state)
     for index in reversed(range(blocks)):
         local_grad = stretch_decay * local_grad + grad_enter[:, index]
-    takes = (place > 0).astype(f32)
-    leaving = carried_in((span_decay * takes, local_grad * takes), "seq", combine, start, True)[1]
+    leaving = carried_in(local_grad, span_decay, place, True)
     carried = leaving
     grad_local = [None] * blocks
     for index in reversed(range(blocks)):
@@ -219,10 +264,8 @@
     grad_key = rotate(from_blocks(grad_k).reshape(span_rows, local_heads, DK), cosine, back_sine)
     grad_key = grad_key.reshape(span_rows, local_heads * DK).astype(bf16)
     grad_value = from_blocks(grad_v).astype(bf16)
-    grad_query_w = product_t(gathered_mix, grad_query)
-    grad_key_w = product_t(gathered_mix, grad_key)
-    grad_value_w = product_t(gathered_mix, grad_value)
-    grad_gate_w = product_t(gathered_mix, grad_gate)
+    grad_in = jnp.concatenate([grad_query, grad_key, grad_value, grad_gate], axis=1)
+    grad_in_w = scatter_pair(product_t(gathered_mix, grad_in))
     part_mix = product_rt(grad_query, w_query) + product_rt(grad_key, w_key)
     part_mix = part_mix + product_rt(grad_value, w_value) + product_rt(grad_gate, w_gate)
     grad_normed_mix = lax.psum_scatter(
@@ -233,30 +276,14 @@
         bf16
     )
     gain_mix_sum, gain_ffn_sum = lax.psum((gain_mix_part, gain_ffn_part), ("seq", "mp"))
-    summed = (
-        lax.psum_scatter(
-            grad_query_w.astype(jnp.bfloat16), "seq", scatter_dimension=0, tiled=True
-        ).astype(jnp.float32),
-        lax.psum_scatter(
-            grad_key_w.astype(jnp.bfloat16), "seq", scatter_dimension=0, tiled=True
-        ).astype(jnp.float32),
-        lax.psum_scatter(
-            grad_value_w.astype(jnp.bfloat16), "seq", scatter_dimension=0, tiled=True
-        ).astype(jnp.float32),
-        lax.psum_scatter(
-            grad_gate_w.astype(jnp.bfloat16), "seq", scatter_dimension=0, tiled=True
-        ).astype(jnp.float32),
-        lax.psum_scatter(
-            grad_out_w.astype(jnp.bfloat16), "seq", scatter_dimension=0, tiled=True
-        ).astype(jnp.float32),
-        lax.psum_scatter(
-            grad_up_w.astype(jnp.bfloat16), "seq", scatter_dimension=0, tiled=True
-        ).astype(jnp.float32),
-        lax.psum_scatter(
-            grad_down.astype(jnp.bfloat16), "seq", scatter_dimension=0, tiled=True
-        ).astype(jnp.float32),
-    )
-    final_query, final_key, final_value, final_gate, final_out, final_up, final_down = summed
+    wide = w_query.shape[1]
+    tall = w_value.shape[1]
+    final_query, final_key, final_value, final_gate = jnp.split(
+        grad_in_w, [wide, 2 * wide, 2 * wide + tall], axis=1
+    )
+    final_out = scatter_pair(grad_out_w)
+    final_up = scatter_far(grad_up_w)
+    final_down = scatter_far(grad_down)
     return (
         output,
         grad_tokens,

time: 1260 us -> 963 us (0.76)
  waiting for transfers between devices: 830 us -> 510 us
  local copies, waits for them, and re-layouts: 59.9 us -> 87.4 us
  blocking collectives: 64.2 us -> 39.4 us
  starting transfers between devices: 2.24 us -> 21.5 us
    reduce_scatter x9 -> x4, waiting for transfers between devices: 336 us -> 21.7 us  [the longest x2 21.6 us: scatter_pair(): lax.psum_scatter(total, 'seq', scatter_dimension=0, tiled=True, axis_inde...]
    ppermute x0 -> x16, waiting for transfers between devices: none -> 262 us  [the longest x6 144 us: mp_swap(): return lax.ppermute(value, 'mp', [(i, i ^ bit) for i in range(count)])]
    all_gather x4, waiting for transfers between devices: 167 us -> 19.3 us  [the longest x2 9.92 us: carried_in(): lax.all_gather(state.astype(jnp.bfloat16), 'seq', axis_index_groups=groups)]
    reduce_scatter x1, waiting for transfers between devices: 76.9 us -> 0.01 us  [shards(): lax.psum_scatter(part_mix.astype(jnp.bfloat16), 'mp', scatter_dimension=0...]
    reduce_scatter x1, waiting for transfers between devices: 87.7 us -> 44.9 us  [shards(): lax.psum_scatter(jnp.dot(gated, w_out, preferred_element_type=f32).astype...]
    ppermute x0 -> x16, starting transfers between devices: none -> 20.2 us  [the longest x6 8.68 us: mp_swap(): return lax.ppermute(value, 'mp', [(i, i ^ bit) for i in range(count)])]
    all_gather x2 -> x0, blocking collectives: 18 us -> none  [carried_in(): lax.all_gather(a.astype(kind), axis)]
    dot_general x7 -> x4, matrix products: 50.5 us -> 45.6 us  [product_t(): lax.dot_general(left, right, (((0,), (0,)), ((), ())), preferred_element_...]
  transfers between devices with their start and end apart: 17 -> 28, of which waited for: 14 -> 15; matrix products, arithmetic and copies ran while one was open for 14% -> 23% of each run, Pallas kernels for 0% -> 0%
where the time goes in v1:
time: 963 us; the launch traced here: 952 us
  waiting for transfers between devices  510 us (53%)
  matrix products  192 us (20%)
  local copies, waits for them, and re-layouts  87.4 us (9%)
  other arithmetic  85.6 us (9%)
  blocking collectives  39.4 us (4%)
  starting transfers between devices  21.5 us (2%)
  between operations  17 us (2%)
    ppermute x6, waiting for transfers between devices, mp_swap(): return lax.ppermute(value, 'mp', [(i, i ^ bit) for i in range(count)])  144 us
    ppermute x2, waiting for transfers between devices, scatter_far(): lax.ppermute(jnp.where(core == 0, second, first), ('seq', 'mp'), crossed)  107 us
    all_gather x1, waiting for transfers between devices, shards(): lax.all_gather(grad_hidden.astype(bf16), 'mp', axis=0, tiled=True)  80.9 us
    all_gather x1, waiting for transfers between devices, shards(): gathered_mix = lax.all_gather(normed_mix, 'mp', axis=0, tiled=True)  80.4 us
    dot_general x7, matrix products, product_rt(): lax.dot_general(left, right, (((1,), (1,)), ((), ())), preferred_element_...  64.9 us
    dot_general x4, matrix products, product_t(): lax.dot_general(left, right, (((0,), (0,)), ((), ())), preferred_element_...  45.6 us
    reduce_scatter x1, waiting for transfers between devices, shards(): lax.psum_scatter(jnp.dot(gated, w_out, preferred_element_type=f32).astype...  44.9 us
    psum x1, blocking collectives, shards(): lax.psum((gain_mix_part, gain_ffn_part), ('seq', 'mp'))  39.4 us
  transfers between devices with their start and end apart: 28, of which 15 were waited for; matrix products, arithmetic and copies ran while one was open for 23% of the time, Pallas kernels for 0%

profile of v1, /device:TPU:0, one launch (start us, length us, event | category | flops | bytes accessed | tf_op | source)
XLA Modules:
  0.0 952.2 jit_solution(14578812332762699062)
XLA Ops:
  11.9 2.6 fusion.33
  14.8 3.0 fusion.91
  17.7 80.4 %all-gather.7.cloned.1.call-done = bf16[1024,2048]{1,0:T(8,128)(2,1)} async-done(((bf16[256,2048]{1,0:T(8,128)(2,1)}), bf16[1024,2048]{1,0:T(8,128)(2,1)}) %all-gather.7.cloned.1.call-update) | async-done | bytes 4194320 | tf_op jit(solution)/shard_map/all_gather | solution.py:162
  98.1 9.3 convolution_convert_fusion.5
  107.4 4.5 reshape.642
  111.9 5.4 fusion.116
  124.8 2.7 fusion.56
  139.6 2.7 fusion.46
  142.3 9.9 %all-gather.9.cloned.1.call-done = bf16[4,2,256,512]{3,2,1,0:T(8,128)(2,1)} async-done(((bf16[1,2,256,512]{3,2,1,0:T(8,128)(2,1)}), bf16[4,2,256,512]{3,2,1,0:T(8,128)(2,1)}) %all-gather.9.cloned.1.call-update) | async-done | bytes 2097168 | tf_op jit(solution)/shard_map/all_gather | solution.py:20
  164.1 5.2 copy.63
  169.3 3.4 copy.100
  174.8 7.2 multiply_convert_fusion.1
  182.0 7.8 convolution_convert_fusion.4
  191.1 2.5 collective-permute-start.2
  193.6 57.3 %collective-permute-done.2 = bf16[256,1024]{1,0:T(8,128)(2,1)} collective-permute-done((bf16[256,1024]{1,0:T(8,128)(2,1)S(1)}, bf16[256,1024]{1,0:T(8,128)(2,1)}, u32[]{:S(2)}, u32[]{:S(2)}) %collective-permute-start.2) | collective-permute-done | bytes 524320 | tf_op jit(solution)/shard_map/ppermute | solution.py:36
  251.2 44.9 %reduce-scatter.7.cloned.1.call-done = bf16[256,2048]{1,0:T(8,128)(2,1)} async-done(((bf16[1024,2048]{1,0:T(8,128)(2,1)}), bf16[256,2048]{1,0:T(8,128)(2,1)}) %reduce-scatter.7.cloned.1.call-update) | async-done | bytes 1048592 | tf_op jit(solution)/shard_map/reduce_scatter | solution.py:208
  301.0 3.2 pad_maximum_fusion.3
  304.4 22.2 %collective-permute-done = bf16[256,2048]{1,0:T(8,128)(2,1)} collective-permute-done((bf16[256,2048]{1,0:T(8,128)(2,1)}, bf16[256,2048]{1,0:T(8,128)(2,1)}, u32[]{:S(2)}, u32[]{:S(2)}) %collective-permute-start) | collective-permute-done | bytes 1048608 | tf_op jit(solution)/shard_map/ppermute | solution.py:36
  326.6 3.1 pad_maximum_fusion.2
  330.7 3.1 collective-permute-start.3
  333.8 23.9 %collective-permute-done.3 = bf16[128,2048]{1,0:T(8,128)(2,1)} collective-permute-done((bf16[128,2048]{1,0:T(8,128)(2,1)S(1)}, bf16[128,2048]{1,0:T(8,128)(2,1)}, u32[]{:S(2)}, u32[]{:S(2)}) %collective-permute-start.3) | collective-permute-done | bytes 524320 | tf_op jit(solution)/shard_map/ppermute | solution.py:36
  362.4 3.1 constant_dynamic-update-slice_fusion
  365.6 19.6 %multiply_convert_fusion = (bf16[1024,1024]{0,1:T(8,128)(2,1)}, f32[1024,1024]{0,1:T(8,128)}, f32[1024,1024]{0,1:T(8,128)}) fusion(bf16[2048,1024]{1,0:T(8,128)(2,1)} %param.19, bf16[2048,1024]{1,0:T(8,128)(2,1)} %all-gather.11.cloned.1.call-done, pred[]{:T(512)S(6)} %eq.15, bf16[512,2048]{1,0:T(8,128)(2,1)} %collective-permute-done.1, ...), kind=kOutput, calls=%fused_computation.38 | convolution fusion | flops 4377804800 | bytes 23068672 | tf_op jit(solution)/shard_map/dot_general | solution.py:218
  385.2 9.4 all-gather.13.cloned.1.call-done
  394.6 12.9 %add_convert_fusion.1 = bf16[1024,1024]{0,1:T(8,128)(2,1)} fusion(f32[1024,1024]{0,1:T(8,128)} %get-tuple-element.27, f32[1024,1024]{0,1:T(8,128)} %get-tuple-element.77, bf16[1024,2048]{1,0:T(8,128)(2,1)} %constant_dynamic-update-slice_fusion, bf16[1024,2048]{1,0:T(8,128)(2,1)} %param.20, bf16[1024,2048]{1,0:T(8,128)(2,1)} %all-gather.13.cloned.1.call-done, ...), kind=kOutput, calls=%fused_computation.37 | convolution fusion | flops 4311744512 | bytes 23068672 | tf_op jit(solution)/shard_map/dot_general | solution.py:144
  407.5 6.2 fusion.63
  415.9 6.6 fusion.65
  422.8 2.8 collective-permute-start.4
  432.0 20.8 %collective-permute-done.9 = bf16[256,2048]{1,0:T(8,128)(2,1)S(1)} collective-permute-done((bf16[256,2048]{1,0:T(8,128)(2,1)S(1)}, bf16[256,2048]{1,0:T(8,128)(2,1)S(1)}, u32[]{:S(2)}, u32[]{:S(2)}) %collective-permute-start.9) | collective-permute-done | bytes 1048608 | tf_op jit(solution)/shard_map/ppermute | solution.py:36
  454.4 19.9 %collective-permute-done.5 = bf16[256,2048]{1,0:T(8,128)(2,1)S(1)} collective-permute-done((bf16[256,2048]{1,0:T(8,128)(2,1)S(1)}, bf16[256,2048]{1,0:T(8,128)(2,1)S(1)}, u32[]{:S(2)}, u32[]{:S(2)}) %collective-permute-start.5) | collective-permute-done | bytes 1048608 | tf_op jit(solution)/shard_map/ppermute | solution.py:36
  474.3 3.1 fusion.103
  477.4 80.9 %all-gather.15.cloned.1.call-done = bf16[1024,2048]{1,0:T(8,128)(2,1)} async-done(((bf16[256,2048]{1,0:T(8,128)(2,1)}), bf16[1024,2048]{1,0:T(8,128)(2,1)}) %all-gather.15.cloned.1.call-update) | async-done | bytes 4194320 | tf_op jit(solution)/shard_map/all_gather | solution.py:229
  558.3 14.2 %fusion.88 = (f32[1024,1024]{0,1:T(8,128)}, bf16[1024,1024]{0,1:T(8,128)(2,1)}) fusion(f32[1024,1024]{0,1:T(8,128)} %get-tuple-element.76, f32[1024,1024]{0,1:T(8,128)} %bitcast.272, bf16[1024,2048]{1,0:T(8,128)(2,1)} %all-gather.15.cloned.1.call-done, bf16[1024,2048]{1,0:T(8,128)(2,1)} %param.17), kind=kOutput, calls=%fused_computation.187 | convolution fusion | flops 4308598784 | bytes 23068672 | tf_op jit(solution)/shard_map/dot_general | solution.py:144
  572.4 5.8 reshape.644
  578.2 5.2 copy.68
  583.4 4.6 bitcast_reduce_fusion
  596.5 9.4 convolution_convert_fusion.2
  606.0 9.3 convolution_convert_fusion.1
  616.0 7.4 convolution_convert_fusion.3
  631.7 2.5 copy.97
  634.2 2.6 copy.96
  636.8 4.8 fusion.118
  641.6 6.9 fusion.120
  648.5 3.7 fusion.12
  652.3 3.3 add_convert_fusion.3
  661.5 2.5 copy.99
  664.0 2.5 copy.98
  666.5 4.9 fusion.14
  671.4 4.3 copy.83
  680.6 6.1 fusion.117
  686.7 6.9 fusion.119
  693.6 11.8 %add_convert_fusion = bf16[1024,2048]{1,0:T(8,128)(2,1)} fusion(f32[1024,2048]{1,0:T(8,128)S(1)} %bitcast.252, f32[1024,2048]{1,0:T(8,128)} %fusion.119, f32[1024,2048]{1,0:T(8,128)} %fusion.117, bf16[1024,512]{0,1:T(8,128)(2,1)} %bitcast.269, bf16[2048,512]{1,0:T(8,128)(2,1)} %param.14), kind=kOutput, calls=%fused_computation.3 | convolution fusion | flops 2155872256 | bytes 32505856 | tf_op jit(solution)/shard_map/dot_general | solution.py:144
  706.6 19.5 %convolution_convert_fusion = bf16[2048,3072]{1,0:T(8,128)(2,1)} fusion(bf16[1024,2048]{1,0:T(8,128)(2,1)} %all-gather.7.cloned.1.call-done, bf16[1024,1024]{0,1:T(8,128)(2,1)} %get-tuple-element.33, bf16[1024,1024]{0,1:T(8,128)(2,1)} %bitcast.276, bf16[1024,512]{0,1:T(8,128)(2,1)S(1)} %bitcast.270, bf16[1024,512]{0,1:T(8,128)(2,1)} %bitcast.279), kind=kOutput, calls=%fused_computation.2 | convolution fusion | flops 12916359168 | bytes 23068672 | tf_op jit(solution)/shard_map/dot_general | solution.py:138
  726.1 3.2 dynamic-slice_bitcast_fusion
  729.4 10.3 %collective-permute-done.10 = bf16[4,256,3072]{2,1,0:T(8,128)(2,1)} collective-permute-done((bf16[4,256,3072]{2,1,0:T(8,128)(2,1)S(1)}, bf16[4,256,3072]{2,1,0:T(8,128)(2,1)}, u32[]{:S(2)}, u32[]{:S(2)}) %collective-permute-start.10) | collective-permute-done | bytes 6291488 | tf_op jit(solution)/shard_map/ppermute | solution.py:31
  739.7 10.1 %fusion = bf16[4,256,3072]{2,1,0:T(8,128)(2,1)} fusion(bf16[4,256,3072]{2,1,0:T(8,128)(2,1)} %collective-permute-done.10, bf16[4,2,256,3072]{3,2,1,0:T(8,128)(2,1)} %bitcast.247, s32[]{:T(128)S(6)} %select_n.190), kind=kLoop, calls=%fused_computation.1 | loop fusion | flops 12582912 | bytes 18874372 | tf_op jit(solution)/shard_map/convert_element_type | solution.py:69
  757.8 2.6 collective-permute-start.14
  760.3 86.5 %collective-permute-done.12 = bf16[256,1024]{1,0:T(8,128)(2,1)} collective-permute-done((bf16[256,1024]{1,0:T(8,128)(2,1)}, bf16[256,1024]{1,0:T(8,128)(2,1)}, u32[]{:S(2)}, u32[]{:S(2)}) %collective-permute-start.12) | collective-permute-done | bytes 524320 | tf_op jit(solution)/shard_map/ppermute | solution.py:94
  846.9 2.4 convert_add_fusion.4
  849.3 20.1 %collective-permute-done.14 = bf16[128,2048]{1,0:T(8,128)(2,1)S(1)} collective-permute-done((bf16[128,2048]{1,0:T(8,128)(2,1)S(1)}, bf16[128,2048]{1,0:T(8,128)(2,1)S(1)}, u32[]{:S(2)}, u32[]{:S(2)}) %collective-permute-start.14) | collective-permute-done | bytes 524320 | tf_op jit(solution)/shard_map/ppermute | solution.py:94
  875.0 39.4 %all-reduce = (f32[2048]{0:T(1024)}, f32[2048]{0:T(1024)}) all-reduce(f32[2048]{0:T(1024)S(1)} %get-tuple-element.16, f32[2048]{0:T(1024)S(1)} %copy-done.61), channel_id=1, replica_groups=mesh['seq'=8,'mp'=4] {'seq','mp'}, use_global_device_ids=true, to_apply=%region_15.16 | all-reduce | flops 4096 | bytes 32768 | tf_op jit(solution)/shard_map/psum | solution.py:278
  914.4 3.7 fusion.37
  918.1 21.6 %reduce-scatter.11.cloned.1.call-done = bf16[256,3072]{1,0:T(8,128)(2,1)} async-done(((bf16[1024,3072]{1,0:T(8,128)(2,1)}), bf16[256,3072]{1,0:T(8,128)(2,1)}) %reduce-scatter.11.cloned.1.call-update) | async-done | bytes 1572880 | tf_op jit(solution)/shard_map/reduce_scatter | solution.py:71
  941.8 2.8 fusion.110
  (296 shorter events, 104.9 us)
Async XLA Ops:
  8.0 109.3 %copy-start = (bf16[2048,512]{1,0:T(8,128)(2,1)S(1)}, bf16[2048,512]{1,0:T(8,128)(2,1)}, u32[]{:S(2)}) copy-start(bf16[2048,512]{1,0:T(8,128)(2,1)} %param.13) | copy-start | bytes 6291460
  8.0 90.1 %all-gather.7.cloned.1.call-start = ((), (), s32[]{:S(2)}) async-start(), calls=%async_computation.6 | async-start | bytes 5242880 | tf_op jit(solution)/shard_map/all_gather | solution.py:162
  14.5 137.7 %all-gather.9.cloned.1.call-start = ((), (), s32[]{:S(2)}) async-start(), calls=%async_computation.7 | async-start | bytes 2621440 | tf_op jit(solution)/shard_map/all_gather | solution.py:20
  14.6 116.8 %copy-start.72 = (f32[2]{0:T(128)}, f32[2]{0:T(128)S(1)}, u32[]{:S(2)}) copy-start(f32[2]{0:T(128)S(1)} %negate_log-plus-one_fusion) | copy-start | bytes 28
  14.7 92.7 %copy-start.68 = (f32[256]{0:T(256)}, f32[256]{0:T(256)S(1)}, u32[]{:S(2)}) copy-start(f32[256]{0:T(256)S(1)} %get-tuple-element.88) | copy-start | bytes 3076
  14.7 92.7 %copy-start.70 = (f32[256]{0:T(256)}, f32[256]{0:T(256)S(1)}, u32[]{:S(2)}) copy-start(f32[256]{0:T(256)S(1)} %get-tuple-element.89) | copy-start | bytes 3076
  14.8 110.1 %copy-start.64 = (f32[2,256]{1,0:T(2,128)}, f32[2,256]{1,0:T(2,128)S(1)}, u32[]{:S(2)}) copy-start(f32[2,256]{1,0:T(2,128)S(1)} %get-tuple-element.71) | copy-start | bytes 6148
  17.7 102.0 %copy-start.16 = (f32[1024,128]{0,1:T(8,128)}, f32[1024,128]{0,1:T(8,128)S(1)}, u32[]{:S(2)}) copy-start(f32[1024,128]{0,1:T(8,128)S(1)} %get-tuple-element.68) | copy-start | bytes 1572868
  111.9 5.4 copy-start.78
  124.8 6.1 copy-start.24
  130.9 165.2 %reduce-scatter.7.cloned.1.call-start = ((), (), s32[]{:S(2)}) async-start(), calls=%async_computation.8 | async-start | bytes 5242880 | tf_op jit(solution)/shard_map/reduce_scatter | solution.py:208
  133.7 8.6 copy-start.18
  135.2 7.1 copy-start.20
  154.2 5.5 copy-start.44
  169.3 5.5 copy-start.79
  172.7 9.3 copy-start.37
  174.8 7.2 copy-start.74
  189.8 106.3 %copy-start.1 = (bf16[256,2048]{1,0:T(8,128)(2,1)S(1)}, bf16[256,2048]{1,0:T(8,128)(2,1)}, u32[]{:S(2)}) copy-start(bf16[256,2048]{1,0:T(8,128)(2,1)} %param.11) | copy-start | bytes 3145732
  189.8 109.7 %copy-start.58 = (f32[2048]{0:T(1024)S(1)}, f32[2048]{0:T(1024)}, u32[]{:S(2)}) copy-start(f32[2048]{0:T(1024)} %param.18) | copy-start | bytes 24580
  189.9 175.7 %all-gather.11.cloned.1.call-start = ((), (), s32[]{:S(2)}) async-start(), calls=%async_computation.9 | async-start | bytes 4718592 | tf_op jit(solution)/shard_map/all_gather | solution.py:59
  191.1 59.7 %collective-permute-start.2 = (bf16[256,1024]{1,0:T(8,128)(2,1)S(1)}, bf16[256,1024]{1,0:T(8,128)(2,1)}, u32[]{:S(2)}, u32[]{:S(2)}) collective-permute-start(bf16[256,1024]{1,0:T(8,128)(2,1)S(1)} %constant_dynamic-slice_fusion.1), channel_id=1, source_target_pairs={{0,2},{1,3},{2,0},{3,1},{4,6},{5,7},{6,4},{7,5},{8,10},{9,11},{10,... | collective-permute-start | bytes 1572872 | tf_op jit(solution)/shard_map/ppermute | solution.py:36
  250.9 143.8 %all-gather.13.cloned.1.call-start = ((), (), s32[]{:S(2)}) async-start(), calls=%async_computation.10 | async-start | bytes 4718592 | tf_op jit(solution)/shard_map/all_gather | solution.py:59
  251.1 49.9 %collective-permute-start.6 = (bf16[256,2048]{1,0:T(8,128)(2,1)}, bf16[256,2048]{1,0:T(8,128)(2,1)}, u32[]{:S(2)}, u32[]{:S(2)}) collective-permute-start(bf16[256,2048]{1,0:T(8,128)(2,1)} %param.21), channel_id=1, source_target_pairs={{0,1},{1,0},{2,3},{3,2},{4,5},{5,4},{6,7},{7,6},{8,9},{9,8},{10,11... | collective-permute-start | bytes 3145736 | tf_op jit(solution)/shard_map/ppermute | solution.py:36
  301.0 25.6 %collective-permute-start = (bf16[256,2048]{1,0:T(8,128)(2,1)}, bf16[256,2048]{1,0:T(8,128)(2,1)}, u32[]{:S(2)}, u32[]{:S(2)}) collective-permute-start(bf16[256,2048]{1,0:T(8,128)(2,1)} %multiply_convert_fusion.4), channel_id=1, source_target_pairs={{0,1},{1,0},{2,3},{3,2},{4,5},{5,4},{6,7},{7,6},{8,9},{9,8},{10,11... | collective-permute-start | bytes 3145736 | tf_op jit(solution)/shard_map/ppermute | solution.py:36
  304.2 58.2 %collective-permute-start.7 = (bf16[512,2048]{1,0:T(8,128)(2,1)}, bf16[512,2048]{1,0:T(8,128)(2,1)}, u32[]{:S(2)}, u32[]{:S(2)}) collective-permute-start(bf16[512,2048]{1,0:T(8,128)(2,1)} %pad_maximum_fusion.3), channel_id=1, source_target_pairs={{0,4},{4,0},{8,12},{12,8},{16,20},{20,16},{24,28},{28,24},{1,5},{5... | collective-permute-start | bytes 6291464 | tf_op jit(solution)/shard_map/ppermute | solution.py:31
  329.7 35.9 %collective-permute-start.1 = (bf16[512,2048]{1,0:T(8,128)(2,1)}, bf16[512,2048]{1,0:T(8,128)(2,1)}, u32[]{:S(2)}, u32[]{:S(2)}) collective-permute-start(bf16[512,2048]{1,0:T(8,128)(2,1)} %pad_maximum_fusion.2), channel_id=1, source_target_pairs={{0,4},{4,0},{8,12},{12,8},{16,20},{20,16},{24,28},{28,24},{1,5},{5... | collective-permute-start | bytes 6291464 | tf_op jit(solution)/shard_map/ppermute | solution.py:31
  330.7 27.0 %collective-permute-start.3 = (bf16[128,2048]{1,0:T(8,128)(2,1)S(1)}, bf16[128,2048]{1,0:T(8,128)(2,1)}, u32[]{:S(2)}, u32[]{:S(2)}) collective-permute-start(bf16[128,2048]{1,0:T(8,128)(2,1)S(1)} %constant_dynamic-slice_fusion), channel_id=1, source_target_pairs={{0,2},{1,3},{2,0},{3,1},{4,6},{5,7},{6,4},{7,5},{8,10},{9,11},{10,... | collective-permute-start | bytes 1572872 | tf_op jit(solution)/shard_map/ppermute | solution.py:36
  357.8 200.5 %all-gather.15.cloned.1.call-start = ((), (), s32[]{:S(2)}) async-start(), calls=%async_computation.11 | async-start | bytes 5242880 | tf_op jit(solution)/shard_map/all_gather | solution.py:229
  394.6 12.9 %copy-start.59 = (bf16[2048,1024]{1,0:T(8,128)(2,1)S(1)}, bf16[2048,1024]{1,0:T(8,128)(2,1)}, u32[]{:S(2)}) copy-start(bf16[2048,1024]{1,0:T(8,128)(2,1)} %param.19) | copy-start | bytes 12582916
  414.0 11.6 %collective-permute-start.8 = (bf16[512,2048]{1,0:T(8,128)(2,1)S(1)}, bf16[512,2048]{1,0:T(8,128)(2,1)S(1)}, u32[]{:S(2)}, u32[]{:S(2)}) collective-permute-start(bf16[512,2048]{1,0:T(8,128)(2,1)S(1)} %slice.278), channel_id=1, source_target_pairs={{0,4},{4,0},{8,12},{12,8},{16,20},{20,16},{24,28},{28,24},{1,5},{5... | collective-permute-start | bytes 6291464 | tf_op jit(solution)/shard_map/ppermute | solution.py:31
  422.8 6.6 collective-permute-start.4
  426.6 26.1 %copy-start.9 = (bf16[256,2048]{1,0:T(8,128)(2,1)S(1)}, bf16[256,2048]{1,0:T(8,128)(2,1)}, u32[]{:S(2)}) copy-start(bf16[256,2048]{1,0:T(8,128)(2,1)} %reduce-scatter.7.cloned.1.call-done) | copy-start | bytes 3145732
  426.6 26.1 %collective-permute-start.9 = (bf16[256,2048]{1,0:T(8,128)(2,1)S(1)}, bf16[256,2048]{1,0:T(8,128)(2,1)S(1)}, u32[]{:S(2)}, u32[]{:S(2)}) collective-permute-start(bf16[256,2048]{1,0:T(8,128)(2,1)S(1)} %slice.280), channel_id=1, source_target_pairs={{0,1},{1,0},{2,3},{3,2},{4,5},{5,4},{6,7},{7,6},{8,9},{9,8},{10,11... | collective-permute-start | bytes 3145736 | tf_op jit(solution)/shard_map/ppermute | solution.py:36
  430.3 44.0 %copy-start.15 = (bf16[256,2048]{1,0:T(8,128)(2,1)S(1)}, bf16[256,2048]{1,0:T(8,128)(2,1)}, u32[]{:S(2)}) copy-start(bf16[256,2048]{1,0:T(8,128)(2,1)} %param.21) | copy-start | bytes 3145732
  430.4 43.8 %collective-permute-start.5 = (bf16[256,2048]{1,0:T(8,128)(2,1)S(1)}, bf16[256,2048]{1,0:T(8,128)(2,1)S(1)}, u32[]{:S(2)}, u32[]{:S(2)}) collective-permute-start(bf16[256,2048]{1,0:T(8,128)(2,1)S(1)} %slice.281), channel_id=1, source_target_pairs={{0,1},{1,0},{2,3},{3,2},{4,5},{5,4},{6,7},{7,6},{8,9},{9,8},{10,11... | collective-permute-start | bytes 3145736 | tf_op jit(solution)/shard_map/ppermute | solution.py:36
  477.4 174.9 %all-gather.17.cloned.1.call-start = ((), (), s32[]{:S(2)}) async-start(), calls=%async_computation.12 | async-start | bytes 2621440 | tf_op jit(solution)/shard_map/all_gather | solution.py:20
  583.4 5.9 copy-start.6
  596.4 153.5 %reduce-scatter.15.cloned.1.call-start = ((), (), s32[]{:S(2)}) async-start(), calls=%async_computation.16 | async-start | bytes 5242880 | tf_op jit(solution)/shard_map/reduce_scatter | solution.py:80
  605.9 149.7 %reduce-scatter.17.cloned.1.call-start = ((), (), s32[]{:S(2)}) async-start(), calls=%async_computation.17 | async-start | bytes 5242880 | tf_op jit(solution)/shard_map/reduce_scatter | solution.py:80
  615.3 255.3 %reduce-scatter.13.cloned.1.call-start = ((), (), s32[]{:S(2)}) async-start(), calls=%async_computation.15 | async-start | bytes 2621440 | tf_op jit(solution)/shard_map/reduce_scatter | solution.py:71
  616.0 9.0 copy-start.46
  625.0 23.5 %collective-permute-start.11 = (bf16[4,128,2048]{2,1,0:T(8,128)(2,1)}, bf16[4,128,2048]{2,1,0:T(8,128)(2,1)}, u32[]{:S(2)}, u32[]{:S(2)}) collective-permute-start(bf16[4,128,2048]{2,1,0:T(8,128)(2,1)} %dynamic-slice_bitcast_fusion.1), channel_id=1, source_target_pairs={{0,4},{4,0},{8,12},{12,8},{16,20},{20,16},{24,28},{28,24},{1,5},{5... | collective-permute-start | bytes 6291464 | tf_op jit(solution)/shard_map/ppermute | solution.py:31
  641.6 6.9 copy-start.30
  652.2 220.6 %reduce-scatter.9.cloned.1.call-start = ((), (), s32[]{:S(2)}) async-start(), calls=%async_computation.13 | async-start | bytes 5242880 | tf_op jit(solution)/shard_map/reduce_scatter | solution.py:271
  652.3 5.3 copy-start.14
  671.4 6.7 copy-start.17
  671.4 6.7 copy-start.41
  678.1 8.6 copy-start.42
  680.6 6.1 copy-start.43
  680.6 6.1 copy-start.77
  680.6 13.0 %slice-start = ((s8[8388608]{0:T(1024)(128)(4,1)}), s8[4194304]{0:T(1024)(128)(4,1)S(1)}, s32[]{:S(2)}) async-start(s8[8388608]{0:T(1024)(128)(4,1)} %bitcast.251), calls=%async_computation.18 | async-start | bytes 8388608
  686.7 6.9 slice-start.1
  705.4 234.3 %reduce-scatter.11.cloned.1.call-start = ((), (), s32[]{:S(2)}) async-start(), calls=%async_computation.14 | async-start | bytes 7864320 | tf_op jit(solution)/shard_map/reduce_scatter | solution.py:71
  729.4 10.4 %collective-permute-start.10 = (bf16[4,256,3072]{2,1,0:T(8,128)(2,1)S(1)}, bf16[4,256,3072]{2,1,0:T(8,128)(2,1)}, u32[]{:S(2)}, u32[]{:S(2)}) collective-permute-start(bf16[4,256,3072]{2,1,0:T(8,128)(2,1)S(1)} %dynamic-slice_bitcast_fusion), channel_id=1, source_target_pairs={{0,4},{4,0},{8,12},{12,8},{16,20},{20,16},{24,28},{28,24},{1,5},{5... | collective-permute-start | bytes 18874376 | tf_op jit(solution)/shard_map/ppermute | solution.py:31
  752.1 8.2 collective-permute-start.13
  753.6 119.1 %copy-start.2 = (bf16[256,2048]{1,0:T(8,128)(2,1)S(1)}, bf16[256,2048]{1,0:T(8,128)(2,1)}, u32[]{:S(2)}) copy-start(bf16[256,2048]{1,0:T(8,128)(2,1)} %param.11) | copy-start | bytes 3145732
  753.6 119.1 %copy-start.57 = (f32[2048]{0:T(1024)S(1)}, f32[2048]{0:T(1024)}, u32[]{:S(2)}) copy-start(f32[2048]{0:T(1024)} %param.12) | copy-start | bytes 24580
  753.6 119.1 %copy-start.63 = (f32[256]{0:T(256)S(1)}, f32[256]{0:T(256)}, u32[]{:S(2)}) copy-start(f32[256]{0:T(256)} %copy-done.62) | copy-start | bytes 3076
  753.6 119.1 %copy-start.67 = (f32[256]{0:T(256)S(1)}, f32[256]{0:T(256)}, u32[]{:S(2)}) copy-start(f32[256]{0:T(256)} %copy-done.66) | copy-start | bytes 3076
  753.6 93.2 %collective-permute-start.12 = (bf16[256,1024]{1,0:T(8,128)(2,1)}, bf16[256,1024]{1,0:T(8,128)(2,1)}, u32[]{:S(2)}, u32[]{:S(2)}) collective-permute-start(bf16[256,1024]{1,0:T(8,128)(2,1)} %get-tuple-element.55), channel_id=1, source_target_pairs={{0,4},{1,5},{2,6},{3,7},{4,2},{5,3},{6,0},{7,1},{8,12},{9,13},{10,... | collective-permute-start | bytes 1572872 | tf_op jit(solution)/shard_map/ppermute | solution.py:94
  755.7 113.8 %copy-start.40 = (bf16[256,2048]{1,0:T(8,128)(2,1)S(1)}, bf16[256,2048]{1,0:T(8,128)(2,1)}, u32[]{:S(2)}) copy-start(bf16[256,2048]{1,0:T(8,128)(2,1)} %reduce-scatter.17.cloned.1.call-done) | copy-start | bytes 3145732
  757.0 92.3 %collective-permute-start.15 = (bf16[128,2048]{1,0:T(8,128)(2,1)S(1)}, bf16[128,2048]{1,0:T(8,128)(2,1)S(1)}, u32[]{:S(2)}, u32[]{:S(2)}) collective-permute-start(bf16[128,2048]{1,0:T(8,128)(2,1)S(1)} %get-tuple-element.52), channel_id=1, source_target_pairs={{4,6},{5,7},{6,4},{7,5},{12,14},{13,15},{14,12},{15,13},{20,22},{2... | collective-permute-start | bytes 1572872 | tf_op jit(solution)/shard_map/ppermute | solution.py:95
  757.7 117.2 %copy-start.61 = (f32[2048]{0:T(1024)S(1)}, f32[2048]{0:T(1024)}, u32[]{:S(2)}) copy-start(f32[2048]{0:T(1024)} %get-tuple-element.11) | copy-start | bytes 24580
  757.8 111.7 %collective-permute-start.14 = (bf16[128,2048]{1,0:T(8,128)(2,1)S(1)}, bf16[128,2048]{1,0:T(8,128)(2,1)S(1)}, u32[]{:S(2)}, u32[]{:S(2)}) collective-permute-start(bf16[128,2048]{1,0:T(8,128)(2,1)S(1)} %get-tuple-element.53), channel_id=1, source_target_pairs={{0,4},{1,5},{2,6},{3,7},{4,2},{5,3},{6,0},{7,1},{8,12},{9,13},{10,... | collective-permute-start | bytes 1572872 | tf_op jit(solution)/shard_map/ppermute | solution.py:94
  (47 other events, 134.1 us)
Sparse Core Ops, SparseCore 0:
  14.6 83.4 all-gather.6
  131.0 21.0 all-gather.8
  190.0 106.0 reduce-scatter.6
  477.5 80.7 all-gather.14
  596.6 21.3 all-gather.16
Sparse Core Ops, SparseCore 1:
  250.9 34.0 all-gather.10
  357.8 36.7 all-gather.12
  606.0 54.0 reduce-scatter.14
  663.1 52.5 reduce-scatter.16
  718.9 35.0 reduce-scatter.12
  756.3 98.1 reduce-scatter.8
  857.6 82.1 reduce-scatter.10

commit v2 on v1

--- a/solution.py
+++ b/solution.py
@@ -3,6 +3,8 @@
 import jax
 import jax.numpy as jnp
 from jax import lax
+from jax.experimental import pallas as pl
+from jax.experimental.pallas import tpu as pltpu
 from jax.sharding import PartitionSpec as P
 
 DK = 256
@@ -146,6 +148,506 @@
     )
 
 
+MESH = pl.DeviceIdType.MESH
+LIMIT = 62 * 1024 * 1024
+
+
+def remote(src, dst, send, recv, s, z):
+    return pltpu.make_async_remote_copy(
+        src_ref=src,
+        dst_ref=dst,
+        send_sem=send,
+        recv_sem=recv,
+        device_id=(s, z),
+        device_id_type=MESH,
+    )
+
+
+def greet(partners):
+    barrier = pltpu.get_barrier_semaphore()
+    count = 0
+    for present, s, z in partners:
+
+        @pl.when(present)
+        def _():
+            pl.semaphore_signal(barrier, inc=1, device_id=(s, z), device_id_type=MESH)
+
+        count = count + jnp.where(present, 1, 0)
+    pl.semaphore_wait(barrier, count)
+
+
+def dot(left, right):
+    return jnp.dot(left, right, preferred_element_type=jnp.float32)
+
+
+def line_push(x, send, recv, s, z, slot, way):
+    return remote(x.at[slot], x.at[slot], send.at[way, slot], recv.at[slot], s, z + 1 - 2 * way)
+
+
+def line_gather(x, send, recv, s, z, depth, use):
+    @pl.when(z < depth - 1)
+    def _():
+        line_push(x, send, recv, s, z, z, 0).start()
+
+    @pl.when(z > 0)
+    def _():
+        line_push(x, send, recv, s, z, z, 1).start()
+
+    def one(turn, _):
+        away = (turn + 1) // 2
+        left, right = z - away, z + away
+
+        @pl.when((turn % 2 == 1) & (left >= 0))
+        def _():
+            remote(x.at[left], x.at[left], send.at[0, left], recv.at[left], s, z - 1).wait_recv()
+
+            @pl.when(z < depth - 1)
+            def _():
+                line_push(x, send, recv, s, z, left, 0).start()
+
+        @pl.when((turn % 2 == 1) & (right < depth))
+        def _():
+            remote(x.at[right], x.at[right], send.at[1, right], recv.at[right], s, z + 1).wait_recv()
+
+            @pl.when(z > 0)
+            def _():
+                line_push(x, send, recv, s, z, right, 1).start()
+
+        slot = jnp.where(turn % 2 == 1, left, right)
+
+        @pl.when((slot >= 0) & (slot < depth))
+        def _():
+            use(slot)
+
+        return 0
+
+    lax.fori_loop(0, 2 * depth - 1, one, 0)
+
+
+def line_gather_end(x, send, recv, s, z, depth):
+    def one(slot, _):
+        @pl.when((slot <= z) & (z < depth - 1))
+        def _():
+            line_push(x, send, recv, s, z, slot, 0).wait_send()
+
+        @pl.when((slot >= z) & (z > 0))
+        def _():
+            line_push(x, send, recv, s, z, slot, 1).wait_send()
+
+        return 0
+
+    lax.fori_loop(0, depth, one, 0)
+
+
+def add_rows(into, other):
+    step = 32
+
+    def one(i, _):
+        rows = pl.ds(pl.multiple_of(i * step, step), step)
+        into[rows, :] = (
+            into[rows, :].astype(jnp.float32) + other[rows, :].astype(jnp.float32)
+        ).astype(into.dtype)
+        return 0
+
+    lax.fori_loop(0, into.shape[0] // step, one, 0)
+
+
+def line_scatter(sbuf, rbuf, total, send, recv, s, z, depth, partial, own):
+    def right(j):
+        return remote(sbuf.at[j], rbuf.at[j], send.at[j], recv.at[j], s, z + 1)
+
+    def left(j):
+        slot = jnp.where(j == z - 1, depth, j)
+        return remote(sbuf.at[j], rbuf.at[slot], send.at[j], recv.at[slot], s, z - 1)
+
+    def arrived(slot, sender):
+        remote(sbuf.at[0], rbuf.at[slot], send.at[0], recv.at[slot], s, sender).wait_recv()
+
+    def first(turn, _):
+        up = depth - 1 + z - turn // 2
+        down = turn // 2 - (depth - 1) + z
+        j = jnp.where(turn % 2 == 0, up, down)
+        valid = jnp.where(turn % 2 == 0, (up > z) & (up < depth), (down >= 0) & (down < z))
+
+        @pl.when(valid)
+        def _():
+            partial(j)
+
+            @pl.when((z == 0) & (j > z))
+            def _():
+                right(j).start()
+
+            @pl.when((z == depth - 1) & (j < z))
+            def _():
+                left(j).start()
+
+        return 0
+
+    lax.fori_loop(0, 2 * (depth - 1), first, 0)
+    own()
+
+    def event(turn, _):
+        up = depth - 1 + z - turn
+        down = turn - (depth - 1) + z
+
+        @pl.when((z > 0) & (up >= z) & (up < depth))
+        def _():
+            arrived(up, z - 1)
+
+            @pl.when(up > z)
+            def _():
+                add_rows(sbuf.at[up], rbuf.at[up])
+                right(up).start()
+
+            @pl.when(up == z)
+            def _():
+                add_rows(total, rbuf.at[up])
+
+        @pl.when((z < depth - 1) & (down >= 0) & (down <= z))
+        def _():
+            slot = jnp.where(down == z, depth, down)
+            arrived(slot, z + 1)
+
+            @pl.when(down < z)
+            def _():
+                add_rows(sbuf.at[down], rbuf.at[down])
+                left(down).start()
+
+            @pl.when(down == z)
+            def _():
+                add_rows(total, rbuf.at[depth])
+
+        return 0
+
+    lax.fori_loop(0, depth, event, 0)
+
+    def end(j, _):
+        @pl.when(j > z)
+        def _():
+            right(j).wait_send()
+
+        @pl.when(j < z)
+        def _():
+            left(j).wait_send()
+
+        return 0
+
+    lax.fori_loop(0, depth, end, 0)
+
+
+def centred(rows):
+    centre = rows - jnp.mean(rows, axis=-1, keepdims=True)
+    inverse = lax.rsqrt(jnp.mean(centre * centre, axis=-1, keepdims=True) + eps)
+    return centre * inverse, inverse
+
+
+def block(rows, index):
+    return pl.ds(pl.multiple_of(index * rows, rows), rows)
+
+
+def attend_kernel(
+    tok,
+    gain,
+    cot,
+    w_query,
+    w_key,
+    w_value,
+    w_gate,
+    w_out,
+    cosine,
+    sine,
+    mask,
+    q_scale,
+    k_scale,
+    decay,
+    x_out,
+    q_out,
+    k_out,
+    v_out,
+    gp_out,
+    gn_out,
+    gated_out,
+    inv_out,
+    p_out,
+    r_out,
+    hidden_out,
+    cot_rows,
+    xg,
+    q,
+    k,
+    v,
+    gp,
+    gn,
+    gated,
+    inv,
+    weights,
+    grown,
+    entering,
+    tile,
+    state,
+    state_in,
+    state_to,
+    rbuf,
+    total,
+    wq,
+    wk,
+    wv,
+    wg,
+    wo,
+    load,
+    save,
+    g_send,
+    g_recv,
+    s_send,
+    s_recv,
+    c_send,
+    c_recv,
+    x_send,
+    x_recv,
+):
+    f32, bf16 = jnp.float32, jnp.bfloat16
+    depth = xg.shape[0]
+    rows = xg.shape[1]
+    heads = mask.shape[0]
+    s, z = lax.axis_index("seq"), lax.axis_index("mp")
+    place = lax.rem(s, SEQ_DEVS)
+    pair = z + 1 - 2 * lax.rem(z, 2)
+    twin = s + 1 - 2 * lax.rem(s, 2)
+    loads = [
+        pltpu.make_async_copy(a, b, load.at[i])
+        for i, (a, b) in enumerate(
+            [(w_query, wq), (w_key, wk), (w_value, wv), (w_gate, wg), (w_out, wo)]
+        )
+    ]
+    for copy in loads:
+        copy.start()
+
+    def norm(i, _):
+        part = pl.ds(pl.multiple_of(i * 32, 32), 32)
+        unit, _ = centred(tok[part, :].astype(f32))
+        xg[z, part, :] = (unit * gain[...]).astype(bf16)
+        return 0
+
+    lax.fori_loop(0, rows // 32, norm, 0)
+    greet(
+        [
+            (z > 0, s, z - 1),
+            (z < depth - 1, s, z + 1),
+            (place > 0, s - 1, z),
+            (place < SEQ_DEVS - 1, s + 1, z),
+        ]
+    )
+
+    @pl.when(place == 0)
+    def _():
+        state_in[...] = jnp.zeros_like(state_in)
+
+    def use(j):
+        at = block(rows, j)
+        @pl.when(j == z)
+        def _():
+            for copy in loads:
+                copy.wait()
+
+        c, sn = cosine[at, :], sine[at, :]
+        for h in range(heads):
+            cols = slice(h * DK, (h + 1) * DK)
+            for w, out in ((wq, q), (wk, k)):
+                p = dot(xg[j], w[:, cols])
+                a, b = p[:, : DK // 2], p[:, DK // 2 :]
+                out[at, h * DK : h * DK + DK // 2] = (a * c - b * sn).astype(bf16)
+                out[at, h * DK + DK // 2 : (h + 1) * DK] = (b * c + a * sn).astype(bf16)
+        for h in range(heads):
+            wide = slice(h * DV, (h + 1) * DV)
+            v[at, wide] = dot(xg[j], wv[:, wide]).astype(bf16)
+            gp[at, wide] = dot(xg[j], wg[:, wide]).astype(bf16)
+        for h in range(heads):
+            cols = slice(h * DK, (h + 1) * DK)
+            wide = slice(h * DV, (h + 1) * DV)
+            kb, vb = k[at, cols], v[at, wide]
+            vd = (vb.astype(f32) * k_scale[h]).astype(bf16)
+            grown[h, j] = product_t(kb, vd)
+            weights[h, j] = (product_rt(q[at, cols], kb) * mask[h]).astype(bf16)
+
+    line_gather(xg, g_send, g_recv, s, z, depth, use)
+    mine = pltpu.make_async_copy(cot, cot_rows.at[0], x_send.at[3])
+    mine.start()
+    swap = remote(cot, cot_rows.at[1], x_send.at[0], x_recv.at[0], s, pair)
+    swap.start()
+    near = remote(cot, cot_rows.at[2], x_send.at[1], x_recv.at[1], twin, z)
+    near.start()
+    for h in range(heads):
+        state[h] = grown[h, 0]
+        for b in range(1, depth):
+            state[h] = decay[h, 0] * state[h] + grown[h, b]
+    chain = remote(state_to, state_in, c_send, c_recv, s + 1, z)
+
+    @pl.when(place > 0)
+    def _():
+        remote(state_to, state_in, c_send, c_recv, s - 1, z).wait_recv()
+
+    @pl.when(place < SEQ_DEVS - 1)
+    def _():
+        for h in range(heads):
+            state_to[h] = (decay[h, 1] * state_in[h].astype(f32) + state[h]).astype(bf16)
+        chain.start()
+
+    saves = [
+        pltpu.make_async_copy(a, b, save.at[i])
+        for i, (a, b) in enumerate(
+            [
+                (xg, x_out),
+                (q, q_out),
+                (k, k_out),
+                (v, v_out),
+                (gp, gp_out),
+                (weights, p_out),
+                (entering, r_out),
+                (gn, gn_out),
+                (gated, gated_out),
+                (inv, inv_out),
+            ]
+        )
+    ]
+    for copy in saves[:6]:
+        copy.start()
+    for h in range(heads):
+        cols = slice(h * DK, (h + 1) * DK)
+        wide = slice(h * DV, (h + 1) * DV)
+        state[h] = state_in[h].astype(f32)
+
+        def cross(b, _):
+            at = block(rows, b)
+            entering[h, b] = state[h].astype(bf16)
+            state[h] = decay[h, 0] * state[h] + grown[h, b]
+            qd = (q[at, cols].astype(f32) * q_scale[h]).astype(bf16)
+            tile[...] = dot(weights[h, b], v[at, wide]) + dot(qd, entering[h, b])
+
+            def norm(i, _):
+                here = block(32, i)
+                there = pl.ds(pl.multiple_of(b * rows + i * 32, 32), 32)
+                unit, inverse = centred(tile[here, :])
+                gate = gp[there, wide].astype(f32)
+                gn[there, wide] = unit.astype(bf16)
+                gated[there, wide] = (unit * gate / (1.0 + jnp.exp(-gate))).astype(bf16)
+                inv[h, there, :] = jnp.broadcast_to(inverse, (32, inv.shape[2]))
+                return 0
+
+            lax.fori_loop(0, rows // 32, norm, 0)
+            return 0
+
+        lax.fori_loop(0, depth, cross, 0)
+    for copy in saves[6:]:
+        copy.start()
+    line_gather_end(xg, g_send, g_recv, s, z, depth)
+    saves[0].wait()
+    swap.wait_recv()
+    far = remote(cot_rows.at[1], cot_rows.at[3], x_send.at[2], x_recv.at[2], twin, z)
+    far.start()
+    wide = 512
+
+    def partial(j):
+        for n in range(0, total.shape[1], wide):
+            xg[j, :, n : n + wide] = dot(gated[block(rows, j), :], wo[:, n : n + wide]).astype(bf16)
+
+    def own():
+        for n in range(0, total.shape[1], wide):
+            total[:, n : n + wide] = tok[:, n : n + wide].astype(f32) + dot(
+                gated[block(rows, z), :], wo[:, n : n + wide]
+            )
+
+    line_scatter(xg, rbuf, total, s_send, s_recv, s, z, depth, partial, own)
+    done = pltpu.make_async_copy(total, hidden_out, save.at[0])
+    done.start()
+
+    @pl.when(place < SEQ_DEVS - 1)
+    def _():
+        chain.wait_send()
+
+    swap.wait_send()
+    near.wait()
+    far.wait()
+    mine.wait()
+    for copy in saves[1:]:
+        copy.wait()
+    done.wait()
+
+
+def attend(
+    tok, gain, cot, w_query, w_key, w_value, w_gate, w_out, cosine, sine, mask, q_scale, k_scale, decay
+):
+    f32, bf16 = jnp.float32, jnp.bfloat16
+    depth = lax.axis_size("mp")
+    rows, width = tok.shape
+    span = depth * rows
+    heads = mask.shape[0]
+    hk, hv = w_query.shape[1], w_value.shape[1]
+    any_ = pl.BlockSpec(memory_space=pl.ANY)
+    vmem = pl.BlockSpec(memory_space=pltpu.VMEM)
+    shapes = [
+        ((depth, rows, width), bf16),
+        ((span, hk), bf16),
+        ((span, hk), bf16),
+        ((span, hv), bf16),
+        ((span, hv), bf16),
+        ((span, hv), bf16),
+        ((span, hv), bf16),
+        ((heads, span, 128), f32),
+        ((heads, depth, rows, rows), bf16),
+        ((heads, depth, DK, DV), bf16),
+        ((rows, width), f32),
+        ((4, rows, width), bf16),
+    ]
+    dma = pltpu.SemaphoreType.DMA
+    return pl.pallas_call(
+        attend_kernel,
+        out_shape=[jax.ShapeDtypeStruct(*one) for one in shapes],
+        in_specs=[vmem, vmem, any_] + [any_] * 5 + [vmem] * 6,
+        out_specs=[any_] * len(shapes),
+        scratch_shapes=[
+            pltpu.VMEM((depth, rows, width), bf16),
+            pltpu.VMEM((span, hk), bf16),
+            pltpu.VMEM((span, hk), bf16),
+            pltpu.VMEM((span, hv), bf16),
+            pltpu.VMEM((span, hv), bf16),
+            pltpu.VMEM((span, hv), bf16),
+            pltpu.VMEM((span, hv), bf16),
+            pltpu.VMEM((heads, span, 128), f32),
+            pltpu.VMEM((heads, depth, rows, rows), bf16),
+            pltpu.VMEM((heads, depth, DK, DV), f32),
+            pltpu.VMEM((heads, depth, DK, DV), bf16),
+            pltpu.VMEM((rows, DV), f32),
+            pltpu.VMEM((heads, DK, DV), f32),
+            pltpu.VMEM((heads, DK, DV), bf16),
+            pltpu.VMEM((heads, DK, DV), bf16),
+            pltpu.VMEM((depth + 1, rows, width), bf16),
+            pltpu.VMEM((rows, width), f32),
+            pltpu.VMEM(w_query.shape, bf16),
+            pltpu.VMEM(w_key.shape, bf16),
+            pltpu.VMEM(w_value.shape, bf16),
+            pltpu.VMEM(w_gate.shape, bf16),
+            pltpu.VMEM(w_out.shape, bf16),
+            dma((5,)),
+            dma((10,)),
+            dma((2, depth)),
+            dma((depth,)),
+            dma((depth,)),
+            dma((depth + 1,)),
+            dma,
+            dma,
+            dma((4,)),
+            dma((3,)),
+        ],
+        compiler_params=pltpu.CompilerParams(
+            collective_id=0, has_side_effects=True, vmem_limit_bytes=LIMIT
+        ),
+        cost_estimate=pl.CostEstimate(
+            flops=30 * 10**9, bytes_accessed=60 * 10**6, transcendentals=2 * 10**6
+        ),
+        name="attend",
+    )(tok, gain, cot, w_query, w_key, w_value, w_gate, w_out, cosine, sine, mask, q_scale, k_scale, decay)
+
+
 def shards(
     tokens, gain_mix, w_query, w_key, w_value, w_gate, w_out, gain_ffn, w_up, w_down, cotangent
 ):
@@ -158,60 +660,41 @@
     core = lax.axis_index("seq") % 2
     resid = tokens.astype(f32)
     unit_mix, inv_mix = normalize(resid)
-    normed_mix = (unit_mix * gain_mix).astype(bf16)
-    gathered_mix = lax.all_gather(normed_mix, "mp", axis=0, tiled=True)
     w_up = jnp.where(core == 0, w_up, far_shard(w_up))
     w_down = jnp.where(core == 0, w_down, far_shard(w_down))
-    cot_rows = group_rows(cotangent)
-    query_pre = jnp.dot(gathered_mix, w_query, preferred_element_type=f32)
-    key_pre = jnp.dot(gathered_mix, w_key, preferred_element_type=f32)
-    value_pre = jnp.dot(gathered_mix, w_value, preferred_element_type=f32)
-    gate_pre = jnp.dot(gathered_mix, w_gate, preferred_element_type=f32)
     positions = place * span_rows + jnp.arange(span_rows, dtype=jnp.int32)
     cosine, sine = angles(positions)
-    query = rotate(query_pre.reshape(span_rows, local_heads, DK), cosine, sine).astype(bf16)
-    keys = rotate(key_pre.reshape(span_rows, local_heads, DK), cosine, sine).astype(bf16)
-    q_blk = to_blocks(query.reshape(span_rows, local_heads * DK), local_heads, DK)
-    k_blk = to_blocks(keys.reshape(span_rows, local_heads * DK), local_heads, DK)
-    v_blk = to_blocks(value_pre.astype(bf16), local_heads, DV)
     heads = (lax.axis_index("mp") * local_heads).astype(f32) + jnp.arange(local_heads, dtype=f32)
     logs = jnp.log1p(-jnp.exp2(-5.0 - heads))
     steps = jnp.arange(STRETCH, dtype=f32)
     gaps = steps[:, None] - steps[None, :]
     mask = jnp.where(gaps >= 0, jnp.exp(logs[:, None, None] * jnp.maximum(gaps, 0.0)), 0.0)
-    q_scale = jnp.exp(logs[:, None] * (steps + 1.0))[:, None, :, None]
-    k_scale = jnp.exp(logs[:, None] * (STRETCH - 1.0 - steps))[:, None, :, None]
+    q_scale = jnp.exp(logs[:, None] * (steps + 1.0))[:, :, None]
+    k_scale = jnp.exp(logs[:, None] * (STRETCH - 1.0 - steps))[:, :, None]
     stretch_decay = jnp.exp(logs * STRETCH)[:, None, None]
     span_decay = jnp.exp(logs * span_rows)
-    scores = jnp.einsum("hcik,hcjk->hcij", q_blk, k_blk, preferred_element_type=f32)
-    weights = (scores * mask[:, None]).astype(bf16)
-    intra = jnp.einsum("hcij,hcjv->hciv", weights, v_blk, preferred_element_type=f32)
+    decay = jnp.broadcast_to(
+        jnp.stack([jnp.exp(logs * STRETCH), span_decay], axis=1)[:, :, None, None],
+        (local_heads, 2, 1, DV),
+    )
+    gathered_mix, q_all, k_all, v_all, gate_pre, unit_rows, gated, inv_wide, weights, entering, hidden, cot_rows = attend(
+        tokens, gain_mix[None, :], cotangent, w_query, w_key, w_value, w_gate, w_out,
+        cosine[:, 0], sine[:, 0], mask, q_scale, k_scale, decay,
+    )
+    gathered_mix = gathered_mix.reshape(span_rows, -1)
+    q_blk = to_blocks(q_all, local_heads, DK)
+    k_blk = to_blocks(k_all, local_heads, DK)
+    v_blk = to_blocks(v_all, local_heads, DV)
+    gate_pre = gate_pre.astype(f32)
+    unit_rows = unit_rows.astype(f32)
+    unit_grp = to_blocks(unit_rows, local_heads, DV)
+    inv_grp = inv_wide[:, :, :1].reshape(local_heads, blocks, STRETCH, 1)
+    swish = jax.nn.silu(gate_pre)
+    q_scale = q_scale[:, None]
+    k_scale = k_scale[:, None]
     value_dec = (v_blk.astype(f32) * k_scale).astype(bf16)
     query_dec = (q_blk.astype(f32) * q_scale).astype(bf16)
-    local_states = jnp.einsum("hcjk,hcjv->hckv", k_blk, value_dec, preferred_element_type=f32)
-    span_state = jnp.zeros_like(local_states[:, 0])
-    for index in range(blocks):
-        span_state = stretch_decay * span_state + local_states[:, index]
-    incoming = carried_in(span_state, span_decay, place, False)
-    carried_state = incoming
-    entering = []
-    for index in range(blocks):
-        entering.append(carried_state)
-        carried_state = stretch_decay * carried_state + local_states[:, index]
-    entering = jnp.stack(entering, axis=1).astype(bf16)
-    cross = jnp.einsum("hcik,hckv->hciv", query_dec, entering, preferred_element_type=f32)
-    mixed = intra + cross
-    unit_grp, inv_grp = normalize(mixed)
-    unit_rows = from_blocks(unit_grp)
-    swish = jax.nn.silu(gate_pre)
-    gated = (swish * unit_rows).astype(bf16)
-    mixer = lax.psum_scatter(
-        jnp.dot(gated, w_out, preferred_element_type=f32).astype(jnp.bfloat16),
-        "mp",
-        scatter_dimension=0,
-        tiled=True,
-    ).astype(jnp.float32)
-    hidden = resid + mixer
+    cot_rows = cot_rows.reshape(span_rows, -1)
     unit_ffn, inv_ffn = normalize(hidden)
     normed_ffn = (unit_ffn * gain_ffn).astype(bf16)
     gathered_ffn = group_rows(normed_ffn)
@@ -242,7 +725,7 @@
         "hciv,hckv->hcik", grad_mixed, entering, preferred_element_type=f32
     )
     grad_enter = jnp.einsum("hcik,hciv->hckv", query_dec, grad_mixed, preferred_element_type=f32)
-    local_grad = jnp.zeros_like(span_state)
+    local_grad = jnp.zeros((local_heads, DK, DV), f32)
     for index in reversed(range(blocks)):
         local_grad = stretch_decay * local_grad + grad_enter[:, index]
     leaving = carried_in(local_grad, span_decay, place, True)

time: 963 us -> 870 us (0.903)
  Pallas kernels: 0 us -> 177 us
  waiting for transfers between devices: 510 us -> 353 us
  matrix products: 192 us -> 139 us
  local copies, waits for them, and re-layouts: 87.4 us -> 47.5 us
  other arithmetic: 85.6 us -> 67.4 us
    pallas_call x0 -> x1, Pallas kernels: none -> 177 us  [attend(): pl.pallas_call(attend_kernel, out_shape=[jax.ShapeDtypeStruct(*one) for o...]
    all_gather x1 -> x0, waiting for transfers between devices: 80.4 us -> none  [shards(): gathered_mix = lax.all_gather(normed_mix, 'mp', axis=0, tiled=True)]
    ppermute x2, waiting for transfers between devices: 107 us -> 60.9 us  [scatter_far(): lax.ppermute(jnp.where(core == 0, second, first), ('seq', 'mp'), crossed)]
    reduce_scatter x1 -> x0, waiting for transfers between devices: 44.9 us -> none  [shards(): lax.psum_scatter(jnp.dot(gated, w_out, preferred_element_type=f32).astype...]
    reduce_scatter x1, waiting for transfers between devices: 0.01 us -> 42.5 us  [shards(): lax.psum_scatter(part_mix.astype(jnp.bfloat16), 'mp', scatter_dimension=0...]
    dot_general x9 -> x0, matrix products: 40.8 us -> none  [the longest x1 9.27 us: shards(): value_pre = jnp.dot(gathered_mix, w_value, preferred_element_type=f32)]
    ppermute x6 -> x5, waiting for transfers between devices: 144 us -> 112 us  [mp_swap(): return lax.ppermute(value, 'mp', [(i, i ^ bit) for i in range(count)])]
    unnamed x174 -> x85, local copies, waits for them, and re-layouts: 38 us -> 11.2 us
  transfers between devices with their start and end apart: 28 -> 23, of which waited for: 15 -> 13; matrix products, arithmetic and copies ran while one was open for 23% -> 22% of each run, Pallas kernels for 0% -> 21%
where the time goes in v2:
time: 870 us; the launch traced here: 862 us
  waiting for transfers between devices  353 us (41%)
  Pallas kernels  177 us (20%)
  matrix products  139 us (16%)
  other arithmetic  67.4 us (8%)
  local copies, waits for them, and re-layouts  47.5 us (5%)
  blocking collectives  40 us (5%)
  starting transfers between devices  23 us (3%)
  between operations  15.1 us (2%)
    pallas_call x1, Pallas kernels, attend(): pl.pallas_call(attend_kernel, out_shape=[jax.ShapeDtypeStruct(*one) for o...  177 us
    ppermute x5, waiting for transfers between devices, mp_swap(): return lax.ppermute(value, 'mp', [(i, i ^ bit) for i in range(count)])  112 us
    all_gather x1, waiting for transfers between devices, shards(): lax.all_gather(grad_hidden.astype(bf16), 'mp', axis=0, tiled=True)  72.6 us
    ppermute x2, waiting for transfers between devices, scatter_far(): lax.ppermute(jnp.where(core == 0, second, first), ('seq', 'mp'), crossed)  60.9 us
    dot_general x7, matrix products, product_rt(): lax.dot_general(left, right, (((1,), (1,)), ((), ())), preferred_element_...  60.9 us
    dot_general x4, matrix products, product_t(): lax.dot_general(left, right, (((0,), (0,)), ((), ())), preferred_element_...  45.6 us
    reduce_scatter x1, waiting for transfers between devices, shards(): lax.psum_scatter(part_mix.astype(jnp.bfloat16), 'mp', scatter_dimension=0...  42.5 us
    psum x1, blocking collectives, shards(): lax.psum((gain_mix_part, gain_ffn_part), ('seq', 'mp'))  40 us
  transfers between devices with their start and end apart: 23, of which 13 were waited for; matrix products, arithmetic and copies ran while one was open for 22% of the time, Pallas kernels for 21%

profile of v2, /device:TPU:0, one launch (start us, length us, event | category | flops | bytes accessed | tf_op | source)
XLA Modules:
  0.0 861.8 jit_solution(3208162894725738082)
XLA Ops:
  8.3 4.1 collective-permute-start.2
  12.5 23.0 %collective-permute-done.2 = bf16[256,1024]{1,0:T(8,128)(2,1)S(1)} collective-permute-done((bf16[256,1024]{1,0:T(8,128)(2,1)S(1)}, bf16[256,1024]{1,0:T(8,128)(2,1)S(1)}, u32[]{:S(2)}, u32[]{:S(2)}) %collective-permute-start.2) | collective-permute-done | bytes 524320 | tf_op jit(solution)/shard_map/ppermute | solution.py:38
  38.5 3.1 fusion.79
  42.3 176.8 %attend.1 = (bf16[4,256,2048]{2,1,0:T(8,128)(2,1)}, bf16[1024,512]{1,0:T(8,128)(2,1)}, bf16[1024,512]{1,0:T(8,128)(2,1)}, bf16[1024,1024]{1,0:T(8,128)(2,1)}, bf...) custom-call(bf16[256,2048]{1,0:T(8,128)(2,1)} %tok.1, ...), custom_call_target="tpu_custom_call" | custom-call | flops 30000001024 | bytes 60000000 | tf_op jit(solution)/shard_map/attend/pallas_call | solution.py:602
  219.1 1.9 reduce_sum.108
  221.1 1.9 multiply_reduce_fusion.2
  223.8 21.9 %collective-permute-done = bf16[256,2048]{1,0:T(8,128)(2,1)} collective-permute-done((bf16[256,2048]{1,0:T(8,128)(2,1)S(1)}, bf16[256,2048]{1,0:T(8,128)(2,1)}, u32[]{:S(2)}, u32[]{:S(2)}) %collective-permute-start) | collective-permute-done | bytes 1048608 | tf_op jit(solution)/shard_map/ppermute | solution.py:38
  245.7 2.7 pad_maximum_fusion.1
  250.5 25.7 %collective-permute-done.3 = bf16[128,2048]{1,0:T(8,128)(2,1)} collective-permute-done((bf16[128,2048]{1,0:T(8,128)(2,1)S(1)}, bf16[128,2048]{1,0:T(8,128)(2,1)}, u32[]{:S(2)}, u32[]{:S(2)}) %collective-permute-start.3) | collective-permute-done | bytes 524320 | tf_op jit(solution)/shard_map/ppermute | solution.py:38
  276.5 19.1 %multiply_convert_fusion.1 = (bf16[1024,1024]{1,0:T(8,128)(2,1)}, f32[1024,1024]{1,0:T(8,128)}, f32[1024,1024]{1,0:T(8,128)}) fusion(bf16[2048,1024]{1,0:T(8,128)(2,1)} %param.19, bf16[2048,1024]{1,0:T(8,128)(2,1)} %all-gather.5.cloned.1.call-done, pred[]{:T(512)S(6)} %eq.15, bf16[512,2048]{1,0:T(8,128)(2,1)} %collective-permute-done.1, ...), kind=kOutput, calls=%fused_computation.45 | convolution fusion | flops 4377804800 | bytes 23068672 | tf_op jit(solution)/shard_map/dot_general | solution.py:701
  295.7 24.9 %all-gather.7.cloned.1.call-done = bf16[1024,2048]{1,0:T(8,128)(2,1)} async-done(((bf16[128,2048]{1,0:T(8,128)(2,1)}), bf16[1024,2048]{1,0:T(8,128)(2,1)}) %all-gather.7.cloned.1.call-update) | async-done | bytes 4194320 | tf_op jit(solution)/shard_map/all_gather | solution.py:61
  320.6 11.6 %add_convert_fusion.1 = bf16[1024,1024]{1,0:T(8,128)(2,1)S(1)} fusion(f32[1024,1024]{1,0:T(8,128)} %get-tuple-element.50, f32[1024,1024]{1,0:T(8,128)} %get-tuple-element.84, bf16[1024,2048]{1,0:T(8,128)(2,1)} %bitcast.199, bf16[1024,2048]{1,0:T(8,128)(2,1)} %param.20, bf16[1024,2048]{1,0:T(8,128)(2,1)} %all-gather.7.cloned.1.call-done, pred[]{:T(512)S(6)} %eq.15), kind=kOutput, calls=%fused_computation.44 | convolution fusion | flops 4311744512 | bytes 23068672 | tf_op jit(solution)/shard_map/dot_general | solution.py:146
  332.2 4.6 fusion.54
  337.1 3.3 collective-permute-start.6
  340.4 4.7 fusion.56
  345.5 4.0 collective-permute-start.4
  350.5 1.6 collective-permute-start.7
  354.4 1.6 collective-permute-start.5
  355.9 20.7 %collective-permute-done.7 = bf16[256,2048]{1,0:T(8,128)(2,1)S(1)} collective-permute-done((bf16[256,2048]{1,0:T(8,128)(2,1)S(1)}, bf16[256,2048]{1,0:T(8,128)(2,1)S(1)}, u32[]{:S(2)}, u32[]{:S(2)}) %collective-permute-start.7) | collective-permute-done | bytes 1048608 | tf_op jit(solution)/shard_map/ppermute | solution.py:38
  377.6 20.6 %collective-permute-done.5 = bf16[256,2048]{1,0:T(8,128)(2,1)S(1)} collective-permute-done((bf16[256,2048]{1,0:T(8,128)(2,1)S(1)}, bf16[256,2048]{1,0:T(8,128)(2,1)S(1)}, u32[]{:S(2)}, u32[]{:S(2)}) %collective-permute-start.5) | collective-permute-done | bytes 1048608 | tf_op jit(solution)/shard_map/ppermute | solution.py:38
  398.2 3.3 fusion.86
  401.6 6.8 reshape.567
  409.9 72.6 %all-gather.9.cloned.1.call-done = bf16[1024,2048]{1,0:T(8,128)(2,1)} async-done(((bf16[256,2048]{1,0:T(8,128)(2,1)}), bf16[1024,2048]{1,0:T(8,128)(2,1)}) %all-gather.9.cloned.1.call-update) | async-done | bytes 4194320 | tf_op jit(solution)/shard_map/all_gather | solution.py:712
  482.5 13.2 %fusion.12 = (f32[1024,1024]{1,0:T(8,128)}, bf16[1024,1024]{1,0:T(8,128)(2,1)}) fusion(bf16[1024,1024]{1,0:T(8,128)(2,1)} %get-tuple-element.26, bf16[1024,1024]{1,0:T(8,128)(2,1)} %get-tuple-element.27, bf16[1024,2048]{1,0:T(8,128)(2,1)} %all-gather.9.cloned.1.call-done, bf16[1024,2048]{1,0:T(8,128)(2,1)} %w_out.1), kind=kOutput, calls=%fused_computation.21 | convolution fusion | flops 4310695936 | bytes 18874368 | tf_op jit(solution)/shard_map/dot_general | solution.py:146
  495.7 6.6 reshape.566
  502.3 5.3 bitcast_reduce_fusion
  508.2 1.7 fusion.22
  510.6 2.1 copy-done.1
  512.7 1.4 fusion.61
  514.4 9.4 %convolution_convert_fusion.2 = bf16[2048,1024]{1,0:T(8,128)(2,1)} fusion(bf16[1024,1024]{1,0:T(8,128)(2,1)} %copy-done.37, bf16[512,2048]{1,0:T(8,128)(2,1)} %collective-permute-done.1, bf16[256,2048]{1,0:T(8,128)(2,1)} %collective-permute-done, bf16[256,2048]{1,0:T(8,128)(2,1)} %copy-done.13), kind=kOutput, calls=%fused_computation.62 | convolution fusion | flops 4309647360 | bytes 10485760 | tf_op jit(solution)/shard_map/dot_general | solution.py:140
  523.8 9.5 %convolution_convert_fusion.1 = bf16[1024,2048]{1,0:T(8,128)(2,1)} fusion(bf16[1024,1024]{1,0:T(8,128)(2,1)} %get-tuple-element.49, bf16[1024,2048]{1,0:T(8,128)(2,1)} %bitcast.200), kind=kOutput, calls=%fused_computation.61 | convolution fusion | flops 4297064448 | bytes 10485760 | tf_op jit(solution)/shard_map/dot_general | solution.py:140
  533.9 4.5 reshape.568
  538.3 2.1 reshape.569
  540.7 7.4 convolution_convert_fusion.3
  548.4 1.2 copy-done.19
  552.3 1.5 fusion.89
  553.9 3.0 fusion.95
  558.4 6.7 fusion.97
  565.1 2.2 fusion.16
  567.4 3.4 fusion.65
  575.0 8.7 %subtract_convert_fusion = (bf16[1024,2,128]{2,1,0:T(2,128)(2,1)S(1)}, bf16[1024,2,128]{2,1,0:T(2,128)(2,1)S(1)}, bf16[1024,2,128]{2,1,0:T(2,128)(2,1)S(1)}, bf16[1024,2,128]{2,1,0:T(2,128)(2,1)S(1)}) fusion(f32[1024,2,128]{2,0,1:T(8,128)S(1)} %get-tuple-element.60, f32[1024,2,128]{2,0,1:T(8,128)S(1)} %get-tuple-element.59, f32[1024,128]{1,0:T(8,128)S(1)} %copy-done.17, ...), kind=kLoop, calls=%fused_computation.146 | loop fusion | flops 4194304 | bytes 7340032 | tf_op jit(solution)/shard_map/convert.6
  587.5 2.2 copy.102
  590.3 6.1 fusion.94
  596.4 6.9 fusion.96
  603.3 11.7 %add_convert_fusion = bf16[1024,2048]{1,0:T(8,128)(2,1)} fusion(f32[1024,2048]{1,0:T(8,128)S(1)} %bitcast.186, f32[1024,2048]{1,0:T(8,128)} %fusion.96, f32[1024,2048]{1,0:T(8,128)} %fusion.94, bf16[1024,512]{1,0:T(8,128)(2,1)S(1)} %bitcast.189, bf16[2048,512]{1,0:T(8,128)(2,1)} %w_key.1), kind=kOutput, calls=%fused_computation.3 | convolution fusion | flops 2155872256 | bytes 32505856 | tf_op jit(solution)/shard_map/dot_general | solution.py:146
  615.1 19.3 %convolution_convert_fusion = bf16[2048,3072]{1,0:T(8,128)(2,1)} fusion(bf16[1024,2048]{1,0:T(8,128)(2,1)} %bitcast.198, bf16[1024,1024]{1,0:T(8,128)(2,1)} %get-tuple-element.52, bf16[1024,1024]{1,0:T(8,128)(2,1)} %bitcast.194, bf16[1024,512]{1,0:T(8,128)(2,1)S(1)} %bitcast.190, bf16[1024,512]{1,0:T(8,128)(2,1)S(1)} %bitcast.196), kind=kOutput, calls=%fused_computation.2 | convolution fusion | flops 12916359168 | bytes 23068672 | tf_op jit(solution)/shard_map/dot_general | solution.py:140
  634.5 3.2 dynamic-slice_bitcast_fusion
  637.8 10.1 %collective-permute-done.8 = bf16[4,256,3072]{2,1,0:T(8,128)(2,1)S(1)} collective-permute-done((bf16[4,256,3072]{2,1,0:T(8,128)(2,1)S(1)}, bf16[4,256,3072]{2,1,0:T(8,128)(2,1)S(1)}, u32[]{:S(2)}, u32[]{:S(2)}) %collective-permute-start.8) | collective-permute-done | bytes 6291488 | tf_op jit(solution)/shard_map/ppermute | solution.py:33
  647.9 8.3 fusion
  656.3 1.2 copy-done.5
  657.7 2.2 fusion.93
  660.1 1.5 collective-permute-start.11
  661.6 1.4 fusion.92
  663.0 3.1 collective-permute-start.12
  667.5 23.6 %collective-permute-done.10 = bf16[256,1024]{1,0:T(8,128)(2,1)} collective-permute-done((bf16[256,1024]{1,0:T(8,128)(2,1)}, bf16[256,1024]{1,0:T(8,128)(2,1)}, u32[]{:S(2)}, u32[]{:S(2)}) %collective-permute-start.10) | collective-permute-done | bytes 524320 | tf_op jit(solution)/shard_map/ppermute | solution.py:96
  691.1 2.4 convert_add_fusion.3
  693.5 37.3 %collective-permute-done.12 = bf16[128,2048]{1,0:T(8,128)(2,1)S(1)} collective-permute-done((bf16[128,2048]{1,0:T(8,128)(2,1)S(1)}, bf16[128,2048]{1,0:T(8,128)(2,1)S(1)}, u32[]{:S(2)}, u32[]{:S(2)}) %collective-permute-start.12) | collective-permute-done | bytes 524320 | tf_op jit(solution)/shard_map/ppermute | solution.py:96
  732.0 2.1 convert_element_type.303
  734.2 42.5 %reduce-scatter.6.cloned.1.call-done = bf16[256,2048]{1,0:T(8,128)(2,1)} async-done(((bf16[1024,2048]{1,0:T(8,128)(2,1)}), bf16[256,2048]{1,0:T(8,128)(2,1)}) %reduce-scatter.6.cloned.1.call-update) | async-done | bytes 1048592 | tf_op jit(solution)/shard_map/reduce_scatter | solution.py:754
  776.6 2.2 fusion.40
  778.8 40.0 %all-reduce = (f32[2048]{0:T(1024)}, f32[2048]{0:T(1024)}) all-reduce(f32[2048]{0:T(1024)S(1)} %get-tuple-element.40, f32[2048]{0:T(1024)S(1)} %get-tuple-element.35), channel_id=1, replica_groups=mesh['seq'=8,'mp'=4] {'seq','mp'}, use_global_device_ids=true, to_apply=%region_12.13 | all-reduce | flops 4096 | bytes 32768 | tf_op jit(solution)/shard_map/psum | solution.py:761
  818.9 3.1 fusion.37
  821.9 28.9 %reduce-scatter.8.cloned.1.call-done = bf16[256,3072]{1,0:T(8,128)(2,1)} async-done(((bf16[1024,3072]{1,0:T(8,128)(2,1)}), bf16[256,3072]{1,0:T(8,128)(2,1)}) %reduce-scatter.8.cloned.1.call-update) | async-done | bytes 1572880 | tf_op jit(solution)/shard_map/reduce_scatter | solution.py:73
  850.9 2.9 fusion.90
  (175 shorter events, 34.1 us)
Async XLA Ops:
  7.2 269.3 %all-gather.5.cloned.1.call-start = ((), (), s32[]{:S(2)}) async-start(), calls=%async_computation.5 | async-start | bytes 4718592 | tf_op jit(solution)/shard_map/all_gather | solution.py:61
  8.3 27.3 %collective-permute-start.2 = (bf16[256,1024]{1,0:T(8,128)(2,1)S(1)}, bf16[256,1024]{1,0:T(8,128)(2,1)S(1)}, u32[]{:S(2)}, u32[]{:S(2)}) collective-permute-start(bf16[256,1024]{1,0:T(8,128)(2,1)S(1)} %constant_dynamic-slice_fusion.1), channel_id=1, source_target_pairs={{0,2},{1,3},{2,0},{3,1},{4,6},{5,7},{6,4},{7,5},{8,10},{9,11},{10,... | collective-permute-start | bytes 1572872 | tf_op jit(solution)/shard_map/ppermute | solution.py:38
  35.6 0.8 copy-start.28
  36.4 284.2 %all-gather.7.cloned.1.call-start = ((), (), s32[]{:S(2)}) async-start(), calls=%async_computation.6 | async-start | bytes 4718592 | tf_op jit(solution)/shard_map/all_gather | solution.py:61
  219.1 3.9 copy-start
  219.1 3.9 copy-start.29
  223.4 72.2 %copy-start.13 = (bf16[256,2048]{1,0:T(8,128)(2,1)}, bf16[256,2048]{1,0:T(8,128)(2,1)S(1)}, u32[]{:S(2)}) copy-start(bf16[256,2048]{1,0:T(8,128)(2,1)S(1)} %multiply_convert_fusion.5) | copy-start | bytes 3145732
  223.4 22.3 %collective-permute-start = (bf16[256,2048]{1,0:T(8,128)(2,1)S(1)}, bf16[256,2048]{1,0:T(8,128)(2,1)}, u32[]{:S(2)}, u32[]{:S(2)}) collective-permute-start(bf16[256,2048]{1,0:T(8,128)(2,1)S(1)} %multiply_convert_fusion.5), channel_id=1, source_target_pairs={{0,1},{1,0},{2,3},{3,2},{4,5},{5,4},{6,7},{7,6},{8,9},{9,8},{10,11... | collective-permute-start | bytes 3145736 | tf_op jit(solution)/shard_map/ppermute | solution.py:38
  248.4 28.0 %collective-permute-start.1 = (bf16[512,2048]{1,0:T(8,128)(2,1)}, bf16[512,2048]{1,0:T(8,128)(2,1)}, u32[]{:S(2)}, u32[]{:S(2)}) collective-permute-start(bf16[512,2048]{1,0:T(8,128)(2,1)} %pad_maximum_fusion.1), channel_id=1, source_target_pairs={{0,4},{4,0},{8,12},{12,8},{16,20},{20,16},{24,28},{28,24},{1,5},{5... | collective-permute-start | bytes 6291464 | tf_op jit(solution)/shard_map/ppermute | solution.py:33
  249.5 26.6 %collective-permute-start.3 = (bf16[128,2048]{1,0:T(8,128)(2,1)S(1)}, bf16[128,2048]{1,0:T(8,128)(2,1)}, u32[]{:S(2)}, u32[]{:S(2)}) collective-permute-start(bf16[128,2048]{1,0:T(8,128)(2,1)S(1)} %constant_dynamic-slice_fusion), channel_id=1, source_target_pairs={{0,2},{1,3},{2,0},{3,1},{4,6},{5,7},{6,4},{7,5},{8,10},{9,11},{10,... | collective-permute-start | bytes 1572872 | tf_op jit(solution)/shard_map/ppermute | solution.py:38
  276.2 206.3 %all-gather.9.cloned.1.call-start = ((), (), s32[]{:S(2)}) async-start(), calls=%async_computation.7 | async-start | bytes 5242880 | tf_op jit(solution)/shard_map/all_gather | solution.py:712
  320.6 11.6 %copy-start.30 = (bf16[2048,1024]{1,0:T(8,128)(2,1)S(1)}, bf16[2048,1024]{1,0:T(8,128)(2,1)}, u32[]{:S(2)}) copy-start(bf16[2048,1024]{1,0:T(8,128)(2,1)} %param.19) | copy-start | bytes 12582916
  332.2 4.6 copy-start.37
  332.2 8.2 copy-start.36
  336.8 3.6 copy-start.31
  337.1 12.4 %collective-permute-start.6 = (bf16[512,2048]{1,0:T(8,128)(2,1)S(1)}, bf16[512,2048]{1,0:T(8,128)(2,1)S(1)}, u32[]{:S(2)}, u32[]{:S(2)}) collective-permute-start(bf16[512,2048]{1,0:T(8,128)(2,1)S(1)} %slice.191), channel_id=1, source_target_pairs={{0,4},{4,0},{8,12},{12,8},{16,20},{20,16},{24,28},{28,24},{1,5},{5... | collective-permute-start | bytes 6291464 | tf_op jit(solution)/shard_map/ppermute | solution.py:33
  345.5 7.8 collective-permute-start.4
  350.5 26.1 %collective-permute-start.7 = (bf16[256,2048]{1,0:T(8,128)(2,1)S(1)}, bf16[256,2048]{1,0:T(8,128)(2,1)S(1)}, u32[]{:S(2)}, u32[]{:S(2)}) collective-permute-start(bf16[256,2048]{1,0:T(8,128)(2,1)S(1)} %slice.193), channel_id=1, source_target_pairs={{0,1},{1,0},{2,3},{3,2},{4,5},{5,4},{6,7},{7,6},{8,9},{9,8},{10,11... | collective-permute-start | bytes 3145736 | tf_op jit(solution)/shard_map/ppermute | solution.py:38
  354.2 44.0 %copy-start.26 = (bf16[256,2048]{1,0:T(8,128)(2,1)S(1)}, bf16[256,2048]{1,0:T(8,128)(2,1)}, u32[]{:S(2)}) copy-start(bf16[256,2048]{1,0:T(8,128)(2,1)} %cot.1) | copy-start | bytes 3145732
  354.4 43.8 %collective-permute-start.5 = (bf16[256,2048]{1,0:T(8,128)(2,1)S(1)}, bf16[256,2048]{1,0:T(8,128)(2,1)S(1)}, u32[]{:S(2)}, u32[]{:S(2)}) collective-permute-start(bf16[256,2048]{1,0:T(8,128)(2,1)S(1)} %slice.194), channel_id=1, source_target_pairs={{0,1},{1,0},{2,3},{3,2},{4,5},{5,4},{6,7},{7,6},{8,9},{9,8},{10,11... | collective-permute-start | bytes 3145736 | tf_op jit(solution)/shard_map/ppermute | solution.py:38
  401.5 6.8 copy-start.25
  401.5 7.2 copy-start.24
  401.5 165.8 %all-gather.11.cloned.1.call-start = ((), (), s32[]{:S(2)}) async-start(), calls=%async_computation.8 | async-start | bytes 2621440 | tf_op jit(solution)/shard_map/all_gather | solution.py:22
  502.3 5.3 copy-start.3
  502.3 5.9 copy-start.4
  510.6 2.1 copy-start.1
  514.1 143.6 %reduce-scatter.12.cloned.1.call-start = ((), (), s32[]{:S(2)}) async-start(), calls=%async_computation.12 | async-start | bytes 5242880 | tf_op jit(solution)/shard_map/reduce_scatter | solution.py:82
  523.8 137.8 %reduce-scatter.14.cloned.1.call-start = ((), (), s32[]{:S(2)}) async-start(), calls=%async_computation.13 | async-start | bytes 5242880 | tf_op jit(solution)/shard_map/reduce_scatter | solution.py:82
  533.4 198.7 %reduce-scatter.10.cloned.1.call-start = ((), (), s32[]{:S(2)}) async-start(), calls=%async_computation.11 | async-start | bytes 2621440 | tf_op jit(solution)/shard_map/reduce_scatter | solution.py:73
  548.1 1.6 copy-start.19
  548.1 1.7 copy-start.27
  548.3 2.2 copy-start.11
  548.4 3.2 copy-start.22
  548.4 16.8 %collective-permute-start.9 = (bf16[4,128,2048]{2,1,0:T(8,128)(2,1)S(1)}, bf16[4,128,2048]{2,1,0:T(8,128)(2,1)S(1)}, u32[]{:S(2)}, u32[]{:S(2)}) collective-permute-start(bf16[4,128,2048]{2,1,0:T(8,128)(2,1)S(1)} %dynamic-slice_bitcast_fusion.1), channel_id=1, source_target_pairs={{0,4},{4,0},{8,12},{12,8},{16,20},{20,16},{24,28},{28,24},{1,5},{5... | collective-permute-start | bytes 6291464 | tf_op jit(solution)/shard_map/ppermute | solution.py:33
  550.5 1.0 copy-start.14
  552.3 1.6 copy-start.23
  553.8 3.4 copy-start.33
  553.8 4.6 copy-start.38
  567.3 209.3 %reduce-scatter.6.cloned.1.call-start = ((), (), s32[]{:S(2)}) async-start(), calls=%async_computation.9 | async-start | bytes 5242880 | tf_op jit(solution)/shard_map/reduce_scatter | solution.py:754
  567.4 3.9 copy-start.2
  567.4 4.6 copy-start.20
  572.0 1.2 copy-start.15
  573.2 1.2 copy-start.9
  573.2 1.5 copy-start.10
  573.2 1.7 copy-start.17
  573.2 1.8 copy-start.18
  583.7 2.8 copy-start.8
  583.8 2.8 copy-start.12
  587.5 2.8 copy-start.35
  590.2 6.2 copy-start.21
  590.2 6.2 copy-start.34
  590.3 13.1 %slice-start = ((s8[8388608]{0:T(1024)(128)(4,1)}), s8[4194304]{0:T(1024)(128)(4,1)S(1)}, s32[]{:S(2)}) async-start(s8[8388608]{0:T(1024)(128)(4,1)} %bitcast.185), calls=%async_computation.14 | async-start | bytes 8388608
  596.4 6.9 slice-start.1
  615.1 235.8 %reduce-scatter.8.cloned.1.call-start = ((), (), s32[]{:S(2)}) async-start(), calls=%async_computation.10 | async-start | bytes 7864320 | tf_op jit(solution)/shard_map/reduce_scatter | solution.py:73
  637.7 10.2 %collective-permute-start.8 = (bf16[4,256,3072]{2,1,0:T(8,128)(2,1)S(1)}, bf16[4,256,3072]{2,1,0:T(8,128)(2,1)S(1)}, u32[]{:S(2)}, u32[]{:S(2)}) collective-permute-start(bf16[4,256,3072]{2,1,0:T(8,128)(2,1)S(1)} %dynamic-slice_bitcast_fusion), channel_id=1, source_target_pairs={{0,4},{4,0},{8,12},{12,8},{16,20},{20,16},{24,28},{28,24},{1,5},{5... | collective-permute-start | bytes 18874376 | tf_op jit(solution)/shard_map/ppermute | solution.py:33
  656.2 1.2 copy-start.5
  660.0 31.1 %collective-permute-start.10 = (bf16[256,1024]{1,0:T(8,128)(2,1)}, bf16[256,1024]{1,0:T(8,128)(2,1)}, u32[]{:S(2)}, u32[]{:S(2)}) collective-permute-start(bf16[256,1024]{1,0:T(8,128)(2,1)} %get-tuple-element.71), channel_id=1, source_target_pairs={{0,4},{1,5},{2,6},{3,7},{4,2},{5,3},{6,0},{7,1},{8,12},{9,13},{10,... | collective-permute-start | bytes 1572872 | tf_op jit(solution)/shard_map/ppermute | solution.py:96
  660.1 31.0 %collective-permute-start.11 = (bf16[256,1024]{1,0:T(8,128)(2,1)}, bf16[256,1024]{1,0:T(8,128)(2,1)}, u32[]{:S(2)}, u32[]{:S(2)}) collective-permute-start(bf16[256,1024]{1,0:T(8,128)(2,1)} %get-tuple-element.70), channel_id=1, source_target_pairs={{4,6},{5,7},{6,4},{7,5},{12,14},{13,15},{14,12},{15,13},{20,22},{2... | collective-permute-start | bytes 1572872 | tf_op jit(solution)/shard_map/ppermute | solution.py:97
  661.6 69.3 %copy-start.16 = (bf16[256,2048]{1,0:T(8,128)(2,1)S(1)}, bf16[256,2048]{1,0:T(8,128)(2,1)}, u32[]{:S(2)}) copy-start(bf16[256,2048]{1,0:T(8,128)(2,1)} %reduce-scatter.14.cloned.1.call-done) | copy-start | bytes 3145732
  663.0 113.7 %copy-start.32 = (f32[2048]{0:T(1024)S(1)}, f32[2048]{0:T(1024)}, u32[]{:S(2)}) copy-start(f32[2048]{0:T(1024)} %param.12) | copy-start | bytes 24580
  663.0 67.9 %collective-permute-start.12 = (bf16[128,2048]{1,0:T(8,128)(2,1)S(1)}, bf16[128,2048]{1,0:T(8,128)(2,1)S(1)}, u32[]{:S(2)}, u32[]{:S(2)}) collective-permute-start(bf16[128,2048]{1,0:T(8,128)(2,1)S(1)} %get-tuple-element.69), channel_id=1, source_target_pairs={{0,4},{1,5},{2,6},{3,7},{4,2},{5,3},{6,0},{7,1},{8,12},{9,13},{10,... | collective-permute-start | bytes 1572872 | tf_op jit(solution)/shard_map/ppermute | solution.py:96
  666.1 64.7 %collective-permute-start.13 = (bf16[128,2048]{1,0:T(8,128)(2,1)S(1)}, bf16[128,2048]{1,0:T(8,128)(2,1)S(1)}, u32[]{:S(2)}, u32[]{:S(2)}) collective-permute-start(bf16[128,2048]{1,0:T(8,128)(2,1)S(1)} %get-tuple-element.68), channel_id=1, source_target_pairs={{4,6},{5,7},{6,4},{7,5},{12,14},{13,15},{14,12},{15,13},{20,22},{2... | collective-permute-start | bytes 1572872 | tf_op jit(solution)/shard_map/ppermute | solution.py:97
  667.5 151.4 %copy-start.6 = (f32[256,2048]{1,0:T(8,128)S(1)}, f32[256,2048]{1,0:T(8,128)}, u32[]{:S(2)}) copy-start(f32[256,2048]{1,0:T(8,128)} %get-tuple-element.48) | copy-start | bytes 6291460
  850.9 2.9 copy-start.7
Sparse Core Ops, SparseCore 0:
  36.5 37.9 all-gather.4
  276.3 44.2 all-gather.6
  401.7 80.7 all-gather.8
  514.2 21.1 all-gather.10
  538.2 52.7 reduce-scatter.11
  594.1 52.6 reduce-scatter.13
  649.7 35.1 reduce-scatter.9
  687.4 89.2 reduce-scatter.5
  779.6 71.1 reduce-scatter.7

commit v3 on v2

v3 whole, which is shorter than its diff:
```python
import math

import jax
import jax.numpy as jnp
from jax import lax
from jax.experimental import pallas as pl
from jax.experimental.pallas import tpu as pltpu
from jax.sharding import PartitionSpec as P

DK = 256
DV = 512
STRETCH = 256
SEQ_DEVS = 4


eps = 1e-05


def same_core():
    count = lax.axis_size("seq")
    return [list(range(core, count, 2)) for core in range(2)]


def angles(positions):
    half = DK // 2
    freq = jnp.exp(-math.log(10000.0) * jnp.arange(half, dtype=jnp.float32) / (half - 1))
    phase = positions.astype(jnp.float32)[:, None] * freq[None, :]
    return (jnp.cos(phase)[:, None, :], jnp.sin(phase)[:, None, :])


def product_t(left, right):
    return lax.dot_general(
        left, right, (((0,), (0,)), ((), ())), preferred_element_type=jnp.float32
    )


def product_rt(left, right):
    return lax.dot_general(
        left, right, (((1,), (1,)), ((), ())), preferred_element_type=jnp.float32
    )


MESH = pl.DeviceIdType.MESH
LIMIT = 62 * 1024 * 1024


def remote(src, dst, send, recv, s, z):
    return pltpu.make_async_remote_copy(
        src_ref=src,
        dst_ref=dst,
        send_sem=send,
        recv_sem=recv,
        device_id=(s, z),
        device_id_type=MESH,
    )


def greet(partners):
    barrier = pltpu.get_barrier_semaphore()
    count = 0
    for present, s, z in partners:

        @pl.when(present)
        def _():
            pl.semaphore_signal(barrier, inc=1, device_id=(s, z), device_id_type=MESH)

        count = count + jnp.where(present, 1, 0)
    pl.semaphore_wait(barrier, count)


def dot(left, right):
    return jnp.dot(left, right, preferred_element_type=jnp.float32)


def line_push(x, send, recv, s, z, slot, way):
    return remote(x.at[slot], x.at[slot], send.at[way, slot], recv.at[slot], s, z + 1 - 2 * way)


def line_gather(x, send, recv, s, z, depth, use, after=None):
    @pl.when(z < depth - 1)
    def _():
        line_push(x, send, recv, s, z, z, 0).start()

    @pl.when(z > 0)
    def _():
        line_push(x, send, recv, s, z, z, 1).start()

    def one(turn, _):
        away = (turn + 1) // 2
        left, right = z - away, z + away

        @pl.when((turn % 2 == 1) & (left >= 0))
        def _():
            remote(x.at[left], x.at[left], send.at[0, left], recv.at[left], s, z - 1).wait_recv()

            @pl.when(z < depth - 1)
            def _():
                line_push(x, send, recv, s, z, left, 0).start()

        @pl.when((turn % 2 == 1) & (right < depth))
        def _():
            remote(x.at[right], x.at[right], send.at[1, right], recv.at[right], s, z + 1).wait_recv()

            @pl.when(z > 0)
            def _():
                line_push(x, send, recv, s, z, right, 1).start()

        if after is not None:
            after(turn)
        slot = jnp.where(turn % 2 == 1, left, right)

        @pl.when((slot >= 0) & (slot < depth))
        def _():
            use(slot)

        return 0

    lax.fori_loop(0, 2 * depth - 1, one, 0)


def line_gather_end(x, send, recv, s, z, depth):
    def one(slot, _):
        @pl.when((slot <= z) & (z < depth - 1))
        def _():
            line_push(x, send, recv, s, z, slot, 0).wait_send()

        @pl.when((slot >= z) & (z > 0))
        def _():
            line_push(x, send, recv, s, z, slot, 1).wait_send()

        return 0

    lax.fori_loop(0, depth, one, 0)


def add_rows(into, other):
    step = 32

    def one(i, _):
        rows = pl.ds(pl.multiple_of(i * step, step), step)
        into[rows, :] = (
            into[rows, :].astype(jnp.float32) + other[rows, :].astype(jnp.float32)
        ).astype(into.dtype)
        return 0

    lax.fori_loop(0, into.shape[0] // step, one, 0)


def line_scatter(sbuf, rbuf, total, send, recv, s, z, depth, partial, own, hook=None):
    def right(j):
        return remote(sbuf.at[j], rbuf.at[j], send.at[j], recv.at[j], s, z + 1)

    def left(j):
        slot = jnp.where(j == z - 1, depth, j)
        return remote(sbuf.at[j], rbuf.at[slot], send.at[j], recv.at[slot], s, z - 1)

    def arrived(slot, sender):
        remote(sbuf.at[0], rbuf.at[slot], send.at[0], recv.at[slot], s, sender).wait_recv()

    def first(turn, _):
        up = depth - 1 + z - turn // 2
        down = turn // 2 - (depth - 1) + z
        j = jnp.where(turn % 2 == 0, up, down)
        valid = jnp.where(turn % 2 == 0, (up > z) & (up < depth), (down >= 0) & (down < z))

        @pl.when(valid)
        def _():
            partial(j)

            @pl.when((z == 0) & (j > z))
            def _():
                right(j).start()

            @pl.when((z == depth - 1) & (j < z))
            def _():
                left(j).start()

        return 0

    lax.fori_loop(0, 2 * (depth - 1), first, 0)
    own()

    def event(turn, _):
        up = depth - 1 + z - turn
        down = turn - (depth - 1) + z

        @pl.when((z > 0) & (up >= z) & (up < depth))
        def _():
            arrived(up, z - 1)

            @pl.when(up > z)
            def _():
                add_rows(sbuf.at[up], rbuf.at[up])
                right(up).start()

            @pl.when(up == z)
            def _():
                add_rows(total, rbuf.at[up])

        @pl.when((z < depth - 1) & (down >= 0) & (down <= z))
        def _():
            slot = jnp.where(down == z, depth, down)
            arrived(slot, z + 1)

            @pl.when(down < z)
            def _():
                add_rows(sbuf.at[down], rbuf.at[down])
                left(down).start()

            @pl.when(down == z)
            def _():
                add_rows(total, rbuf.at[depth])

        if hook is not None:
            hook(turn)
        return 0

    lax.fori_loop(0, depth, event, 0)

    def end(j, _):
        @pl.when(j > z)
        def _():
            right(j).wait_send()

        @pl.when(j < z)
        def _():
            left(j).wait_send()

        return 0

    lax.fori_loop(0, depth, end, 0)


def centred(rows):
    centre = rows - jnp.mean(rows, axis=-1, keepdims=True)
    inverse = lax.rsqrt(jnp.mean(centre * centre, axis=-1, keepdims=True) + eps)
    return centre * inverse, inverse


def block(rows, index):
    return pl.ds(pl.multiple_of(index * rows, rows), rows)


def attend_kernel(
    tok,
    gain,
    cot,
    w_query,
    w_key,
    w_value,
    w_gate,
    w_out,
    w_up,
    w_down,
    cosine,
    sine,
    mask,
    q_scale,
    k_scale,
    decay,
    x_out,
    q_out,
    k_out,
    v_out,
    gp_out,
    gn_out,
    gated_out,
    inv_out,
    p_out,
    r_out,
    hidden_out,
    cot_rows,
    far_up,
    far_down,
    xg,
    q,
    k,
    v,
    gp,
    gn,
    gated,
    inv,
    weights,
    grown,
    entering,
    tile,
    state,
    state_in,
    state_to,
    rbuf,
    total,
    wq,
    wk,
    wv,
    wg,
    wo,
    load,
    save,
    g_send,
    g_recv,
    s_send,
    s_recv,
    c_send,
    c_recv,
    x_send,
    x_recv,
    f_send,
    f_recv,
    p_send,
    p_recv,
):
    f32, bf16 = jnp.float32, jnp.bfloat16
    depth = xg.shape[0]
    rows = xg.shape[1]
    heads = mask.shape[0]
    s, z = lax.axis_index("seq"), lax.axis_index("mp")
    place = lax.rem(s, SEQ_DEVS)
    pair = z + 1 - 2 * lax.rem(z, 2)
    twin = s + 1 - 2 * lax.rem(s, 2)
    loads = [
        pltpu.make_async_copy(a, b, load.at[i])
        for i, (a, b) in enumerate(
            [(w_query, wq), (w_key, wk), (w_value, wv), (w_gate, wg), (w_out, wo)]
        )
    ]
    for copy in loads:
        copy.start()

    def norm(i, _):
        part = pl.ds(pl.multiple_of(i * 32, 32), 32)
        unit, _ = centred(tok[part, :].astype(f32))
        xg[z, part, :] = (unit * gain[...]).astype(bf16)
        return 0

    lax.fori_loop(0, rows // 32, norm, 0)
    count = lax.axis_size("seq")
    across = flip(z, 2)
    greet(
        [(z > 0, s, z - 1), (z < depth - 1, s, z + 1), (z >= 0, s, across)]
        + [(s != other, other, z) for other in range(count)]
    )
    tall, few = w_up.shape[0] // count, w_down.shape[0] // count
    mine = pltpu.make_async_copy(cot, cot_rows.at[0], x_send.at[3])
    near = remote(cot, cot_rows.at[2], x_send.at[1], x_recv.at[1], twin, z)
    swap = remote(cot, cot_rows.at[1], x_send.at[0], x_recv.at[0], s, pair)
    far = remote(cot_rows.at[1], cot_rows.at[3], x_send.at[2], x_recv.at[2], twin, z)

    def piece(source):
        return block(tall, source), block(few, source)

    up_at, down_at = piece(s)
    moves = [
        remote(w_up.at[up_at], far_up.at[up_at], f_send.at[0], f_recv.at[0], s, across),
        remote(w_down.at[down_at], far_down.at[down_at], f_send.at[1], f_recv.at[1], s, across),
    ]
    edge = (z == 0) | (z == depth - 1)

    def spread(source, chip):
        up_, down_ = piece(source)
        to = 2 * chip + 1
        return [
            remote(far_up.at[up_], far_up.at[up_], p_send.at[0, chip], p_recv.at[0, source], to, z),
            remote(
                far_down.at[down_], far_down.at[down_], p_send.at[1, chip], p_recv.at[1, source], to, z
            ),
        ]

    mine.start()
    near.start()

    @pl.when(place == 0)
    def _():
        state_in[...] = jnp.zeros_like(state_in)

    def after(turn):
        @pl.when(edge & (turn == 1))
        def _():
            swap.start()

        @pl.when(edge & (turn == 3))
        def _():
            for copy in moves:
                copy.start()

    def use(j):
        at = block(rows, j)

        @pl.when(j == z)
        def _():
            for copy in loads:
                copy.wait()

        c, sn = cosine[at, :], sine[at, :]
        for h in range(heads):
            cols = slice(h * DK, (h + 1) * DK)
            for w, out in ((wq, q), (wk, k)):
                p = dot(xg[j], w[:, cols])
                a, b = p[:, : DK // 2], p[:, DK // 2 :]
                out[at, h * DK : h * DK + DK // 2] = (a * c - b * sn).astype(bf16)
                out[at, h * DK + DK // 2 : (h + 1) * DK] = (b * c + a * sn).astype(bf16)
        for h in range(heads):
            wide = slice(h * DV, (h + 1) * DV)
            v[at, wide] = dot(xg[j], wv[:, wide]).astype(bf16)
            gp[at, wide] = dot(xg[j], wg[:, wide])
        for h in range(heads):
            cols = slice(h * DK, (h + 1) * DK)
            wide = slice(h * DV, (h + 1) * DV)
            kb, vb = k[at, cols], v[at, wide]
            vd = (vb.astype(f32) * k_scale[h]).astype(bf16)
            grown[h, j] = product_t(kb, vd)
            weights[h, j] = (product_rt(q[at, cols], kb) * mask[h]).astype(bf16)

    line_gather(xg, g_send, g_recv, s, z, depth, use, after)
    @pl.when(jnp.logical_not(edge))
    def _():
        for copy in moves:
            copy.start()

    for h in range(heads):
        state[h] = grown[h, 0]
        for b in range(1, depth):
            state[h] = decay[h, 0] * state[h] + grown[h, b]
    chain = remote(state_to, state_in, c_send, c_recv, s + 1, z)

    @pl.when(place > 0)
    def _():
        remote(state_to, state_in, c_send, c_recv, s - 1, z).wait_recv()

    @pl.when(place < SEQ_DEVS - 1)
    def _():
        for h in range(heads):
            state_to[h] = (decay[h, 1] * state_in[h].astype(f32) + state[h]).astype(bf16)
        chain.start()

    saves = [
        pltpu.make_async_copy(a, b, save.at[i])
        for i, (a, b) in enumerate(
            [
                (xg, x_out),
                (q, q_out),
                (k, k_out),
                (v, v_out),
                (gp, gp_out),
                (weights, p_out),
                (entering, r_out),
                (gn, gn_out),
                (gated, gated_out),
                (inv, inv_out),
            ]
        )
    ]
    for copy in saves[:6]:
        copy.start()

    def hand_out():
        for copy in moves:
            copy.wait_recv()

        def to_chip(chip, _):
            @pl.when(2 * chip + 1 != s)
            def _():
                for copy in spread(s, chip):
                    copy.start()

            return 0

        lax.fori_loop(0, count // 2, to_chip, 0)

    @pl.when(jnp.logical_not(edge))
    def _():
        hand_out()

    for h in range(heads):
        cols = slice(h * DK, (h + 1) * DK)
        wide = slice(h * DV, (h + 1) * DV)
        state[h] = state_in[h].astype(f32)

        def cross(b, _):
            at = block(rows, b)
            entering[h, b] = state[h].astype(bf16)
            state[h] = decay[h, 0] * state[h] + grown[h, b]
            qd = (q[at, cols].astype(f32) * q_scale[h]).astype(bf16)
            tile[...] = dot(weights[h, b], v[at, wide]) + dot(qd, entering[h, b])

            def norm(i, _):
                here = block(32, i)
                there = pl.ds(pl.multiple_of(b * rows + i * 32, 32), 32)
                unit, inverse = centred(tile[here, :])
                gate = gp[there, wide]
                gn[there, wide] = unit
                gated[there, wide] = (unit * gate / (1.0 + jnp.exp(-gate))).astype(bf16)
                inv[h, there, :] = jnp.broadcast_to(inverse, (32, inv.shape[2]))
                return 0

            lax.fori_loop(0, rows // 32, norm, 0)
            return 0

        lax.fori_loop(0, depth, cross, 0)
    for copy in saves[6:]:
        copy.start()
    line_gather_end(xg, g_send, g_recv, s, z, depth)
    saves[0].wait()
    wide = 512

    def hook(turn):
        @pl.when((turn == 0) & jnp.logical_not(edge))
        def _():
            swap.start()

        @pl.when((turn == 0) & edge)
        def _():
            hand_out()

        @pl.when(turn == 2)
        def _():
            swap.wait_recv()
            far.start()

    def partial(j):
        for n in range(0, total.shape[1], wide):
            xg[j, :, n : n + wide] = dot(gated[block(rows, j), :], wo[:, n : n + wide]).astype(bf16)

    def own():
        for n in range(0, total.shape[1], wide):
            total[:, n : n + wide] = tok[:, n : n + wide].astype(f32) + dot(
                gated[block(rows, z), :], wo[:, n : n + wide]
            )

    line_scatter(xg, rbuf, total, s_send, s_recv, s, z, depth, partial, own, hook)
    done = pltpu.make_async_copy(total, hidden_out, save.at[0])
    done.start()

    @pl.when(place < SEQ_DEVS - 1)
    def _():
        chain.wait_send()

    def sent(chip, _):
        @pl.when(2 * chip + 1 != s)
        def _():
            for copy in spread(s, chip):
                copy.wait_send()

        return 0

    lax.fori_loop(0, count // 2, sent, 0)

    def came(source, _):
        @pl.when((source != s) & (lax.rem(s, 2) == 1))
        def _():
            for copy in spread(source, 0):
                copy.wait_recv()

        return 0

    lax.fori_loop(0, count, came, 0)
    for copy in moves:
        copy.wait_send()
    swap.wait_send()
    near.wait()
    far.wait()
    mine.wait()
    for copy in saves[1:]:
        copy.wait()
    done.wait()


def attend(
    tok, gain, cot, w_query, w_key, w_value, w_gate, w_out, w_up, w_down, cosine, sine, mask, q_scale, k_scale, decay
):
    f32, bf16 = jnp.float32, jnp.bfloat16
    depth = lax.axis_size("mp")
    rows, width = tok.shape
    span = depth * rows
    heads = mask.shape[0]
    hk, hv = w_query.shape[1], w_value.shape[1]
    any_ = pl.BlockSpec(memory_space=pl.ANY)
    vmem = pl.BlockSpec(memory_space=pltpu.VMEM)
    shapes = [
        ((depth, rows, width), bf16),
        ((span, hk), bf16),
        ((span, hk), bf16),
        ((span, hv), bf16),
        ((span, hv), f32),
        ((span, hv), f32),
        ((span, hv), bf16),
        ((heads, span, 128), f32),
        ((heads, depth, rows, rows), bf16),
        ((heads, depth, DK, DV), bf16),
        ((rows, width), f32),
        ((4, rows, width), bf16),
        (w_up.shape, bf16),
        (w_down.shape, bf16),
    ]
    count = lax.axis_size("seq")
    dma = pltpu.SemaphoreType.DMA
    return pl.pallas_call(
        attend_kernel,
        out_shape=[jax.ShapeDtypeStruct(*one) for one in shapes],
        in_specs=[vmem, vmem, any_] + [any_] * 7 + [vmem] * 6,
        out_specs=[any_] * len(shapes),
        scratch_shapes=[
            pltpu.VMEM((depth, rows, width), bf16),
            pltpu.VMEM((span, hk), bf16),
            pltpu.VMEM((span, hk), bf16),
            pltpu.VMEM((span, hv), bf16),
            pltpu.VMEM((span, hv), f32),
            pltpu.VMEM((span, hv), f32),
            pltpu.VMEM((span, hv), bf16),
            pltpu.VMEM((heads, span, 128), f32),
            pltpu.VMEM((heads, depth, rows, rows), bf16),
            pltpu.VMEM((heads, depth, DK, DV), f32),
            pltpu.VMEM((heads, depth, DK, DV), bf16),
            pltpu.VMEM((rows, DV), f32),
            pltpu.VMEM((heads, DK, DV), f32),
            pltpu.VMEM((heads, DK, DV), bf16),
            pltpu.VMEM((heads, DK, DV), bf16),
            pltpu.VMEM((depth + 1, rows, width), bf16),
            pltpu.VMEM((rows, width), f32),
            pltpu.VMEM(w_query.shape, bf16),
            pltpu.VMEM(w_key.shape, bf16),
            pltpu.VMEM(w_value.shape, bf16),
            pltpu.VMEM(w_gate.shape, bf16),
            pltpu.VMEM(w_out.shape, bf16),
            dma((5,)),
            dma((10,)),
            dma((2, depth)),
            dma((depth,)),
            dma((depth,)),
            dma((depth + 1,)),
            dma,
            dma,
            dma((4,)),
            dma((3,)),
            dma((2,)),
            dma((2,)),
            dma((2, count // 2)),
            dma((2, count)),
        ],
        compiler_params=pltpu.CompilerParams(
            collective_id=0, has_side_effects=True, vmem_limit_bytes=LIMIT
        ),
        cost_estimate=pl.CostEstimate(
            flops=190 * 10**9, bytes_accessed=60 * 10**6, transcendentals=2 * 10**6
        ),
        name="attend",
    )(tok, gain, cot, w_query, w_key, w_value, w_gate, w_out, w_up, w_down, cosine, sine, mask, q_scale, k_scale, decay)


def row_loop(rows, step, body):
    def one(i, _):
        body(pl.ds(pl.multiple_of(i * step, step), step), i)
        return 0

    lax.fori_loop(0, rows // step, one, 0)


def norm_rows_back(grad_hat, unit, inverse):
    first = jnp.mean(grad_hat, axis=-1, keepdims=True)
    second = jnp.mean(grad_hat * unit, axis=-1, keepdims=True)
    return inverse * (grad_hat - first - unit * second)


def feed_kernel(
    hidden,
    gain,
    cot,
    cot_rows,
    w_up,
    w_down,
    far_up,
    far_down,
    y_keep,
    y_send,
    grad_hidden,
    gain_part,
    g_all_out,
    x,
    dy,
    act,
    du,
    part_y,
    part_x,
    got_x,
    got_y,
    u_tile,
    d_tile,
    g_all,
    up,
    down,
    load,
    save,
    send,
    recv,
):
    f32, bf16 = jnp.float32, jnp.bfloat16
    rows, width = hidden.shape
    units = up.shape[1]
    s, z = lax.axis_index("seq"), lax.axis_index("mp")
    pair = z + 1 - 2 * lax.rem(z, 2)
    twin = s + 1 - 2 * lax.rem(s, 2)
    own_loads = [
        pltpu.make_async_copy(w_up, up, load.at[0]),
        pltpu.make_async_copy(w_down, down, load.at[1]),
    ]
    far_loads = [
        pltpu.make_async_copy(far_up, up, load.at[0]),
        pltpu.make_async_copy(far_down, down, load.at[1]),
    ]

    @pl.when(lax.rem(s, 2) == 0)
    def _():
        for copy in own_loads:
            copy.start()

    @pl.when(lax.rem(s, 2) == 1)
    def _():
        for copy in far_loads:
            copy.start()

    rest = [
        pltpu.make_async_copy(cot_rows.at[r], dy.at[pl.ds(r * rows, rows)], load.at[2 + r])
        for r in range(4)
    ]
    loads = own_loads + rest
    for copy in rest:
        copy.start()

    def norm(here, i):
        unit, _ = centred(hidden[here, :])
        x[here, :] = (unit * gain[...]).astype(bf16)

    row_loop(rows, 32, norm)
    greet([(z >= 0, s, pair), (z >= 0, twin, z)])
    slot = [pl.ds(r * rows, rows) for r in range(4)]
    over = remote(x.at[slot[0]], x.at[slot[1]], send.at[0], recv.at[0], s, pair)
    near = remote(x.at[slot[0]], x.at[slot[2]], send.at[1], recv.at[1], twin, z)
    far = remote(x.at[slot[1]], x.at[slot[3]], send.at[2], recv.at[2], twin, z)
    near.start()
    over.start()
    back_near = remote(part_x.at[slot[2]], got_x.at[0], send.at[3], recv.at[3], twin, z)
    back_far = remote(part_x.at[slot[3]], got_x.at[1], send.at[4], recv.at[4], twin, z)
    back_over = remote(part_x.at[slot[1]], got_x.at[2], send.at[5], recv.at[5], s, pair)
    y_back = remote(
        part_y.at[pl.ds(2 * rows, 2 * rows)], got_y, send.at[6], recv.at[6], twin, z
    )
    for copy in loads:
        copy.wait()
    step = 512

    def one(turn, _):
        r = lax.rem(turn, 2) * 2 + turn // 2
        at = block(rows, r)

        @pl.when(turn == 1)
        def _():
            near.wait_recv()

        @pl.when(turn == 2)
        def _():
            over.wait_recv()
            far.start()

        @pl.when(turn == 3)
        def _():
            far.wait_recv()

        for n in range(0, units, step):
            cols = slice(n, n + step)
            u_tile[...] = dot(x[at, :], up[:, cols])
            d_tile[...] = product_rt(dy[at, :], down[cols, :])

            def gelu(here, i):
                there = pl.ds(pl.multiple_of(r * rows + i * 32, 32), 32)
                u = u_tile[here, :]
                normal = 0.5 * (1.0 + lax.erf(u * (2.0**-0.5)))
                slope = normal + u * (jnp.exp(-0.5 * u * u) * ((2.0 * math.pi) ** -0.5))
                act[there, cols] = (u * normal).astype(bf16)
                du[there, cols] = (d_tile[here, :] * slope).astype(bf16)

            row_loop(rows, 32, gelu)
        for n in range(0, width, step):
            part_x[at, n : n + step] = product_rt(du[at, :], up[n : n + step, :]).astype(bf16)

        @pl.when(turn == 1)
        def _():
            back_near.start()

        @pl.when(turn == 3)
        def _():
            back_far.start()

        return 0

    lax.fori_loop(0, 4, one, 0)
    back_far.wait_recv()
    add_rows(part_x.at[slot[1]], got_x.at[1])
    back_over.start()

    def y_terms(r, _):
        at = block(rows, r)
        for n in range(0, width, step):
            part_y[at, n : n + step] = dot(act[at, :], down[:, n : n + step]).astype(bf16)
        return 0

    lax.fori_loop(0, 4, y_terms, 0)
    y_back.start()

    chips, _, high, _ = g_all.shape
    few = units // (2 * chips)
    tall = width // (2 * chips)

    def up_terms(m, _):
        cols = pl.ds(pl.multiple_of(m * 256, 256), 256)
        for n in range(0, units, step):
            value = product_t(x[:, cols], du[:, n : n + step]).astype(bf16)
            for part in range(256 // tall):
                to = m * (256 // tall) + part
                g_all[to // 2, lax.rem(to, 2), 0:tall, n : n + step] = value[
                    part * tall : (part + 1) * tall
                ]
        return 0

    lax.fori_loop(0, width // 256, up_terms, 0)

    def down_terms(m, _):
        cols = pl.ds(pl.multiple_of(m * 256, 256), 256)
        for n in range(0, width, step):
            value = product_t(act[:, cols], dy[:, n : n + step]).astype(bf16)
            first = tall + n // units * few
            for part in range(256 // few):
                to = m * (256 // few) + part
                g_all[to // 2, lax.rem(to, 2), first : first + few, n % units : n % units + step] = (
                    value[part * few : (part + 1) * few]
                )
        return 0

    lax.fori_loop(0, units // 256, down_terms, 0)
    saves = [pltpu.make_async_copy(g_all, g_all_out, save.at[0])]
    saves[0].start()
    y_back.wait_recv()

    def y_sum(here, i):
        there = pl.ds(pl.multiple_of(rows + i * 32, 32), 32)
        y_keep[here, :] = (
            hidden[here, :] + part_y[here, :].astype(f32) + got_y[here, :].astype(f32)
        )
        y_send[here, :] = (part_y[there, :].astype(f32) + got_y[there, :].astype(f32)).astype(bf16)

    row_loop(rows, 32, y_sum)
    back_near.wait_recv()
    back_over.wait_recv()
    gain_part[...] = jnp.zeros_like(gain_part)

    def finish(here, i):
        unit, inverse = centred(hidden[here, :])
        grad = (
            part_x[here, :].astype(f32) + got_x[0, here, :].astype(f32)
        ) + got_x[2, here, :].astype(f32)
        gain_part[...] += jnp.sum(grad * unit, axis=0, keepdims=True)
        grad_hidden[here, :] = cot[here, :].astype(f32) + norm_rows_back(
            grad * gain[...], unit, inverse
        )

    row_loop(rows, 32, finish)
    for copy in (near, over, far, back_near, back_far, back_over, y_back):
        copy.wait_send()
    for copy in saves:
        copy.wait()


def feed(hidden, gain, cot, cot_rows, w_up, w_down, far_up, far_down):
    f32, bf16 = jnp.float32, jnp.bfloat16
    rows, width = hidden.shape
    units = w_up.shape[1]
    count = lax.axis_size("seq")
    gathered = (count // 2, 2, width // count + width // count, units)
    any_ = pl.BlockSpec(memory_space=pl.ANY)
    vmem = pl.BlockSpec(memory_space=pltpu.VMEM)
    dma = pltpu.SemaphoreType.DMA
    return pl.pallas_call(
        feed_kernel,
        out_shape=[
            jax.ShapeDtypeStruct((rows, width), f32),
            jax.ShapeDtypeStruct((rows, width), bf16),
            jax.ShapeDtypeStruct((rows, width), f32),
            jax.ShapeDtypeStruct((1, width), f32),
            jax.ShapeDtypeStruct(gathered, bf16),
        ],
        in_specs=[vmem, vmem, vmem] + [any_] * 5,
        out_specs=[vmem] * 4 + [any_],
        scratch_shapes=[
            pltpu.VMEM((4 * rows, width), bf16),
            pltpu.VMEM((4 * rows, width), bf16),
            pltpu.VMEM((4 * rows, units), bf16),
            pltpu.VMEM((4 * rows, units), bf16),
            pltpu.VMEM((4 * rows, width), bf16),
            pltpu.VMEM((4 * rows, width), bf16),
            pltpu.VMEM((3, rows, width), bf16),
            pltpu.VMEM((2 * rows, width), bf16),
            pltpu.VMEM((rows, 512), f32),
            pltpu.VMEM((rows, 512), f32),
            pltpu.VMEM(gathered, bf16),
            pltpu.VMEM(w_up.shape, bf16),
            pltpu.VMEM(w_down.shape, bf16),
            dma((6,)),
            dma((1,)),
            dma((7,)),
            dma((7,)),
        ],
        compiler_params=pltpu.CompilerParams(
            collective_id=1, has_side_effects=True, vmem_limit_bytes=LIMIT
        ),
        cost_estimate=pl.CostEstimate(
            flops=75 * 10**9, bytes_accessed=30 * 10**6, transcendentals=2 * 10**6
        ),
        name="feed",
    )(hidden, gain, cot, cot_rows, w_up, w_down, far_up, far_down)


def retract_kernel(
    grad_hidden,
    y_send,
    w_out,
    q_in,
    k_in,
    v_in,
    gp_in,
    gn_in,
    gated_in,
    inv_in,
    p_in,
    r_in,
    cosine,
    sine,
    mask,
    q_scale,
    k_scale,
    decay,
    d_out,
    g_out,
    y_got,
    dx,
    q,
    k,
    v,
    gp,
    gn,
    gated,
    inv,
    weights,
    entering,
    wo,
    dall,
    do,
    tile,
    grown,
    dk,
    dv,
    state,
    state_in,
    state_to,
    g_wo,
    load,
    save,
    g_send,
    g_recv,
    c_send,
    c_recv,
    y_sems,
):
    f32, bf16 = jnp.float32, jnp.bfloat16
    depth, rows, width = dx.shape
    heads = mask.shape[0]
    hk, hv = q.shape[1], v.shape[1]
    s, z = lax.axis_index("seq"), lax.axis_index("mp")
    place = lax.rem(s, SEQ_DEVS)
    pair = z + 1 - 2 * lax.rem(z, 2)
    loads = [
        pltpu.make_async_copy(a, b, load.at[i])
        for i, (a, b) in enumerate(
            [
                (w_out, wo),
                (q_in, q),
                (k_in, k),
                (v_in, v),
                (gp_in, gp),
                (gn_in, gn),
                (gated_in, gated),
                (inv_in, inv),
                (p_in, weights),
                (r_in, entering),
            ]
        )
    ]
    for copy in loads:
        copy.start()

    def low(here, i):
        dx[z, here, :] = grad_hidden[here, :].astype(bf16)

    row_loop(rows, 32, low)
    greet(
        [
            (z > 0, s, z - 1),
            (z < depth - 1, s, z + 1),
            (place > 0, s - 1, z),
            (place < SEQ_DEVS - 1, s + 1, z),
        ]
    )

    @pl.when(place == SEQ_DEVS - 1)
    def _():
        state_in[...] = jnp.zeros_like(state_in)

    def turn_back(value, at, start):
        c, sn = cosine[at, :], sine[at, :]
        half = DK // 2
        a, b = value[:, :half], value[:, half:]
        dall[at, start : start + half] = (a * c + b * sn).astype(bf16)
        dall[at, start + half : start + DK] = (b * c - a * sn).astype(bf16)

    def use(j):
        at = block(rows, j)

        @pl.when(j == z)
        def _():
            for copy in loads:
                copy.wait()

        for h in range(heads):
            wide = slice(h * DV, (h + 1) * DV)
            tile[...] = product_rt(dx[j], wo[wide, :])

            def gate_back(here, i):
                there = pl.ds(pl.multiple_of(j * rows + i * 32, 32), 32)
                grad = tile[here, :]
                gate = gp[there, wide]
                unit = gn[there, wide]
                open_ = 1.0 / (1.0 + jnp.exp(-gate))
                slope = open_ * (1.0 + gate * (1.0 - open_))
                first = 2 * hk + hv + h * DV
                dall[there, first : first + DV] = (grad * unit * slope).astype(bf16)
                inverse = inv[h, there, :][:, :1]
                do[there, wide] = norm_rows_back(grad * gate * open_, unit, inverse).astype(bf16)

            row_loop(rows, 32, gate_back)
        for h in range(heads):
            cols = slice(h * DK, (h + 1) * DK)
            wide = slice(h * DV, (h + 1) * DV)
            qb, kb, vb, db = q[at, cols], k[at, cols], v[at, wide], do[at, wide]
            ds = (product_rt(db, vb) * mask[h]).astype(bf16)
            dv[at, wide] = product_t(weights[h, j], db)
            dk[at, cols] = product_t(ds, qb)
            turn_back(dot(ds, kb) + q_scale[h] * product_rt(db, entering[h, j]), at, h * DK)
            qd = (qb.astype(f32) * q_scale[h]).astype(bf16)
            grown[h, j] = product_t(qd, db)

    line_gather(dx, g_send, g_recv, s, z, depth, use)
    swap = remote(y_send, y_got, y_sems.at[0], y_sems.at[1], s, pair)
    swap.start()
    for h in range(heads):
        state[h] = grown[h, depth - 1]
        for b in reversed(range(depth - 1)):
            state[h] = decay[h, 0] * state[h] + grown[h, b]

    def out_terms(m, _):
        cols = pl.ds(pl.multiple_of(m * 256, 256), 256)
        for n in range(0, width, 512):
            right = dx[:, :, n : n + 512].reshape(depth * rows, 512)
            g_wo[cols, n : n + 512] = product_t(gated[:, cols], right).astype(bf16)
        return 0

    def out_grad():
        lax.fori_loop(0, hv // 256, out_terms, 0)

    @pl.when(place <= 1)
    def _():
        out_grad()

    @pl.when(place < SEQ_DEVS - 1)
    def _():
        remote(state_to, state_in, c_send, c_recv, s + 1, z).wait_recv()

    chain = remote(state_to, state_in, c_send, c_recv, s - 1, z)

    @pl.when(place > 0)
    def _():
        for h in range(heads):
            state_to[h] = (decay[h, 1] * state_in[h].astype(f32) + state[h]).astype(bf16)
        chain.start()

    for h in range(heads):
        cols = slice(h * DK, (h + 1) * DK)
        wide = slice(h * DV, (h + 1) * DV)
        state[h] = state_in[h].astype(f32)

        def cross(turn, _):
            b = depth - 1 - turn
            at = block(rows, b)
            leaving = state[h].astype(bf16)
            state[h] = grown[h, b] + decay[h, 0] * state[h]
            kb = k[at, cols]
            vd = (v[at, wide].astype(f32) * k_scale[h]).astype(bf16)
            turn_back(dk[at, cols] + product_rt(vd, leaving), at, hk + h * DK)
            dall[at, 2 * hk + h * DV : 2 * hk + (h + 1) * DV] = (
                dv[at, wide] + k_scale[h] * dot(kb, leaving)
            ).astype(bf16)
            return 0

        lax.fori_loop(0, depth, cross, 0)
    saves = [
        pltpu.make_async_copy(dall, d_out, save.at[0]),
        pltpu.make_async_copy(g_wo, g_out, save.at[1]),
    ]
    saves[0].start()

    @pl.when(place > 1)
    def _():
        out_grad()

    saves[1].start()
    line_gather_end(dx, g_send, g_recv, s, z, depth)

    @pl.when(place > 0)
    def _():
        chain.wait_send()

    swap.wait()
    for copy in saves:
        copy.wait()


def retract(
    grad_hidden, y_send, w_out, q, k, v, gp, gn, gated, inv, p, r, cosine, sine, mask, q_scale, k_scale, decay
):
    f32, bf16 = jnp.float32, jnp.bfloat16
    depth = lax.axis_size("mp")
    rows, width = grad_hidden.shape
    span = depth * rows
    heads = mask.shape[0]
    hk, hv = q.shape[1], v.shape[1]
    any_ = pl.BlockSpec(memory_space=pl.ANY)
    vmem = pl.BlockSpec(memory_space=pltpu.VMEM)
    dma = pltpu.SemaphoreType.DMA
    return pl.pallas_call(
        retract_kernel,
        out_shape=[
            jax.ShapeDtypeStruct((span, 2 * hk + 2 * hv), bf16),
            jax.ShapeDtypeStruct((hv, width), bf16),
            jax.ShapeDtypeStruct((rows, width), bf16),
        ],
        in_specs=[vmem] + [any_] * 11 + [vmem] * 6,
        out_specs=[any_] * 3,
        scratch_shapes=[
            pltpu.VMEM((depth, rows, width), bf16),
            pltpu.VMEM((span, hk), bf16),
            pltpu.VMEM((span, hk), bf16),
            pltpu.VMEM((span, hv), bf16),
            pltpu.VMEM((span, hv), f32),
            pltpu.VMEM((span, hv), f32),
            pltpu.VMEM((span, hv), bf16),
            pltpu.VMEM((heads, span, 128), f32),
            pltpu.VMEM((heads, depth, rows, rows), bf16),
            pltpu.VMEM((heads, depth, DK, DV), bf16),
            pltpu.VMEM(w_out.shape, bf16),
            pltpu.VMEM((span, 2 * hk + 2 * hv), bf16),
            pltpu.VMEM((span, hv), bf16),
            pltpu.VMEM((rows, DV), f32),
            pltpu.VMEM((heads, depth, DK, DV), f32),
            pltpu.VMEM((span, hk), f32),
            pltpu.VMEM((span, hv), f32),
            pltpu.VMEM((heads, DK, DV), f32),
            pltpu.VMEM((heads, DK, DV), bf16),
            pltpu.VMEM((heads, DK, DV), bf16),
            pltpu.VMEM((hv, width), bf16),
            dma((10,)),
            dma((2,)),
            dma((2, depth)),
            dma((depth,)),
            dma,
            dma,
            dma((2,)),
        ],
        compiler_params=pltpu.CompilerParams(
            collective_id=2, has_side_effects=True, vmem_limit_bytes=LIMIT
        ),
        cost_estimate=pl.CostEstimate(
            flops=120 * 10**9, bytes_accessed=40 * 10**6, transcendentals=2 * 10**6
        ),
        name="retract",
    )(grad_hidden, y_send, w_out, q, k, v, gp, gn, gated, inv, p, r, cosine, sine, mask, q_scale, k_scale, decay)


def flip(index, bit):
    return index + bit - 2 * bit * lax.rem(index // bit, 2)


def pair_kernel(
    x, d, wo_parts, far, out, far_got, stage, got, wo_mine, wo_got, result, save, send, recv, w_sems, f_sems
):
    f32, bf16 = jnp.float32, jnp.bfloat16
    _, chips, rows, _ = stage.shape
    few = wo_mine.shape[1]
    third = result.shape[2]
    s, z = lax.axis_index("seq"), lax.axis_index("mp")
    core = lax.rem(s, 2)
    twin = flip(s, 1)
    across = flip(z, 2)
    edge = (z == 0) | (z == lax.axis_size("mp") - 1)
    greet([(z >= 0, twin, z), (z >= 0, s, across), (z >= 0, twin, across)])
    crossed = remote(far.at[0], far_got, f_sems.at[0], f_sems.at[1], twin, across)
    straight = remote(far.at[1], far_got, f_sems.at[2], f_sems.at[3], s, across)

    @pl.when(edge & (core == 1))
    def _():
        crossed.start()
        straight.start()

    wo_load = pltpu.make_async_copy(wo_parts.at[:, core], wo_mine, w_sems.at[0])
    wo_load.start()
    wo_send = remote(wo_parts.at[:, 1 - core], wo_got, w_sems.at[1], w_sems.at[2], twin, z)
    wo_send.start()
    span = max(256, 2 * rows)
    each = span // (2 * rows)

    def give(i):
        return remote(stage.at[1 - core, i], got.at[i], send.at[i], recv.at[i], twin, z)

    def keep(i):
        return pltpu.make_async_copy(result.at[i], out.at[i], save.at[i])

    def take(i):
        give(i).wait_recv()
        for t in range(d.shape[1] // third):

            def add(here, r):
                there = pl.ds(pl.multiple_of(t * rows + r * 32, 32), 32)
                cols = slice(t * third, (t + 1) * third)
                result[i, there, :] = (
                    stage[core, i, here, cols].astype(f32) + got[i, here, cols].astype(f32)
                ).astype(bf16)

            row_loop(rows, 32, add)

    def one(g, _):
        for c in range(span // 256):
            chunk = g * (span // 256) + c
            cols = pl.ds(pl.multiple_of(chunk * 256, 256), 256)
            for n in range(0, d.shape[1], 512):
                value = product_t(x[:, cols], d[:, n : n + 512]).astype(bf16)
                for part in range(max(1, 256 // rows)):
                    to = (c if each == 1 and rows >= 256 else part) % 2
                    i = g * each + (0 if rows >= 256 else part // 2)
                    stage[to, i, :, n : n + 512] = value[part * rows : (part + 1) * rows]
        for e in range(each):
            give(g * each + e).start()

        @pl.when(g > 0)
        def _():
            for e in range(each):
                take((g - 1) * each + e)

        return 0

    groups = chips // each
    lax.fori_loop(0, groups, one, 0)
    wo_load.wait()
    wo_send.wait()
    base = rows * (d.shape[1] // third)

    def wo_add(i, _):
        for t in range(wo_mine.shape[2] // third):
            cols = slice(t * third, (t + 1) * third)
            result[i, base + t * few : base + (t + 1) * few, :] = (
                wo_mine[i, :, cols].astype(f32) + wo_got[i, :, cols].astype(f32)
            ).astype(bf16)
        return 0

    lax.fori_loop(0, chips, wo_add, 0)
    for e in range(each):
        take((groups - 1) * each + e)

    def begin(i, _):
        keep(i).start()
        return 0

    def end(i, _):
        keep(i).wait()
        give(i).wait_send()
        return 0

    lax.fori_loop(0, chips, begin, 0)
    lax.fori_loop(0, chips, end, 0)

    @pl.when(edge & (core == 1))
    def _():
        crossed.wait_send()
        straight.wait_send()

    @pl.when(jnp.logical_not(edge) & (core == 0))
    def _():
        crossed.wait_recv()

    @pl.when(jnp.logical_not(edge) & (core == 1))
    def _():
        straight.wait_recv()


def pair_sum(x, d, g_out, far):
    bf16 = jnp.bfloat16
    count = lax.axis_size("seq")
    chips = count // 2
    rows, few = x.shape[1] // count, g_out.shape[0] // count
    wide, third = d.shape[1], d.shape[1] // 3
    high = 3 * rows + few * g_out.shape[1] // third
    any_ = pl.BlockSpec(memory_space=pl.ANY)
    vmem = pl.BlockSpec(memory_space=pltpu.VMEM)
    dma = pltpu.SemaphoreType.DMA
    return pl.pallas_call(
        pair_kernel,
        out_shape=[
            jax.ShapeDtypeStruct((chips, high, third), bf16),
            jax.ShapeDtypeStruct(far.shape[1:], bf16),
        ],
        in_specs=[vmem, vmem, any_, any_],
        out_specs=[any_, any_],
        scratch_shapes=[
            pltpu.VMEM((2, chips, rows, wide), bf16),
            pltpu.VMEM((chips, rows, wide), bf16),
            pltpu.VMEM((chips, few, g_out.shape[1]), bf16),
            pltpu.VMEM((chips, few, g_out.shape[1]), bf16),
            pltpu.VMEM((chips, high, third), bf16),
            dma((chips,)),
            dma((chips,)),
            dma((chips,)),
            dma((3,)),
            dma((4,)),
        ],
        compiler_params=pltpu.CompilerParams(
            collective_id=3, has_side_effects=True, vmem_limit_bytes=LIMIT
        ),
        cost_estimate=pl.CostEstimate(
            flops=25 * 10**9, bytes_accessed=30 * 10**6, transcendentals=0
        ),
        name="pair_sum",
    )(x, d, g_out.reshape(chips, 2, few, g_out.shape[1]), far)


def finish_kernel(
    d,
    x,
    tok,
    gain,
    gain_part,
    grad_hidden,
    w_query,
    w_key,
    w_value,
    w_gate,
    far,
    far_got,
    grad_tok,
    gains,
    g_up,
    g_down,
    sbuf,
    rbuf,
    total,
    wq,
    wk,
    wv,
    wg,
    mine,
    other,
    gain_all,
    gain_line,
    load,
    s_send,
    s_recv,
    f_sems,
    h_send,
    h_recv,
    l_send,
    l_recv,
):
    f32, bf16 = jnp.float32, jnp.bfloat16
    depth, rows, width = x.shape
    s, z = lax.axis_index("seq"), lax.axis_index("mp")
    core = lax.rem(s, 2)
    twin, across = flip(s, 1), flip(z, 2)
    count = lax.axis_size("seq")
    loads = [
        pltpu.make_async_copy(a, b, load.at[i])
        for i, (a, b) in enumerate([(w_query, wq), (w_key, wk), (w_value, wv), (w_gate, wg)])
    ]
    for copy in loads:
        copy.start()
    gains[...] = jnp.zeros_like(gains)
    gains[1:2, :] = gain_part[...]
    greet(
        [(z >= 0, twin, across)]
        + [(z != other, s, other) for other in range(depth)]
        + [(s != other, other, z) for other in range(count)]
    )
    near = remote(far.at[1], other, f_sems.at[0], f_sems.at[1], twin, z)
    crossed = remote(far.at[0], other, f_sems.at[0], f_sems.at[1], twin, across)
    straight = remote(far.at[1], mine, f_sems.at[2], f_sems.at[3], s, across)
    edge = (z == 0) | (z == depth - 1)
    inner = jnp.logical_not(edge)
    local = pltpu.make_async_copy(far.at[0], mine, f_sems.at[4])
    to_other = pltpu.make_async_copy(far_got, other, f_sems.at[5])
    to_mine = pltpu.make_async_copy(far_got, mine, f_sems.at[5])

    @pl.when(core == 0)
    def _():
        near.start()
        local.start()

    @pl.when(inner & (core == 0))
    def _():
        to_other.start()

    @pl.when(inner & (core == 1))
    def _():
        to_mine.start()
        crossed.start()
        straight.start()

    for copy in loads:
        copy.wait()
    step = 512
    starts, at_col = [], 0
    for w in (wq, wk, wv, wg):
        starts.append((w, at_col, at_col + w.shape[1]))
        at_col += w.shape[1]

    def term(j, n):
        at = block(rows, j)
        value = None
        for w, a, b in starts:
            one = product_rt(d[at, a:b], w[n : n + step, :])
            value = one if value is None else value + one
        gains[0:1, n : n + step] += jnp.sum(
            value * x[j, :, n : n + step].astype(f32), axis=0, keepdims=True
        )
        return value

    def partial(j):
        for n in range(0, width, step):
            sbuf[j, :, n : n + step] = term(j, n).astype(bf16)

    def plane(to):
        return remote(gain_all.at[s], gain_all.at[s], h_send.at[to], h_recv.at[s], to, z)

    def line(to):
        return remote(gain_line.at[z], gain_line.at[z], l_send.at[to], l_recv.at[z], s, to)

    def others(count, me, act):
        def one(i, _):
            @pl.when(i != me)
            def _():
                act(i)

            return 0

        lax.fori_loop(0, count, one, 0)

    def own():
        for n in range(0, width, step):
            total[:, n : n + step] = term(z, n)
        gains[0:1, :] = gains[0:1, :] / gain[...]
        gain_all[s] = gains[...]
        others(count, s, lambda to: plane(to).start())

    line_scatter(sbuf, rbuf, total, s_send, s_recv, s, z, depth, partial, own)

    def plane_came(i):
        remote(gain_all.at[i], gain_all.at[i], h_send.at[i], h_recv.at[i], twin, z).wait_recv()

    def line_came(i):
        remote(gain_line.at[i], gain_line.at[i], l_send.at[i], l_recv.at[i], s, across).wait_recv()

    others(count, s, plane_came)
    gains[...] = gain_all[0]
    for i in range(1, count):
        gains[...] += gain_all[i]
    gain_line[z] = gains[...]
    others(depth, z, lambda to: line(to).start())

    def last(here, i):
        unit, inverse = centred(tok[here, :].astype(f32))
        grad_tok[here, :] = (
            grad_hidden[here, :] + norm_rows_back(total[here, :] * gain[...], unit, inverse)
        ).astype(bf16)

    row_loop(rows, 32, last)
    others(depth, z, line_came)
    gains[...] = gain_line[0]
    for i in range(1, depth):
        gains[...] += gain_line[i]
    others(count, s, lambda to: plane(to).wait_send())
    others(depth, z, lambda to: line(to).wait_send())

    @pl.when(core == 0)
    def _():
        near.wait_send()
        local.wait()

    @pl.when(core == 1)
    def _():
        near.wait_recv()

    @pl.when(inner & (core == 0))
    def _():
        to_other.wait()

    @pl.when(edge & (core == 0))
    def _():
        crossed.wait_recv()

    @pl.when(inner & (core == 1))
    def _():
        to_mine.wait()
        crossed.wait_send()
        straight.wait_send()

    @pl.when(edge & (core == 1))
    def _():
        straight.wait_recv()

    high, few = g_up.shape[0], g_down.shape[0]
    third = g_up.shape[1]

    g_up[...] = mine[0:high, :].astype(f32) + other[0:high, :].astype(f32)
    for t in range(g_down.shape[1] // third):
        at = slice(high + t * few, high + (t + 1) * few)
        g_down[:, t * third : (t + 1) * third] = mine[at, :].astype(f32) + other[at, :].astype(f32)


def finish(d, x, tok, gain, gain_part, grad_hidden, w_query, w_key, w_value, w_gate, far, far_got):
    f32, bf16 = jnp.float32, jnp.bfloat16
    depth, rows, width = x.shape
    count = lax.axis_size("seq")
    units = far.shape[2]
    any_ = pl.BlockSpec(memory_space=pl.ANY)
    vmem = pl.BlockSpec(memory_space=pltpu.VMEM)
    dma = pltpu.SemaphoreType.DMA
    return pl.pallas_call(
        finish_kernel,
        out_shape=[
            jax.ShapeDtypeStruct((rows, width), bf16),
            jax.ShapeDtypeStruct((8, width), f32),
            jax.ShapeDtypeStruct((width // count, units), f32),
            jax.ShapeDtypeStruct((units // count, width), f32),
        ],
        in_specs=[vmem] * 6 + [any_] * 6,
        out_specs=[vmem] * 4,
        scratch_shapes=[
            pltpu.VMEM((depth, rows, width), bf16),
            pltpu.VMEM((depth + 1, rows, width), bf16),
            pltpu.VMEM((rows, width), f32),
            pltpu.VMEM(w_query.shape, bf16),
            pltpu.VMEM(w_key.shape, bf16),
            pltpu.VMEM(w_value.shape, bf16),
            pltpu.VMEM(w_gate.shape, bf16),
            pltpu.VMEM(far.shape[1:], bf16),
            pltpu.VMEM(far.shape[1:], bf16),
            pltpu.VMEM((count, 8, width), f32),
            pltpu.VMEM((depth, 8, width), f32),
            dma((4,)),
            dma((depth,)),
            dma((depth + 1,)),
            dma((6,)),
            dma((count,)),
            dma((count,)),
            dma((depth,)),
            dma((depth,)),
        ],
        compiler_params=pltpu.CompilerParams(
            collective_id=4, has_side_effects=True, vmem_limit_bytes=LIMIT
        ),
        cost_estimate=pl.CostEstimate(
            flops=110 * 10**9, bytes_accessed=30 * 10**6, transcendentals=0
        ),
        name="finish",
    )(d, x, tok, gain, gain_part, grad_hidden, w_query, w_key, w_value, w_gate, far, far_got)


def shards(
    tokens, gain_mix, w_query, w_key, w_value, w_gate, w_out, gain_ffn, w_up, w_down, cotangent
):
    bf16 = jnp.bfloat16
    f32 = jnp.float32
    span_rows = lax.axis_size("mp") * tokens.shape[0]
    local_heads = w_query.shape[1] // DK
    place = lax.axis_index("seq") % SEQ_DEVS
    positions = place * span_rows + jnp.arange(span_rows, dtype=jnp.int32)
    cosine, sine = angles(positions)
    heads = (lax.axis_index("mp") * local_heads).astype(f32) + jnp.arange(local_heads, dtype=f32)
    logs = jnp.log1p(-jnp.exp2(-5.0 - heads))
    steps = jnp.arange(STRETCH, dtype=f32)
    gaps = steps[:, None] - steps[None, :]
    mask = jnp.where(gaps >= 0, jnp.exp(logs[:, None, None] * jnp.maximum(gaps, 0.0)), 0.0)
    q_scale = jnp.exp(logs[:, None] * (steps + 1.0))[:, :, None]
    k_scale = jnp.exp(logs[:, None] * (STRETCH - 1.0 - steps))[:, :, None]
    span_decay = jnp.exp(logs * span_rows)
    decay = jnp.broadcast_to(
        jnp.stack([jnp.exp(logs * STRETCH), span_decay], axis=1)[:, :, None, None],
        (local_heads, 2, 1, DV),
    )
    trig = (cosine[:, 0], sine[:, 0], mask, q_scale, k_scale, decay)
    (
        x_rows,
        q_all,
        k_all,
        v_all,
        gate,
        unit,
        gated,
        inverse,
        weights,
        entering,
        hidden,
        cot_rows,
        far_up,
        far_down,
    ) = attend(
        tokens, gain_mix[None, :], cotangent, w_query, w_key, w_value, w_gate, w_out, w_up, w_down, *trig
    )
    y_keep, y_send, grad_hidden, gain_ffn_part, grad_ffn = feed(
        hidden, gain_ffn[None, :], cotangent, cot_rows, w_up, w_down, far_up, far_down
    )
    far = lax.psum_scatter(
        grad_ffn, "seq", scatter_dimension=0, tiled=False, axis_index_groups=same_core()
    )
    grad_in, grad_out_w, y_got = retract(
        grad_hidden, y_send, w_out, q_all, k_all, v_all, gate, unit, gated, inverse, weights, entering, *trig
    )
    output = (y_keep + y_got.astype(f32)).astype(bf16)
    pairs, far_got = pair_sum(x_rows.reshape(span_rows, -1), grad_in, grad_out_w, far)
    summed = lax.psum_scatter(
        pairs, "seq", scatter_dimension=0, tiled=False, axis_index_groups=same_core()
    )
    grad_in, pairs = lax.optimization_barrier((grad_in, pairs))
    grad_tokens, gains, final_up, final_down = finish(
        grad_in, x_rows, tokens, gain_mix[None, :], gain_ffn_part, grad_hidden, w_query, w_key, w_value, w_gate, far, far_got
    )
    summed, gains = lax.optimization_barrier((summed, gains))
    summed = summed.astype(f32)
    gain_mix_sum, gain_ffn_sum = gains[0], gains[1]
    count = lax.axis_size("seq")
    rows, few = w_query.shape[0] // count, w_out.shape[0] // count
    wide, tall = w_query.shape[1], w_value.shape[1]
    final_query = summed[:rows, :wide]
    final_key = summed[:rows, wide:]
    final_value = summed[rows : 2 * rows]
    final_gate = summed[2 * rows : 3 * rows]
    final_out = jnp.concatenate(
        [summed[3 * rows : 3 * rows + few], summed[3 * rows + few :]], axis=1
    )
    return (
        output,
        grad_tokens,
        gain_mix_sum,
        final_query,
        final_key,
        final_value,
        final_gate,
        final_out,
        gain_ffn_sum,
        final_up,
        final_down,
    )


def solution(mesh):
    return jax.shard_map(
        shards,
        mesh=mesh,
        in_specs=(
            P(("seq", "mp"), None),
            P(),
            P(None, "mp"),
            P(None, "mp"),
            P(None, "mp"),
            P(None, "mp"),
            P("mp", None),
            P(),
            P(None, "mp"),
            P("mp", None),
            P(("seq", "mp"), None),
        ),
        out_specs=(
            P(("seq", "mp"), None),
            P(("seq", "mp"), None),
            P(),
            P("seq", "mp"),
            P("seq", "mp"),
            P("seq", "mp"),
            P("seq", "mp"),
            P(("mp", "seq"), None),
            P(),
            P("seq", "mp"),
            P(("mp", "seq"), None),
        ),
        check_vma=False,
    )
```

time: 870 us -> 538 us (0.62)
  waiting for transfers between devices: 353 us -> 0.08 us
  Pallas kernels: 177 us -> 502 us
  matrix products: 139 us -> 0 us
  other arithmetic: 67.4 us -> 7.48 us
  blocking collectives: 40 us -> 0 us
  local copies, waits for them, and re-layouts: 47.5 us -> 10.9 us
  starting transfers between devices: 23 us -> 0.08 us
    pallas_call x0 -> x4, Pallas kernels: none -> 306 us  [the longest x1 109 us: retract(): pl.pallas_call(retract_kernel, out_shape=[jax.ShapeDtypeStruct((span, 2 *...]
    ppermute x14 -> x0, waiting for transfers between devices: 184 us -> none  [the longest x5 112 us: mp_swap(): return lax.ppermute(value, 'mp', [(i, i ^ bit) for i in range(count)])]
    dot_general x21 -> x0, matrix products: 139 us -> none  [the longest x7 60.9 us: product_rt(): lax.dot_general(left, right, (((1,), (1,)), ((), ())), preferred_element_...]
    all_gather x4 -> x0, waiting for transfers between devices: 97.6 us -> none  [the longest x1 72.6 us: shards(): lax.all_gather(grad_hidden.astype(bf16), 'mp', axis=0, tiled=True)]
    reduce_scatter x5 -> x0, waiting for transfers between devices: 71.4 us -> none  [the longest x1 42.5 us: shards(): lax.psum_scatter(part_mix.astype(jnp.bfloat16), 'mp', scatter_dimension=0...]
    psum x1 -> x0, blocking collectives: 40 us -> none  [shards(): lax.psum((gain_mix_part, gain_ffn_part), ('seq', 'mp'))]
    ppermute x14 -> x0, starting transfers between devices: 21.8 us -> none  [the longest x5 8.61 us: mp_swap(): return lax.ppermute(value, 'mp', [(i, i ^ bit) for i in range(count)])]
    convert_element_type x8 -> x1, other arithmetic: 22.4 us -> 1.25 us  [shards(): output = (y_keep + y_got.astype(f32)).astype(bf16)]
  transfers between devices with their start and end apart: 23 -> 2, of which waited for: 13 -> 0; matrix products, arithmetic and copies ran while one was open for 22% -> 0% of each run, Pallas kernels for 21% -> 39%
where the time goes in v3:
time: 538 us; the launch traced here: 534 us
  Pallas kernels  502 us (93%)
  between operations  14.2 us (3%)
  local copies, waits for them, and re-layouts  10.9 us (2%)
  other arithmetic  7.48 us (1%)
    pallas_call x1, Pallas kernels, attend(): pl.pallas_call(attend_kernel, out_shape=[jax.ShapeDtypeStruct(*one) for o...  195 us
    pallas_call x1, Pallas kernels, retract(): pl.pallas_call(retract_kernel, out_shape=[jax.ShapeDtypeStruct((span, 2 *...  109 us
    pallas_call x1, Pallas kernels, finish(): pl.pallas_call(finish_kernel, out_shape=[jax.ShapeDtypeStruct((rows, widt...  98.7 us
    pallas_call x1, Pallas kernels, feed(): pl.pallas_call(feed_kernel, out_shape=[jax.ShapeDtypeStruct((rows, width)...  72.2 us
    pallas_call x1, Pallas kernels, pair_sum(): pl.pallas_call(pair_kernel, out_shape=[jax.ShapeDtypeStruct((chips, high,...  26.5 us
  transfers between devices with their start and end apart: 2, of which 0 were waited for; matrix products, arithmetic and copies ran while one was open for 0% of the time, Pallas kernels for 39%

profile of v3, /device:TPU:0, one launch (start us, length us, event | category | flops | bytes accessed | tf_op | source)
XLA Modules:
  0.0 534.3 jit_solution(14343610103419480023)
XLA Ops:
  7.2 0.0 reduce-scatter.7.cloned.1.call-start
  7.3 0.1 fusion.1
  7.4 0.1 fusion
  7.5 0.1 pad_maximum_fusion.1
  7.6 0.9 exponential_select_fusion.mask
  8.5 0.9 multiply_exponential_fusion
  9.4 3.0 multiply_sine_fusion
  12.5 0.7 broadcast_in_dim.17.decay
  13.1 195.4 %attend.1 = (bf16[4,256,2048]{2,1,0:T(8,128)(2,1)}, bf16[1024,512]{1,0:T(8,128)(2,1)}, bf16[1024,512]{1,0:T(8,128)(2,1)}, bf16[1024,1024]{1,0:T(8,128)(2,1)}, f3...) custom-call(bf16[256,2048]{1,0:T(8,128)(2,1)} %tok.3, ...), custom_call_target="tpu_custom_call" | custom-call | flops 190000005120 | bytes 60000000 | tf_op jit(solution)/shard_map/attend/pallas_call | solution.py:596
  208.5 72.2 %feed.1 = (f32[256,2048]{1,0:T(8,128)}, bf16[256,2048]{1,0:T(8,128)(2,1)}, f32[256,2048]{1,0:T(8,128)}, f32[1,2048]{1,0:T(1,128)}, bf16[4,2,512,1024]{3,2,1,0:T(8,128)(2,1)}) custom-call(f32[256,2048]{1,0:T(8,128)} %get-tuple-element.42.hidden, f32[1,2048]{1,0:T(1,128)} %bitcast.16, bf16[256,2048]{1,0:T(8,128)(2,1)} %cot.3, ...), custom_call_target="tpu_custom_call" | custom-call | flops 74999996416 | bytes 30000000 | tf_op jit(solution)/shard_map/feed/pallas_call | solution.py:880
  280.7 0.0 reduce-scatter.7.cloned.1.call-update
  280.8 0.0 reduce-scatter.9.cloned.1.call-start
  280.8 108.7 %retract.1 = (bf16[1024,3072]{1,0:T(8,128)(2,1)}, bf16[1024,2048]{1,0:T(8,128)(2,1)}, bf16[256,2048]{1,0:T(8,128)(2,1)}) custom-call(f32[256,2048]{1,0:T(8,128)} %get-tuple-element.47.grad_hidden, bf16[256,2048]{1,0:T(8,128)(2,1)} %get-tuple-element.48.y_send, bf16[1024,2048]{1,0:T(8,128)(2,1)} %w_out.3, bf16[1024,512]{1,0:T(8,128)(2,1)} %get-tuple-element.49.q_in, ...), custom_call_target="tpu_custom_call" | custom-call | flops 120000004096 | bytes 40000000 | tf_op jit(solution)/shard_map/retract/pallas_call | solution.py:1145
  389.5 0.0 reduce-scatter.7.cloned.1.call-done
  389.5 26.5 %pair_sum.1 = (bf16[4,1024,1024]{2,1,0:T(8,128)(2,1)}, bf16[512,1024]{1,0:T(8,128)(2,1)}) custom-call(bf16[1024,2048]{1,0:T(8,128)(2,1)} %bitcast.19, bf16[1024,3072]{1,0:T(8,128)(2,1)} %get-tuple-element.64.d, bf16[4,2,128,2048]{3,2,1,0:T(8,128)(2,1)} %bitcast.20, bf16[2,512,1024]{2,1,0:T(8,128)(2,1)} %bitcast.14), custom_call_target="tpu_custom_call" | custom-call | flops 24999999488 | bytes 30000000 | tf_op jit(solution)/shard_map/pair_sum/pallas_call | solution.py:1319
  416.1 0.0 copy-start.1
  416.1 0.0 copy-start.5
  416.1 0.0 reduce-scatter.9.cloned.1.call-update
  416.1 1.5 copy-done.1
  417.7 0.3 copy-done.5
  417.9 1.3 add_convert_fusion
  419.2 98.7 %finish.1 = (bf16[256,2048]{1,0:T(8,128)(2,1)}, f32[8,2048]{1,0:T(8,128)}, f32[256,1024]{1,0:T(8,128)}, f32[128,2048]{1,0:T(8,128)}) custom-call(bf16[1024,3072]{1,0:T(8,128)(2,1)} %get-tuple-element.64.d, bf16[4,256,2048]{2,1,0:T(8,128)(2,1)} %get-tuple-element.60.x, bf16[256,2048]{1,0:T(8,128)(2,1)} %tok.3, f32[1,2048]{1,0:T(1,128)} %bitcast.18, ...), custom_call_target="tpu_custom_call" | custom-call | flops 109999996928 | bytes 30000000 | tf_op jit(solution)/shard_map/finish/pallas_call | solution.py:1548
  517.9 0.0 reduce-scatter.9.cloned.1.call-done
  518.0 0.0 copy-start
  518.0 2.3 fusion.4
  520.2 0.0 copy-done
  520.2 0.1 fusion.2
  520.4 1.6 fusion.3
  521.9 0.0 copy-start.4
  521.9 1.6 fusion.5
  523.5 0.0 copy-start.3
  523.5 1.0 pad_maximum_fusion
  524.5 0.0 copy-done.4
  524.5 0.0 copy-start.2
  524.5 1.0 copy.27
  525.5 0.0 copy-done.3
  525.5 1.0 copy.28
  526.5 0.0 copy-done.2
  526.5 1.0 copy.29
  (5 shorter events, 0.1 us)
Async XLA Ops:
  7.2 382.3 %reduce-scatter.7.cloned.1.call-start = ((), (), s32[]{:S(2)}) async-start(), calls=%async_computation.2 | async-start | bytes 10485760
  280.8 237.2 %reduce-scatter.9.cloned.1.call-start = ((), (), s32[]{:S(2)}) async-start(), calls=%async_computation.3 | async-start | bytes 10485760
  416.1 1.6 copy-start.1
  416.1 1.8 copy-start.5
  518.0 2.3 copy-start
  521.9 2.6 copy-start.4
  523.5 2.0 copy-start.3
  524.5 1.9 copy-start.2
Sparse Core Ops, SparseCore 0:
  280.9 94.4 reduce-scatter.6
  416.2 100.0 reduce-scatter.8

commit v4 on v3

--- a/solution.py
+++ b/solution.py
@@ -411,26 +411,22 @@
             weights[h, j] = (product_rt(q[at, cols], kb) * mask[h]).astype(bf16)
 
     line_gather(xg, g_send, g_recv, s, z, depth, use, after)
-    @pl.when(jnp.logical_not(edge))
-    def _():
-        for copy in moves:
-            copy.start()
+    def chain(h, to):
+        return remote(state_to.at[h], state_in.at[h], c_send.at[h], c_recv.at[h], to, z)
 
     for h in range(heads):
         state[h] = grown[h, 0]
         for b in range(1, depth):
             state[h] = decay[h, 0] * state[h] + grown[h, b]
-    chain = remote(state_to, state_in, c_send, c_recv, s + 1, z)
-
-    @pl.when(place > 0)
-    def _():
-        remote(state_to, state_in, c_send, c_recv, s - 1, z).wait_recv()
-
-    @pl.when(place < SEQ_DEVS - 1)
-    def _():
-        for h in range(heads):
+
+        @pl.when(place > 0)
+        def _():
+            chain(h, s - 1).wait_recv()
+
+        @pl.when(place < SEQ_DEVS - 1)
+        def _():
             state_to[h] = (decay[h, 1] * state_in[h].astype(f32) + state[h]).astype(bf16)
-        chain.start()
+            chain(h, s + 1).start()
 
     saves = [
         pltpu.make_async_copy(a, b, save.at[i])
@@ -466,10 +462,6 @@
 
         lax.fori_loop(0, count // 2, to_chip, 0)
 
-    @pl.when(jnp.logical_not(edge))
-    def _():
-        hand_out()
-
     for h in range(heads):
         cols = slice(h * DK, (h + 1) * DK)
         wide = slice(h * DV, (h + 1) * DV)
@@ -499,12 +491,19 @@
     for copy in saves[6:]:
         copy.start()
     line_gather_end(xg, g_send, g_recv, s, z, depth)
+
+    @pl.when(jnp.logical_not(edge))
+    def _():
+        hand_out()
+
     saves[0].wait()
     wide = 512
 
     def hook(turn):
         @pl.when((turn == 0) & jnp.logical_not(edge))
         def _():
+            for copy in moves:
+                copy.start()
             swap.start()
 
         @pl.when((turn == 0) & edge)
@@ -532,7 +531,8 @@
 
     @pl.when(place < SEQ_DEVS - 1)
     def _():
-        chain.wait_send()
+        for h in range(heads):
+            chain(h, s + 1).wait_send()
 
     def sent(chip, _):
         @pl.when(2 * chip + 1 != s)
@@ -627,8 +627,8 @@
             dma((depth,)),
             dma((depth,)),
             dma((depth + 1,)),
-            dma,
-            dma,
+            dma((heads,)),
+            dma((heads,)),
             dma((4,)),
             dma((3,)),
             dma((2,)),
@@ -952,6 +952,7 @@
     wo,
     dall,
     do,
+    do_low,
     tile,
     grown,
     dk,
@@ -1041,14 +1042,18 @@
                 first = 2 * hk + hv + h * DV
                 dall[there, first : first + DV] = (grad * unit * slope).astype(bf16)
                 inverse = inv[h, there, :][:, :1]
-                do[there, wide] = norm_rows_back(grad * gate * open_, unit, inverse).astype(bf16)
+                value = norm_rows_back(grad * gate * open_, unit, inverse)
+                high = value.astype(bf16)
+                do[there, wide] = high
+                do_low[here, wide] = (value - high.astype(f32)).astype(bf16)
 
             row_loop(rows, 32, gate_back)
         for h in range(heads):
             cols = slice(h * DK, (h + 1) * DK)
             wide = slice(h * DV, (h + 1) * DV)
             qb, kb, vb, db = q[at, cols], k[at, cols], v[at, wide], do[at, wide]
-            ds = (product_rt(db, vb) * mask[h]).astype(bf16)
+            raw = product_rt(db, vb) + product_rt(do_low[:, wide], vb)
+            ds = (raw * mask[h]).astype(bf16)
             dv[at, wide] = product_t(weights[h, j], db)
             dk[at, cols] = product_t(ds, qb)
             turn_back(dot(ds, kb) + q_scale[h] * product_rt(db, entering[h, j]), at, h * DK)
@@ -1058,11 +1063,6 @@
     line_gather(dx, g_send, g_recv, s, z, depth, use)
     swap = remote(y_send, y_got, y_sems.at[0], y_sems.at[1], s, pair)
     swap.start()
-    for h in range(heads):
-        state[h] = grown[h, depth - 1]
-        for b in reversed(range(depth - 1)):
-            state[h] = decay[h, 0] * state[h] + grown[h, b]
-
     def out_terms(m, _):
         cols = pl.ds(pl.multiple_of(m * 256, 256), 256)
         for n in range(0, width, 512):
@@ -1073,21 +1073,28 @@
     def out_grad():
         lax.fori_loop(0, hv // 256, out_terms, 0)
 
+    for h in range(heads):
+        state[h] = grown[h, depth - 1]
+        for b in reversed(range(depth - 1)):
+            state[h] = decay[h, 0] * state[h] + grown[h, b]
+
     @pl.when(place <= 1)
     def _():
         out_grad()
 
-    @pl.when(place < SEQ_DEVS - 1)
-    def _():
-        remote(state_to, state_in, c_send, c_recv, s + 1, z).wait_recv()
-
-    chain = remote(state_to, state_in, c_send, c_recv, s - 1, z)
-
-    @pl.when(place > 0)
-    def _():
-        for h in range(heads):
+    def chain(h, to):
+        return remote(state_to.at[h], state_in.at[h], c_send.at[h], c_recv.at[h], to, z)
+
+    for h in range(heads):
+
+        @pl.when(place < SEQ_DEVS - 1)
+        def _():
+            chain(h, s + 1).wait_recv()
+
+        @pl.when(place > 0)
+        def _():
             state_to[h] = (decay[h, 1] * state_in[h].astype(f32) + state[h]).astype(bf16)
-        chain.start()
+            chain(h, s - 1).start()
 
     for h in range(heads):
         cols = slice(h * DK, (h + 1) * DK)
@@ -1123,7 +1130,8 @@
 
     @pl.when(place > 0)
     def _():
-        chain.wait_send()
+        for h in range(heads):
+            chain(h, s - 1).wait_send()
 
     swap.wait()
     for copy in saves:
@@ -1165,6 +1173,7 @@
             pltpu.VMEM(w_out.shape, bf16),
             pltpu.VMEM((span, 2 * hk + 2 * hv), bf16),
             pltpu.VMEM((span, hv), bf16),
+            pltpu.VMEM((rows, hv), bf16),
             pltpu.VMEM((rows, DV), f32),
             pltpu.VMEM((heads, depth, DK, DV), f32),
             pltpu.VMEM((span, hk), f32),
@@ -1177,8 +1186,8 @@
             dma((2,)),
             dma((2, depth)),
             dma((depth,)),
-            dma,
-            dma,
+            dma((heads,)),
+            dma((heads,)),
             dma((2,)),
         ],
         compiler_params=pltpu.CompilerParams(
@@ -1246,12 +1255,12 @@
         for c in range(span // 256):
             chunk = g * (span // 256) + c
             cols = pl.ds(pl.multiple_of(chunk * 256, 256), 256)
-            for n in range(0, d.shape[1], 512):
-                value = product_t(x[:, cols], d[:, n : n + 512]).astype(bf16)
+            for n in range(0, d.shape[1], 1024):
+                value = product_t(x[:, cols], d[:, n : n + 1024]).astype(bf16)
                 for part in range(max(1, 256 // rows)):
                     to = (c if each == 1 and rows >= 256 else part) % 2
                     i = g * each + (0 if rows >= 256 else part // 2)
-                    stage[to, i, :, n : n + 512] = value[part * rows : (part + 1) * rows]
+                    stage[to, i, :, n : n + 1024] = value[part * rows : (part + 1) * rows]
         for e in range(each):
             give(g * each + e).start()
 
@@ -1347,12 +1356,12 @@
 
 
 def finish_kernel(
-    d,
-    x,
-    tok,
+    d_in,
+    x_in,
+    tok_in,
     gain,
     gain_part,
-    grad_hidden,
+    grad_hidden_in,
     w_query,
     w_key,
     w_value,
@@ -1363,6 +1372,10 @@
     gains,
     g_up,
     g_down,
+    d,
+    x,
+    tok,
+    grad_hidden,
     sbuf,
     rbuf,
     total,
@@ -1391,9 +1404,15 @@
     count = lax.axis_size("seq")
     loads = [
         pltpu.make_async_copy(a, b, load.at[i])
-        for i, (a, b) in enumerate([(w_query, wq), (w_key, wk), (w_value, wv), (w_gate, wg)])
+        for i, (a, b) in enumerate(
+            [(d_in, d), (w_query, wq), (w_key, wk), (w_value, wv), (w_gate, wg), (x_in, x)]
+        )
     ]
-    for copy in loads:
+    late = [
+        pltpu.make_async_copy(a, b, load.at[6 + i])
+        for i, (a, b) in enumerate([(tok_in, tok), (grad_hidden_in, grad_hidden)])
+    ]
+    for copy in loads + late:
         copy.start()
     gains[...] = jnp.zeros_like(gains)
     gains[1:2, :] = gain_part[...]
@@ -1487,6 +1506,9 @@
     gain_line[z] = gains[...]
     others(depth, z, lambda to: line(to).start())
 
+    for copy in late:
+        copy.wait()
+
     def last(here, i):
         unit, inverse = centred(tok[here, :].astype(f32))
         grad_tok[here, :] = (
@@ -1553,9 +1575,13 @@
             jax.ShapeDtypeStruct((width // count, units), f32),
             jax.ShapeDtypeStruct((units // count, width), f32),
         ],
-        in_specs=[vmem] * 6 + [any_] * 6,
+        in_specs=[any_] * 3 + [vmem] * 2 + [any_] * 7,
         out_specs=[vmem] * 4,
         scratch_shapes=[
+            pltpu.VMEM(d.shape, bf16),
+            pltpu.VMEM(x.shape, bf16),
+            pltpu.VMEM((rows, width), bf16),
+            pltpu.VMEM((rows, width), f32),
             pltpu.VMEM((depth, rows, width), bf16),
             pltpu.VMEM((depth + 1, rows, width), bf16),
             pltpu.VMEM((rows, width), f32),
@@ -1567,7 +1593,7 @@
             pltpu.VMEM(far.shape[1:], bf16),
             pltpu.VMEM((count, 8, width), f32),
             pltpu.VMEM((depth, 8, width), f32),
-            dma((4,)),
+            dma((8,)),
             dma((depth,)),
             dma((depth + 1,)),
             dma((6,)),
@@ -1584,6 +1610,37 @@
         ),
         name="finish",
     )(d, x, tok, gain, gain_part, grad_hidden, w_query, w_key, w_value, w_gate, far, far_got)
+
+
+def unpack_kernel(summed, tok, up, down, query, key, value, gate, out, tok_out, up_out, down_out):
+    f32 = jnp.float32
+    rows, wide = query.shape
+    few, tall = out.shape[0], value.shape[1]
+    query[...] = summed[0:rows, 0:wide].astype(f32)
+    key[...] = summed[0:rows, wide : 2 * wide].astype(f32)
+    value[...] = summed[rows : 2 * rows, :].astype(f32)
+    gate[...] = summed[2 * rows : 3 * rows, :].astype(f32)
+    for t in range(out.shape[1] // tall):
+        at = slice(3 * rows + t * few, 3 * rows + (t + 1) * few)
+        out[:, t * tall : (t + 1) * tall] = summed[at, :].astype(f32)
+    tok_out[...] = tok[...]
+    up_out[...] = up[...]
+    down_out[...] = down[...]
+
+
+def unpack(summed, tok, up, down, wide):
+    f32 = jnp.float32
+    count = lax.axis_size("seq")
+    width, tall = tok.shape[1], summed.shape[1]
+    rows, few = width // count, tall // count
+    shapes = [(rows, wide)] * 2 + [(rows, tall)] * 2 + [(few, width)]
+    return pl.pallas_call(
+        unpack_kernel,
+        out_shape=[jax.ShapeDtypeStruct(one, f32) for one in shapes]
+        + [jax.ShapeDtypeStruct(a.shape, a.dtype) for a in (tok, up, down)],
+        compiler_params=pltpu.CompilerParams(vmem_limit_bytes=LIMIT),
+        name="unpack",
+    )(summed, tok, up, down)
 
 
 def shards(
@@ -1646,18 +1703,17 @@
         grad_in, x_rows, tokens, gain_mix[None, :], gain_ffn_part, grad_hidden, w_query, w_key, w_value, w_gate, far, far_got
     )
     summed, gains = lax.optimization_barrier((summed, gains))
-    summed = summed.astype(f32)
     gain_mix_sum, gain_ffn_sum = gains[0], gains[1]
-    count = lax.axis_size("seq")
-    rows, few = w_query.shape[0] // count, w_out.shape[0] // count
-    wide, tall = w_query.shape[1], w_value.shape[1]
-    final_query = summed[:rows, :wide]
-    final_key = summed[:rows, wide:]
-    final_value = summed[rows : 2 * rows]
-    final_gate = summed[2 * rows : 3 * rows]
-    final_out = jnp.concatenate(
-        [summed[3 * rows : 3 * rows + few], summed[3 * rows + few :]], axis=1
-    )
+    (
+        final_query,
+        final_key,
+        final_value,
+        final_gate,
+        final_out,
+        grad_tokens,
+        final_up,
+        final_down,
+    ) = unpack(summed, grad_tokens, final_up, final_down, w_query.shape[1])
     return (
         output,
         grad_tokens,

time: 538 us -> 509 us (0.946)
  Pallas kernels: 502 us -> 481 us
  local copies, waits for them, and re-layouts: 10.9 us -> 4.01 us
    pallas_call x1, Pallas kernels: 195 us -> 174 us  [attend(): pl.pallas_call(attend_kernel, out_shape=[jax.ShapeDtypeStruct(*one) for o...]
    pallas_call x0 -> x1, Pallas kernels: none -> 5.51 us  [unpack(): pl.pallas_call(unpack_kernel, out_shape=[jax.ShapeDtypeStruct(one, f32) f...]
  transfers between devices with their start and end apart: 2 -> 2, of which waited for: 0 -> 1; matrix products, arithmetic and copies ran while one was open for 0% -> 0% of each run, Pallas kernels for 39% -> 40%
where the time goes in v4:
time: 509 us; the launch traced here: 506 us
  Pallas kernels  481 us (94%)
  between operations  14.2 us (3%)
  other arithmetic  6.44 us (1%)
    pallas_call x1, Pallas kernels, attend(): pl.pallas_call(attend_kernel, out_shape=[jax.ShapeDtypeStruct(*one) for o...  174 us
    pallas_call x1, Pallas kernels, retract(): pl.pallas_call(retract_kernel, out_shape=[jax.ShapeDtypeStruct((span, 2 *...  107 us
    pallas_call x1, Pallas kernels, finish(): pl.pallas_call(finish_kernel, out_shape=[jax.ShapeDtypeStruct((rows, widt...  94.9 us
    pallas_call x1, Pallas kernels, feed(): pl.pallas_call(feed_kernel, out_shape=[jax.ShapeDtypeStruct((rows, width)...  72.8 us
    pallas_call x1, Pallas kernels, pair_sum(): pl.pallas_call(pair_kernel, out_shape=[jax.ShapeDtypeStruct((chips, high,...  26.4 us
  transfers between devices with their start and end apart: 2, of which 1 were waited for; matrix products, arithmetic and copies ran while one was open for 0% of the time, Pallas kernels for 40%

profile of v4, /device:TPU:0, one launch (start us, length us, event | category | flops | bytes accessed | tf_op | source)
XLA Modules:
  0.0 506.1 jit_solution(646588381263301310)
XLA Ops:
  7.2 0.0 reduce-scatter.7.cloned.1.call-start
  7.3 0.1 fusion.1
  7.4 0.1 fusion
  7.5 0.1 pad_maximum_fusion
  7.6 0.9 exponential_select_fusion.mask
  8.5 0.9 multiply_exponential_fusion
  9.4 3.0 multiply_sine_fusion
  12.5 0.7 broadcast_in_dim.17.decay
  13.1 173.8 %attend.1 = (bf16[4,256,2048]{2,1,0:T(8,128)(2,1)}, bf16[1024,512]{1,0:T(8,128)(2,1)}, bf16[1024,512]{1,0:T(8,128)(2,1)}, bf16[1024,1024]{1,0:T(8,128)(2,1)}, f3...) custom-call(bf16[256,2048]{1,0:T(8,128)(2,1)} %tok_in.1, ...), custom_call_target="tpu_custom_call" | custom-call | flops 190000005120 | bytes 60000000 | tf_op jit(solution)/shard_map/attend/pallas_call | solution.py:596
  187.0 72.8 %feed.1 = (f32[256,2048]{1,0:T(8,128)}, bf16[256,2048]{1,0:T(8,128)(2,1)}, f32[256,2048]{1,0:T(8,128)}, f32[1,2048]{1,0:T(1,128)}, bf16[4,2,512,1024]{3,2,1,0:T(8,128)(2,1)}) custom-call(f32[256,2048]{1,0:T(8,128)} %get-tuple-element.50.hidden, f32[1,2048]{1,0:T(1,128)} %bitcast.14, bf16[256,2048]{1,0:T(8,128)(2,1)} %cot.3, ...), custom_call_target="tpu_custom_call" | custom-call | flops 74999996416 | bytes 30000000 | tf_op jit(solution)/shard_map/feed/pallas_call | solution.py:880
  259.8 0.0 reduce-scatter.7.cloned.1.call-update
  259.8 0.0 reduce-scatter.9.cloned.1.call-start
  259.8 107.0 %retract.1 = (bf16[1024,3072]{1,0:T(8,128)(2,1)}, bf16[1024,2048]{1,0:T(8,128)(2,1)}, bf16[256,2048]{1,0:T(8,128)(2,1)}) custom-call(f32[256,2048]{1,0:T(8,128)} %get-tuple-element.55.grad_hidden.grad_hidden_in, bf16[256,2048]{1,0:T(8,128)(2,1)} %get-tuple-element.56.y_send, bf16[1024,2048]{1,0:T(8,128)(2,1)} %w_out.3, ...), custom_call_target="tpu_custom_call" | custom-call | flops 120000004096 | bytes 40000000 | tf_op jit(solution)/shard_map/retract/pallas_call | solution.py:1153
  366.9 0.0 reduce-scatter.7.cloned.1.call-done
  366.9 26.4 %pair_sum.1 = (bf16[4,1024,1024]{2,1,0:T(8,128)(2,1)}, bf16[512,1024]{1,0:T(8,128)(2,1)}) custom-call(bf16[1024,2048]{1,0:T(8,128)(2,1)} %bitcast.17, bf16[1024,3072]{1,0:T(8,128)(2,1)} %get-tuple-element.72.d.d_in, bf16[4,2,128,2048]{3,2,1,0:T(8,128)(2,1)} %bitcast.18, bf16[2,512,1024]{2,1,0:T(8,128)(2,1)} %bitcast.12), custom_call_target="tpu_custom_call" | custom-call | flops 24999999488 | bytes 30000000 | tf_op jit(solution)/shard_map/pair_sum/pallas_call | solution.py:1328
  393.3 0.0 copy-start
  393.3 0.0 copy-start.1
  393.3 0.0 reduce-scatter.9.cloned.1.call-update
  393.4 1.5 copy-done
  394.9 0.3 copy-done.1
  395.2 1.3 add_convert_fusion
  396.4 94.9 %finish.1 = (bf16[256,2048]{1,0:T(8,128)(2,1)}, f32[8,2048]{1,0:T(8,128)}, f32[256,1024]{1,0:T(8,128)}, f32[128,2048]{1,0:T(8,128)}) custom-call(bf16[1024,3072]{1,0:T(8,128)(2,1)} %get-tuple-element.72.d.d_in, bf16[4,256,2048]{2,1,0:T(8,128)(2,1)} %get-tuple-element.67.x_in, bf16[256,2048]{1,0:T(8,128)(2,1)} %tok_in.1, f32[1,2048]{1,0:T(1,128)} %bitcast.16, ...), custom_call_target="tpu_custom_call" | custom-call | flops 109999996928 | bytes 30000000 | tf_op jit(solution)/shard_map/finish/pallas_call | solution.py:1570
  491.4 0.8 reduce-scatter.9.cloned.1.call-done
  492.2 1.5 fusion.2
  493.8 5.5 %unpack.1 = (f32[256,512]{1,0:T(8,128)}, f32[256,512]{1,0:T(8,128)}, f32[256,1024]{1,0:T(8,128)}, f32[256,1024]{1,0:T(8,128)}, f32[128,2048]{1,0:T(8,128)}, /*in...) custom-call(bf16[1024,1024]{1,0:T(8,128)(2,1)} %bitcast.9, ...), custom_call_target="tpu_custom_call" | custom-call | tf_op jit(solution)/shard_map/unpack/pallas_call | solution.py:1637
  (5 shorter events, 0.1 us)
Async XLA Ops:
  7.2 359.7 %reduce-scatter.7.cloned.1.call-start = ((), (), s32[]{:S(2)}) async-start(), calls=%async_computation.2 | async-start | bytes 10485760
  259.8 232.4 %reduce-scatter.9.cloned.1.call-start = ((), (), s32[]{:S(2)}) async-start(), calls=%async_computation.3 | async-start | bytes 10485760
  393.3 1.6 copy-start
  393.3 1.8 copy-start.1
Sparse Core Ops, SparseCore 0:
  259.9 93.0 reduce-scatter.6
  393.5 98.6 reduce-scatter.8

commit v5 on v4

--- a/solution.py
+++ b/solution.py
@@ -2,6 +2,7 @@
 
 import jax
 import jax.numpy as jnp
+import numpy as np
 from jax import lax
 from jax.experimental import pallas as pl
 from jax.experimental.pallas import tpu as pltpu
@@ -21,11 +22,24 @@
     return [list(range(core, count, 2)) for core in range(2)]
 
 
-def angles(positions):
+def decay_tables(span_rows, heads):
     half = DK // 2
-    freq = jnp.exp(-math.log(10000.0) * jnp.arange(half, dtype=jnp.float32) / (half - 1))
-    phase = positions.astype(jnp.float32)[:, None] * freq[None, :]
-    return (jnp.cos(phase)[:, None, :], jnp.sin(phase)[:, None, :])
+    f32 = np.float32
+    freq = np.exp(f32(-math.log(10000.0)) * np.arange(half, dtype=f32) / f32(half - 1)).astype(f32)
+    phase = np.arange(SEQ_DEVS * span_rows, dtype=f32)[:, None] * freq[None, :]
+    phase = phase.astype(np.float64)
+    logs = np.log1p(-np.exp2(-5.0 - np.arange(heads)))
+    steps = np.arange(STRETCH)
+    gaps = steps[:, None] - steps[None, :]
+    mask = np.where(gaps >= 0, np.exp(logs[:, None, None] * np.maximum(gaps, 0)), 0.0)
+    q_scale = np.exp(logs[:, None] * (steps + 1))[:, :, None]
+    k_scale = np.exp(logs[:, None] * (STRETCH - 1 - steps))[:, :, None]
+    decay = np.exp(logs[:, None] * np.array([STRETCH, span_rows]))[:, :, None, None]
+    decay = np.broadcast_to(decay, (heads, 2, 1, DV))
+    return tuple(
+        jnp.asarray(a.astype(f32))
+        for a in (np.cos(phase), np.sin(phase), mask, q_scale, k_scale, decay)
+    )
 
 
 def product_t(left, right):
@@ -252,12 +266,12 @@
     w_out,
     w_up,
     w_down,
-    cosine,
-    sine,
-    mask,
-    q_scale,
-    k_scale,
-    decay,
+    cosine_all,
+    sine_all,
+    mask_all,
+    q_scale_all,
+    k_scale_all,
+    decay_all,
     x_out,
     q_out,
     k_out,
@@ -272,6 +286,12 @@
     cot_rows,
     far_up,
     far_down,
+    cosine,
+    sine,
+    mask,
+    q_scale,
+    k_scale,
+    decay,
     xg,
     q,
     k,
@@ -317,10 +337,23 @@
     place = lax.rem(s, SEQ_DEVS)
     pair = z + 1 - 2 * lax.rem(z, 2)
     twin = s + 1 - 2 * lax.rem(s, 2)
+    def tables(place, z):
+        at = block(cosine.shape[0], place)
+        some = pl.ds(z * heads, heads)
+        return [
+            (cosine_all.at[at], cosine),
+            (sine_all.at[at], sine),
+            (mask_all.at[some], mask),
+            (q_scale_all.at[some], q_scale),
+            (k_scale_all.at[some], k_scale),
+            (decay_all.at[some], decay),
+        ]
+
     loads = [
         pltpu.make_async_copy(a, b, load.at[i])
         for i, (a, b) in enumerate(
             [(w_query, wq), (w_key, wk), (w_value, wv), (w_gate, wg), (w_out, wo)]
+            + tables(place, z)
         )
     ]
     for copy in loads:
@@ -390,25 +423,37 @@
             for copy in loads:
                 copy.wait()
 
-        c, sn = cosine[at, :], sine[at, :]
-        for h in range(heads):
-            cols = slice(h * DK, (h + 1) * DK)
-            for w, out in ((wq, q), (wk, k)):
-                p = dot(xg[j], w[:, cols])
-                a, b = p[:, : DK // 2], p[:, DK // 2 :]
-                out[at, h * DK : h * DK + DK // 2] = (a * c - b * sn).astype(bf16)
-                out[at, h * DK + DK // 2 : (h + 1) * DK] = (b * c + a * sn).astype(bf16)
-        for h in range(heads):
-            wide = slice(h * DV, (h + 1) * DV)
-            v[at, wide] = dot(xg[j], wv[:, wide]).astype(bf16)
-            gp[at, wide] = dot(xg[j], wg[:, wide])
+        rotated(j, wk, k)
         for h in range(heads):
             cols = slice(h * DK, (h + 1) * DK)
             wide = slice(h * DV, (h + 1) * DV)
-            kb, vb = k[at, cols], v[at, wide]
-            vd = (vb.astype(f32) * k_scale[h]).astype(bf16)
-            grown[h, j] = product_t(kb, vd)
-            weights[h, j] = (product_rt(q[at, cols], kb) * mask[h]).astype(bf16)
+            v[at, wide] = dot(xg[j], wv[:, wide]).astype(bf16)
+            vd = (v[at, wide].astype(f32) * k_scale[h]).astype(bf16)
+            grown[h, j] = product_t(k[at, cols], vd)
+
+        @pl.when(j != last)
+        def _():
+            rest(j)
+
+    last = jnp.where(z < depth // 2, depth - 1, 0)
+
+    def rotated(j, w, out):
+        at = block(rows, j)
+        c, sn = cosine[at, :], sine[at, :]
+        for h in range(heads):
+            p = dot(xg[j], w[:, h * DK : (h + 1) * DK])
+            a, b = p[:, : DK // 2], p[:, DK // 2 :]
+            out[at, h * DK : h * DK + DK // 2] = (a * c - b * sn).astype(bf16)
+            out[at, h * DK + DK // 2 : (h + 1) * DK] = (b * c + a * sn).astype(bf16)
+
+    def rest(j):
+        at = block(rows, j)
+        rotated(j, wq, q)
+        for h in range(heads):
+            cols = slice(h * DK, (h + 1) * DK)
+            wide = slice(h * DV, (h + 1) * DV)
+            gp[at, wide] = dot(xg[j], wg[:, wide])
+            weights[h, j] = (product_rt(q[at, cols], k[at, cols]) * mask[h]).astype(bf16)
 
     line_gather(xg, g_send, g_recv, s, z, depth, use, after)
     def chain(h, to):
@@ -419,14 +464,22 @@
         for b in range(1, depth):
             state[h] = decay[h, 0] * state[h] + grown[h, b]
 
-        @pl.when(place > 0)
-        def _():
+        @pl.when(place == 0)
+        def _():
+            state_to[h] = state[h].astype(bf16)
+            chain(h, s + 1).start()
+
+    rest(last)
+
+    @pl.when(place > 0)
+    def _():
+        for h in range(heads):
             chain(h, s - 1).wait_recv()
 
-        @pl.when(place < SEQ_DEVS - 1)
-        def _():
-            state_to[h] = (decay[h, 1] * state_in[h].astype(f32) + state[h]).astype(bf16)
-            chain(h, s + 1).start()
+            @pl.when(place < SEQ_DEVS - 1)
+            def _():
+                state_to[h] = (decay[h, 1] * state_in[h].astype(f32) + state[h]).astype(bf16)
+                chain(h, s + 1).start()
 
     saves = [
         pltpu.make_async_copy(a, b, save.at[i])
@@ -571,7 +624,7 @@
     depth = lax.axis_size("mp")
     rows, width = tok.shape
     span = depth * rows
-    heads = mask.shape[0]
+    heads = w_query.shape[1] // DK
     hk, hv = w_query.shape[1], w_value.shape[1]
     any_ = pl.BlockSpec(memory_space=pl.ANY)
     vmem = pl.BlockSpec(memory_space=pltpu.VMEM)
@@ -596,9 +649,15 @@
     return pl.pallas_call(
         attend_kernel,
         out_shape=[jax.ShapeDtypeStruct(*one) for one in shapes],
-        in_specs=[vmem, vmem, any_] + [any_] * 7 + [vmem] * 6,
+        in_specs=[vmem, vmem, any_] + [any_] * 13,
         out_specs=[any_] * len(shapes),
         scratch_shapes=[
+            pltpu.VMEM((span, DK // 2), f32),
+            pltpu.VMEM((span, DK // 2), f32),
+            pltpu.VMEM((heads, rows, rows), f32),
+            pltpu.VMEM((heads, rows, 1), f32),
+            pltpu.VMEM((heads, rows, 1), f32),
+            pltpu.VMEM((heads, 2, 1, DV), f32),
             pltpu.VMEM((depth, rows, width), bf16),
             pltpu.VMEM((span, hk), bf16),
             pltpu.VMEM((span, hk), bf16),
@@ -621,7 +680,7 @@
             pltpu.VMEM(w_value.shape, bf16),
             pltpu.VMEM(w_gate.shape, bf16),
             pltpu.VMEM(w_out.shape, bf16),
-            dma((5,)),
+            dma((11,)),
             dma((10,)),
             dma((2, depth)),
             dma((depth,)),
@@ -681,6 +740,7 @@
     part_y,
     part_x,
     got_x,
+    got_own,
     got_y,
     u_tile,
     d_tile,
@@ -695,6 +755,7 @@
     f32, bf16 = jnp.float32, jnp.bfloat16
     rows, width = hidden.shape
     units = up.shape[1]
+    half = rows // 2
     s, z = lax.axis_index("seq"), lax.axis_index("mp")
     pair = z + 1 - 2 * lax.rem(z, 2)
     twin = s + 1 - 2 * lax.rem(s, 2)
@@ -718,8 +779,17 @@
             copy.start()
 
     rest = [
-        pltpu.make_async_copy(cot_rows.at[r], dy.at[pl.ds(r * rows, rows)], load.at[2 + r])
-        for r in range(4)
+        pltpu.make_async_copy(cot_rows.at[a, pl.ds(at, n)], dy.at[pl.ds(to, n)], load.at[2 + i])
+        for i, (a, at, n, to) in enumerate(
+            [
+                (0, 0, rows, 0),
+                (2, 0, rows, rows),
+                (1, 0, half, 2 * rows),
+                (3, 0, half, 2 * rows + half),
+                (1, half, half, 3 * rows),
+                (3, half, half, 3 * rows + half),
+            ]
+        )
     ]
     loads = own_loads + rest
     for copy in rest:
@@ -731,38 +801,67 @@
 
     row_loop(rows, 32, norm)
     greet([(z >= 0, s, pair), (z >= 0, twin, z)])
-    slot = [pl.ds(r * rows, rows) for r in range(4)]
-    over = remote(x.at[slot[0]], x.at[slot[1]], send.at[0], recv.at[0], s, pair)
-    near = remote(x.at[slot[0]], x.at[slot[2]], send.at[1], recv.at[1], twin, z)
-    far = remote(x.at[slot[1]], x.at[slot[3]], send.at[2], recv.at[2], twin, z)
+    mine, theirs = pl.ds(0, rows), pl.ds(rows, rows)
+    parts = [pl.ds(0, half), pl.ds(half, half)]
+    pairs = [pl.ds(2 * rows, half), pl.ds(3 * rows, half)]
+    twins = [pl.ds(2 * rows + half, half), pl.ds(3 * rows + half, half)]
+    near = remote(x.at[mine], x.at[theirs], send.at[0], recv.at[0], twin, z)
+    over, far, back_far, back_over, y_far = [], [], [], [], []
+    for i in range(2):
+        k = 1 + 5 * i
+        over.append(remote(x.at[parts[i]], x.at[pairs[i]], send.at[k], recv.at[k], s, pair))
+        far.append(remote(x.at[pairs[i]], x.at[twins[i]], send.at[k + 1], recv.at[k + 1], twin, z))
+        back_far.append(
+            remote(part_x.at[twins[i]], got_x.at[i], send.at[k + 2], recv.at[k + 2], twin, z)
+        )
+        back_over.append(
+            remote(part_x.at[pairs[i]], got_x.at[2 + i], send.at[k + 3], recv.at[k + 3], s, pair)
+        )
+        y_far.append(
+            remote(
+                part_y.at[twins[i]], got_y.at[pl.ds(rows + i * half, half)], send.at[k + 4],
+                recv.at[k + 4], twin, z,
+            )
+        )
+    back_near = remote(part_x.at[theirs], got_own, send.at[11], recv.at[11], twin, z)
+    y_near = remote(part_y.at[theirs], got_y.at[mine], send.at[12], recv.at[12], twin, z)
+    over[0].start()
     near.start()
-    over.start()
-    back_near = remote(part_x.at[slot[2]], got_x.at[0], send.at[3], recv.at[3], twin, z)
-    back_far = remote(part_x.at[slot[3]], got_x.at[1], send.at[4], recv.at[4], twin, z)
-    back_over = remote(part_x.at[slot[1]], got_x.at[2], send.at[5], recv.at[5], s, pair)
-    y_back = remote(
-        part_y.at[pl.ds(2 * rows, 2 * rows)], got_y, send.at[6], recv.at[6], twin, z
-    )
+    over[1].start()
     for copy in loads:
         copy.wait()
     step = 512
 
-    def one(turn, _):
-        r = lax.rem(turn, 2) * 2 + turn // 2
+    def y_terms(r):
         at = block(rows, r)
-
-        @pl.when(turn == 1)
+        for n in range(0, width, step):
+            part_y[at, n : n + step] = dot(act[at, :], down[:, n : n + step]).astype(bf16)
+
+    def return_pair(i):
+        back_far[i].wait_recv()
+        add_rows(part_x.at[pairs[i]], got_x.at[i])
+        back_over[i].start()
+
+    def one(r, _):
+        at = block(rows, r)
+
+        @pl.when(r == 1)
         def _():
             near.wait_recv()
 
-        @pl.when(turn == 2)
-        def _():
-            over.wait_recv()
-            far.start()
-
-        @pl.when(turn == 3)
-        def _():
-            far.wait_recv()
+        @pl.when(r == 2)
+        def _():
+            over[0].wait_recv()
+            far[0].start()
+            far[0].wait_recv()
+
+        @pl.when(r == 3)
+        def _():
+            return_pair(0)
+            lax.fori_loop(0, 2, lambda i, c: (y_terms(i), c)[1], 0)
+            over[1].wait_recv()
+            far[1].start()
+            far[1].wait_recv()
 
         for n in range(0, units, step):
             cols = slice(n, n + step)
@@ -781,88 +880,92 @@
         for n in range(0, width, step):
             part_x[at, n : n + step] = product_rt(du[at, :], up[n : n + step, :]).astype(bf16)
 
-        @pl.when(turn == 1)
+        @pl.when(r == 1)
         def _():
             back_near.start()
 
-        @pl.when(turn == 3)
-        def _():
-            back_far.start()
+        @pl.when(r == 2)
+        def _():
+            back_far[0].start()
+
+        @pl.when(r == 3)
+        def _():
+            back_far[1].start()
 
         return 0
 
     lax.fori_loop(0, 4, one, 0)
-    back_far.wait_recv()
-    add_rows(part_x.at[slot[1]], got_x.at[1])
-    back_over.start()
-
-    def y_terms(r, _):
-        at = block(rows, r)
-        for n in range(0, width, step):
-            part_y[at, n : n + step] = dot(act[at, :], down[:, n : n + step]).astype(bf16)
-        return 0
-
-    lax.fori_loop(0, 4, y_terms, 0)
-    y_back.start()
-
+    return_pair(1)
+    lax.fori_loop(2, 4, lambda i, c: (y_terms(i), c)[1], 0)
+    y_near.start()
+    for copy in y_far:
+        copy.start()
     chips, _, high, _ = g_all.shape
     few = units // (2 * chips)
     tall = width // (2 * chips)
 
     def up_terms(m, _):
         cols = pl.ds(pl.multiple_of(m * 256, 256), 256)
-        for n in range(0, units, step):
-            value = product_t(x[:, cols], du[:, n : n + step]).astype(bf16)
-            for part in range(256 // tall):
-                to = m * (256 // tall) + part
-                g_all[to // 2, lax.rem(to, 2), 0:tall, n : n + step] = value[
-                    part * tall : (part + 1) * tall
-                ]
+        value = product_t(x[:, cols], du[...]).astype(bf16)
+        for part in range(256 // tall):
+            to = m * (256 // tall) + part
+            g_all[to // 2, lax.rem(to, 2), 0:tall, :] = value[part * tall : (part + 1) * tall]
         return 0
 
     lax.fori_loop(0, width // 256, up_terms, 0)
 
     def down_terms(m, _):
         cols = pl.ds(pl.multiple_of(m * 256, 256), 256)
-        for n in range(0, width, step):
-            value = product_t(act[:, cols], dy[:, n : n + step]).astype(bf16)
+        for n in range(0, width, units):
+            value = product_t(act[:, cols], dy[:, n : n + units]).astype(bf16)
             first = tall + n // units * few
             for part in range(256 // few):
                 to = m * (256 // few) + part
-                g_all[to // 2, lax.rem(to, 2), first : first + few, n % units : n % units + step] = (
-                    value[part * few : (part + 1) * few]
-                )
+                g_all[to // 2, lax.rem(to, 2), first : first + few, :] = value[
+                    part * few : (part + 1) * few
+                ]
         return 0
 
     lax.fori_loop(0, units // 256, down_terms, 0)
     saves = [pltpu.make_async_copy(g_all, g_all_out, save.at[0])]
     saves[0].start()
-    y_back.wait_recv()
+    y_near.wait_recv()
+    for copy in y_far:
+        copy.wait_recv()
 
     def y_sum(here, i):
-        there = pl.ds(pl.multiple_of(rows + i * 32, 32), 32)
         y_keep[here, :] = (
             hidden[here, :] + part_y[here, :].astype(f32) + got_y[here, :].astype(f32)
         )
-        y_send[here, :] = (part_y[there, :].astype(f32) + got_y[there, :].astype(f32)).astype(bf16)
 
     row_loop(rows, 32, y_sum)
+    for i in range(2):
+
+        def y_pair(here, j):
+            there = pl.ds(pl.multiple_of((2 + i) * rows + j * 32, 32), 32)
+            came = pl.ds(pl.multiple_of(rows + i * half + j * 32, 32), 32)
+            to = pl.ds(pl.multiple_of(i * half + j * 32, 32), 32)
+            y_send[to, :] = (part_y[there, :].astype(f32) + got_y[came, :].astype(f32)).astype(bf16)
+
+        row_loop(half, 32, y_pair)
     back_near.wait_recv()
-    back_over.wait_recv()
     gain_part[...] = jnp.zeros_like(gain_part)
-
-    def finish(here, i):
-        unit, inverse = centred(hidden[here, :])
-        grad = (
-            part_x[here, :].astype(f32) + got_x[0, here, :].astype(f32)
-        ) + got_x[2, here, :].astype(f32)
-        gain_part[...] += jnp.sum(grad * unit, axis=0, keepdims=True)
-        grad_hidden[here, :] = cot[here, :].astype(f32) + norm_rows_back(
-            grad * gain[...], unit, inverse
-        )
-
-    row_loop(rows, 32, finish)
-    for copy in (near, over, far, back_near, back_far, back_over, y_back):
+    for i in range(2):
+        back_over[i].wait_recv()
+
+        def finish(here, j):
+            at = pl.ds(pl.multiple_of(i * half + j * 32, 32), 32)
+            unit, inverse = centred(hidden[at, :])
+            grad = (part_x[at, :].astype(f32) + got_own[at, :].astype(f32)) + got_x[
+                2 + i, here, :
+            ].astype(f32)
+            gain_part[...] += jnp.sum(grad * unit, axis=0, keepdims=True)
+            grad_hidden[at, :] = cot[at, :].astype(f32) + norm_rows_back(
+                grad * gain[...], unit, inverse
+            )
+
+        row_loop(half, 32, finish)
+    for copy in [near, back_near, y_near] + over + far + back_far + back_over + y_far:
         copy.wait_send()
     for copy in saves:
         copy.wait()
@@ -895,17 +998,18 @@
             pltpu.VMEM((4 * rows, units), bf16),
             pltpu.VMEM((4 * rows, width), bf16),
             pltpu.VMEM((4 * rows, width), bf16),
-            pltpu.VMEM((3, rows, width), bf16),
+            pltpu.VMEM((4, rows // 2, width), bf16),
+            pltpu.VMEM((rows, width), bf16),
             pltpu.VMEM((2 * rows, width), bf16),
             pltpu.VMEM((rows, 512), f32),
             pltpu.VMEM((rows, 512), f32),
             pltpu.VMEM(gathered, bf16),
             pltpu.VMEM(w_up.shape, bf16),
             pltpu.VMEM(w_down.shape, bf16),
-            dma((6,)),
+            dma((8,)),
             dma((1,)),
-            dma((7,)),
-            dma((7,)),
+            dma((13,)),
+            dma((13,)),
         ],
         compiler_params=pltpu.CompilerParams(
             collective_id=1, has_side_effects=True, vmem_limit_bytes=LIMIT
@@ -930,15 +1034,21 @@
     inv_in,
     p_in,
     r_in,
+    cosine_all,
+    sine_all,
+    mask_all,
+    q_scale_all,
+    k_scale_all,
+    decay_all,
+    d_out,
+    g_out,
+    y_got,
     cosine,
     sine,
     mask,
     q_scale,
     k_scale,
     decay,
-    d_out,
-    g_out,
-    y_got,
     dx,
     q,
     k,
@@ -963,6 +1073,7 @@
     g_wo,
     load,
     save,
+    save_rows,
     g_send,
     g_recv,
     c_send,
@@ -976,6 +1087,18 @@
     s, z = lax.axis_index("seq"), lax.axis_index("mp")
     place = lax.rem(s, SEQ_DEVS)
     pair = z + 1 - 2 * lax.rem(z, 2)
+    def tables(place, z):
+        at = block(cosine.shape[0], place)
+        some = pl.ds(z * heads, heads)
+        return [
+            (cosine_all.at[at], cosine),
+            (sine_all.at[at], sine),
+            (mask_all.at[some], mask),
+            (q_scale_all.at[some], q_scale),
+            (k_scale_all.at[some], k_scale),
+            (decay_all.at[some], decay),
+        ]
+
     loads = [
         pltpu.make_async_copy(a, b, load.at[i])
         for i, (a, b) in enumerate(
@@ -991,6 +1114,7 @@
                 (p_in, weights),
                 (r_in, entering),
             ]
+            + tables(place, z)
         )
     ]
     for copy in loads:
@@ -1051,14 +1175,29 @@
         for h in range(heads):
             cols = slice(h * DK, (h + 1) * DK)
             wide = slice(h * DV, (h + 1) * DV)
+            qd = (q[at, cols].astype(f32) * q_scale[h]).astype(bf16)
+            grown[h, j] = product_t(qd, do[at, wide])
+
+        @pl.when(j != last)
+        def _():
+            rest(j)
+
+    last = jnp.where(z < depth // 2, depth - 1, 0)
+
+    def rest(j):
+        at = block(rows, j)
+        for h in range(heads):
+            cols = slice(h * DK, (h + 1) * DK)
+            wide = slice(h * DV, (h + 1) * DV)
             qb, kb, vb, db = q[at, cols], k[at, cols], v[at, wide], do[at, wide]
             raw = product_rt(db, vb) + product_rt(do_low[:, wide], vb)
             ds = (raw * mask[h]).astype(bf16)
             dv[at, wide] = product_t(weights[h, j], db)
             dk[at, cols] = product_t(ds, qb)
             turn_back(dot(ds, kb) + q_scale[h] * product_rt(db, entering[h, j]), at, h * DK)
-            qd = (qb.astype(f32) * q_scale[h]).astype(bf16)
-            grown[h, j] = product_t(qd, db)
+
+    def chain(h, to):
+        return remote(state_to.at[h], state_in.at[h], c_send.at[h], c_recv.at[h], to, z)
 
     line_gather(dx, g_send, g_recv, s, z, depth, use)
     swap = remote(y_send, y_got, y_sems.at[0], y_sems.at[1], s, pair)
@@ -1078,32 +1217,41 @@
         for b in reversed(range(depth - 1)):
             state[h] = decay[h, 0] * state[h] + grown[h, b]
 
-    @pl.when(place <= 1)
+        @pl.when(place == SEQ_DEVS - 1)
+        def _():
+            state_to[h] = state[h].astype(bf16)
+            chain(h, s - 1).start()
+
+    rest(last)
+
+    @pl.when(place == 0)
     def _():
         out_grad()
 
-    def chain(h, to):
-        return remote(state_to.at[h], state_in.at[h], c_send.at[h], c_recv.at[h], to, z)
-
     for h in range(heads):
 
         @pl.when(place < SEQ_DEVS - 1)
         def _():
             chain(h, s + 1).wait_recv()
 
-        @pl.when(place > 0)
+        @pl.when((place > 0) & (place < SEQ_DEVS - 1))
         def _():
             state_to[h] = (decay[h, 1] * state_in[h].astype(f32) + state[h]).astype(bf16)
             chain(h, s - 1).start()
 
     for h in range(heads):
-        cols = slice(h * DK, (h + 1) * DK)
-        wide = slice(h * DV, (h + 1) * DV)
         state[h] = state_in[h].astype(f32)
 
-        def cross(turn, _):
-            b = depth - 1 - turn
-            at = block(rows, b)
+    def done(b):
+        at = block(rows, b)
+        return pltpu.make_async_copy(dall.at[at], d_out.at[at], save_rows.at[b])
+
+    def cross(turn, _):
+        b = depth - 1 - turn
+        at = block(rows, b)
+        for h in range(heads):
+            cols = slice(h * DK, (h + 1) * DK)
+            wide = slice(h * DV, (h + 1) * DV)
             leaving = state[h].astype(bf16)
             state[h] = grown[h, b] + decay[h, 0] * state[h]
             kb = k[at, cols]
@@ -1112,20 +1260,18 @@
             dall[at, 2 * hk + h * DV : 2 * hk + (h + 1) * DV] = (
                 dv[at, wide] + k_scale[h] * dot(kb, leaving)
             ).astype(bf16)
-            return 0
-
-        lax.fori_loop(0, depth, cross, 0)
-    saves = [
-        pltpu.make_async_copy(dall, d_out, save.at[0]),
-        pltpu.make_async_copy(g_wo, g_out, save.at[1]),
-    ]
+        done(b).start()
+        return 0
+
+    lax.fori_loop(0, depth, cross, 0)
+    saves = [pltpu.make_async_copy(g_wo, g_out, save.at[0])]
+
+    @pl.when(place > 0)
+    def _():
+        out_grad()
+
     saves[0].start()
-
-    @pl.when(place > 1)
-    def _():
-        out_grad()
-
-    saves[1].start()
+    lax.fori_loop(0, depth, lambda b, c: (done(b).wait(), c)[1], 0)
     line_gather_end(dx, g_send, g_recv, s, z, depth)
 
     @pl.when(place > 0)
@@ -1145,7 +1291,7 @@
     depth = lax.axis_size("mp")
     rows, width = grad_hidden.shape
     span = depth * rows
-    heads = mask.shape[0]
+    heads = q.shape[1] // DK
     hk, hv = q.shape[1], v.shape[1]
     any_ = pl.BlockSpec(memory_space=pl.ANY)
     vmem = pl.BlockSpec(memory_space=pltpu.VMEM)
@@ -1157,9 +1303,15 @@
             jax.ShapeDtypeStruct((hv, width), bf16),
             jax.ShapeDtypeStruct((rows, width), bf16),
         ],
-        in_specs=[vmem] + [any_] * 11 + [vmem] * 6,
+        in_specs=[vmem] + [any_] * 17,
         out_specs=[any_] * 3,
         scratch_shapes=[
+            pltpu.VMEM((span, DK // 2), f32),
+            pltpu.VMEM((span, DK // 2), f32),
+            pltpu.VMEM((heads, rows, rows), f32),
+            pltpu.VMEM((heads, rows, 1), f32),
+            pltpu.VMEM((heads, rows, 1), f32),
+            pltpu.VMEM((heads, 2, 1, DV), f32),
             pltpu.VMEM((depth, rows, width), bf16),
             pltpu.VMEM((span, hk), bf16),
             pltpu.VMEM((span, hk), bf16),
@@ -1182,8 +1334,9 @@
             pltpu.VMEM((heads, DK, DV), bf16),
             pltpu.VMEM((heads, DK, DV), bf16),
             pltpu.VMEM((hv, width), bf16),
-            dma((10,)),
-            dma((2,)),
+            dma((16,)),
+            dma((1,)),
+            dma((depth,)),
             dma((2, depth)),
             dma((depth,)),
             dma((heads,)),
@@ -1388,6 +1541,8 @@
     gain_all,
     gain_line,
     load,
+    d_load,
+    x_load,
     s_send,
     s_recv,
     f_sems,
@@ -1405,14 +1560,31 @@
     loads = [
         pltpu.make_async_copy(a, b, load.at[i])
         for i, (a, b) in enumerate(
-            [(d_in, d), (w_query, wq), (w_key, wk), (w_value, wv), (w_gate, wg), (x_in, x)]
+            [(w_query, wq), (w_key, wk), (w_value, wv), (w_gate, wg)]
         )
     ]
+
+    def slot_loads(j):
+        at = block(rows, j)
+        return [
+            pltpu.make_async_copy(d_in.at[at], d.at[at], d_load.at[j]),
+            pltpu.make_async_copy(x_in.at[j], x.at[j], x_load.at[j]),
+        ]
+
     late = [
-        pltpu.make_async_copy(a, b, load.at[6 + i])
+        pltpu.make_async_copy(a, b, load.at[4 + i])
         for i, (a, b) in enumerate([(tok_in, tok), (grad_hidden_in, grad_hidden)])
     ]
-    for copy in loads + late:
+    for copy in loads:
+        copy.start()
+
+    def pull(i, _):
+        for copy in slot_loads(jnp.where(z < depth // 2, depth - 1 - i, i)):
+            copy.start()
+        return 0
+
+    lax.fori_loop(0, depth, pull, 0)
+    for copy in late:
         copy.start()
     gains[...] = jnp.zeros_like(gains)
     gains[1:2, :] = gain_part[...]
@@ -1465,6 +1637,8 @@
         return value
 
     def partial(j):
+        for copy in slot_loads(j):
+            copy.wait()
         for n in range(0, width, step):
             sbuf[j, :, n : n + step] = term(j, n).astype(bf16)
 
@@ -1485,6 +1659,8 @@
         lax.fori_loop(0, count, one, 0)
 
     def own():
+        for copy in slot_loads(z):
+            copy.wait()
         for n in range(0, width, step):
             total[:, n : n + step] = term(z, n)
         gains[0:1, :] = gains[0:1, :] / gain[...]
@@ -1593,7 +1769,9 @@
             pltpu.VMEM(far.shape[1:], bf16),
             pltpu.VMEM((count, 8, width), f32),
             pltpu.VMEM((depth, 8, width), f32),
-            dma((8,)),
+            dma((6,)),
+            dma((depth,)),
+            dma((depth,)),
             dma((depth,)),
             dma((depth + 1,)),
             dma((6,)),
@@ -1650,22 +1828,7 @@
     f32 = jnp.float32
     span_rows = lax.axis_size("mp") * tokens.shape[0]
     local_heads = w_query.shape[1] // DK
-    place = lax.axis_index("seq") % SEQ_DEVS
-    positions = place * span_rows + jnp.arange(span_rows, dtype=jnp.int32)
-    cosine, sine = angles(positions)
-    heads = (lax.axis_index("mp") * local_heads).astype(f32) + jnp.arange(local_heads, dtype=f32)
-    logs = jnp.log1p(-jnp.exp2(-5.0 - heads))
-    steps = jnp.arange(STRETCH, dtype=f32)
-    gaps = steps[:, None] - steps[None, :]
-    mask = jnp.where(gaps >= 0, jnp.exp(logs[:, None, None] * jnp.maximum(gaps, 0.0)), 0.0)
-    q_scale = jnp.exp(logs[:, None] * (steps + 1.0))[:, :, None]
-    k_scale = jnp.exp(logs[:, None] * (STRETCH - 1.0 - steps))[:, :, None]
-    span_decay = jnp.exp(logs * span_rows)
-    decay = jnp.broadcast_to(
-        jnp.stack([jnp.exp(logs * STRETCH), span_decay], axis=1)[:, :, None, None],
-        (local_heads, 2, 1, DV),
-    )
-    trig = (cosine[:, 0], sine[:, 0], mask, q_scale, k_scale, decay)
+    trig = decay_tables(span_rows, local_heads * lax.axis_size("mp"))
     (
         x_rows,
         q_all,

time: 509 us -> 485 us (0.953)
  Pallas kernels: 481 us -> 463 us
  other arithmetic: 6.44 us -> 1.25 us
    pallas_call x1, Pallas kernels: 72.8 us -> 57.5 us  [feed(): pl.pallas_call(feed_kernel, out_shape=[jax.ShapeDtypeStruct((rows, width)...]
    pallas_call x1, Pallas kernels: 94.9 us -> 89.6 us  [finish(): pl.pallas_call(finish_kernel, out_shape=[jax.ShapeDtypeStruct((rows, widt...]
where the time goes in v5:
time: 485 us
  Pallas kernels  463 us (95%)
  between operations  14.1 us (3%)
    pallas_call x1, Pallas kernels, attend(): pl.pallas_call(attend_kernel, out_shape=[jax.ShapeDtypeStruct(*one) for o...  174 us
    pallas_call x1, Pallas kernels, retract(): pl.pallas_call(retract_kernel, out_shape=[jax.ShapeDtypeStruct((span, 2 *...  107 us
    pallas_call x1, Pallas kernels, finish(): pl.pallas_call(finish_kernel, out_shape=[jax.ShapeDtypeStruct((rows, widt...  89.6 us
    pallas_call x1, Pallas kernels, feed(): pl.pallas_call(feed_kernel, out_shape=[jax.ShapeDtypeStruct((rows, width)...  57.5 us
    pallas_call x1, Pallas kernels, pair_sum(): pl.pallas_call(pair_kernel, out_shape=[jax.ShapeDtypeStruct((chips, high,...  29.6 us
  transfers between devices with their start and end apart: 2, of which 1 were waited for; matrix products, arithmetic and copies ran while one was open for 0% of the time, Pallas kernels for 40%

profile of v5, /device:TPU:0, one launch (start us, length us, event | category | flops | bytes accessed | tf_op | source)
XLA Modules:
  0.0 484.8 jit_solution(15949920878500653733)
XLA Ops:
  7.2 0.0 reduce-scatter.7.cloned.1.call-start
  7.2 174.1 %attend.1 = (bf16[4,256,2048]{2,1,0:T(8,128)(2,1)}, bf16[1024,512]{1,0:T(8,128)(2,1)}, bf16[1024,512]{1,0:T(8,128)(2,1)}, bf16[1024,1024]{1,0:T(8,128)(2,1)}, f3...) custom-call(bf16[256,2048]{1,0:T(8,128)(2,1)} %tok_in.1, ...), custom_call_target="tpu_custom_call" | custom-call | flops 190000005120 | bytes 60000000 | tf_op jit(solution)/shard_map/attend/pallas_call | solution.py:649
  181.3 57.5 %feed.1 = (f32[256,2048]{1,0:T(8,128)}, bf16[256,2048]{1,0:T(8,128)(2,1)}, f32[256,2048]{1,0:T(8,128)}, f32[1,2048]{1,0:T(1,128)}, bf16[4,2,512,1024]{3,2,1,0:T(8,128)(2,1)}) custom-call(f32[256,2048]{1,0:T(8,128)} %get-tuple-element.50.hidden, f32[1,2048]{1,0:T(1,128)} %bitcast.14, bf16[256,2048]{1,0:T(8,128)(2,1)} %cot.3, ...), custom_call_target="tpu_custom_call" | custom-call | flops 74999996416 | bytes 30000000 | tf_op jit(solution)/shard_map/feed/pallas_call | solution.py:983
  238.8 0.0 reduce-scatter.7.cloned.1.call-update
  238.8 0.0 reduce-scatter.9.cloned.1.call-start
  238.8 106.6 %retract.1 = (bf16[1024,3072]{1,0:T(8,128)(2,1)}, bf16[1024,2048]{1,0:T(8,128)(2,1)}, bf16[256,2048]{1,0:T(8,128)(2,1)}) custom-call(f32[256,2048]{1,0:T(8,128)} %get-tuple-element.55.grad_hidden.grad_hidden_in, bf16[256,2048]{1,0:T(8,128)(2,1)} %get-tuple-element.56.y_send, bf16[1024,2048]{1,0:T(8,128)(2,1)} %w_out.3, ...), custom_call_target="tpu_custom_call" | custom-call | flops 120000004096 | bytes 40000000 | tf_op jit(solution)/shard_map/retract/pallas_call | solution.py:1299
  345.5 0.0 reduce-scatter.7.cloned.1.call-done
  345.5 29.6 %pair_sum.1 = (bf16[4,1024,1024]{2,1,0:T(8,128)(2,1)}, bf16[512,1024]{1,0:T(8,128)(2,1)}) custom-call(bf16[1024,2048]{1,0:T(8,128)(2,1)} %bitcast.17, bf16[1024,3072]{1,0:T(8,128)(2,1)} %get-tuple-element.72.d.d_in, bf16[4,2,128,2048]{3,2,1,0:T(8,128)(2,1)} %bitcast.18, bf16[2,512,1024]{2,1,0:T(8,128)(2,1)} %bitcast.12), custom_call_target="tpu_custom_call" | custom-call | flops 24999999488 | bytes 30000000 | tf_op jit(solution)/shard_map/pair_sum/pallas_call | solution.py:1481
  375.2 0.0 copy-start
  375.2 0.0 copy-start.1
  375.2 0.0 reduce-scatter.9.cloned.1.call-update
  375.2 1.5 copy-done
  376.8 0.3 copy-done.1
  377.0 1.3 add_convert_fusion
  378.3 89.6 %finish.1 = (bf16[256,2048]{1,0:T(8,128)(2,1)}, f32[8,2048]{1,0:T(8,128)}, f32[256,1024]{1,0:T(8,128)}, f32[128,2048]{1,0:T(8,128)}) custom-call(bf16[1024,3072]{1,0:T(8,128)(2,1)} %get-tuple-element.72.d.d_in, bf16[4,256,2048]{2,1,0:T(8,128)(2,1)} %get-tuple-element.67.x_in, bf16[256,2048]{1,0:T(8,128)(2,1)} %tok_in.1, f32[1,2048]{1,0:T(1,128)} %bitcast.16, ...), custom_call_target="tpu_custom_call" | custom-call | flops 109999996928 | bytes 30000000 | tf_op jit(solution)/shard_map/finish/pallas_call | solution.py:1746
  467.9 3.1 reduce-scatter.9.cloned.1.call-done
  471.0 1.5 fusion
  472.5 5.5 %unpack.1 = (f32[256,512]{1,0:T(8,128)}, f32[256,512]{1,0:T(8,128)}, f32[256,1024]{1,0:T(8,128)}, f32[256,1024]{1,0:T(8,128)}, f32[128,2048]{1,0:T(8,128)}, /*in...) custom-call(bf16[1024,1024]{1,0:T(8,128)(2,1)} %bitcast.9, ...), custom_call_target="tpu_custom_call" | custom-call | tf_op jit(solution)/shard_map/unpack/pallas_call | solution.py:1815
Async XLA Ops:
  7.2 338.3 %reduce-scatter.7.cloned.1.call-start = ((), (), s32[]{:S(2)}) async-start(), calls=%async_computation.2 | async-start | bytes 10485760
  238.8 232.2 %reduce-scatter.9.cloned.1.call-start = ((), (), s32[]{:S(2)}) async-start(), calls=%async_computation.3 | async-start | bytes 10485760
  375.2 1.6 copy-start
  375.2 1.8 copy-start.1
Sparse Core Ops, SparseCore 0:
  238.9 94.0 reduce-scatter.6
  375.3 95.5 reduce-scatter.8

commit v6 on v5

--- a/solution.py
+++ b/solution.py
@@ -86,42 +86,60 @@
     return jnp.dot(left, right, preferred_element_type=jnp.float32)
 
 
-def line_push(x, send, recv, s, z, slot, way):
-    return remote(x.at[slot], x.at[slot], send.at[way, slot], recv.at[slot], s, z + 1 - 2 * way)
-
-
-def line_gather(x, send, recv, s, z, depth, use, after=None):
-    @pl.when(z < depth - 1)
-    def _():
-        line_push(x, send, recv, s, z, z, 0).start()
-
-    @pl.when(z > 0)
-    def _():
-        line_push(x, send, recv, s, z, z, 1).start()
+HALVES = 2
+
+
+def part_of(rows, part):
+    return pl.ds(part * (rows // HALVES), rows // HALVES)
+
+
+def line_copy(x, send, recv, s, to, slot, part, way):
+    at = x.at[slot, part_of(x.shape[1], part)]
+    return remote(at, at, send.at[way, slot, part], recv.at[slot, part], s, to)
+
+
+def line_gather(x, send, recv, s, z, depth, use, ready, after=None):
+    def right(slot, part):
+        return line_copy(x, send, recv, s, z + 1, slot, part, 0)
+
+    def left(slot, part):
+        return line_copy(x, send, recv, s, z - 1, slot, part, 1)
+
+    for part in range(HALVES):
+        ready(part)
+
+        @pl.when(z < depth - 1)
+        def _():
+            right(z, part).start()
+
+        @pl.when(z > 0)
+        def _():
+            left(z, part).start()
 
     def one(turn, _):
         away = (turn + 1) // 2
-        left, right = z - away, z + away
-
-        @pl.when((turn % 2 == 1) & (left >= 0))
-        def _():
-            remote(x.at[left], x.at[left], send.at[0, left], recv.at[left], s, z - 1).wait_recv()
-
-            @pl.when(z < depth - 1)
+        low, high = z - away, z + away
+        for part in range(HALVES):
+
+            @pl.when((turn % 2 == 1) & (low >= 0))
             def _():
-                line_push(x, send, recv, s, z, left, 0).start()
-
-        @pl.when((turn % 2 == 1) & (right < depth))
-        def _():
-            remote(x.at[right], x.at[right], send.at[1, right], recv.at[right], s, z + 1).wait_recv()
-
-            @pl.when(z > 0)
+                line_copy(x, send, recv, s, z - 1, low, part, 0).wait_recv()
+
+                @pl.when(z < depth - 1)
+                def _():
+                    right(low, part).start()
+
+            @pl.when((turn % 2 == 1) & (high < depth))
             def _():
-                line_push(x, send, recv, s, z, right, 1).start()
+                line_copy(x, send, recv, s, z + 1, high, part, 1).wait_recv()
+
+                @pl.when(z > 0)
+                def _():
+                    left(high, part).start()
 
         if after is not None:
             after(turn)
-        slot = jnp.where(turn % 2 == 1, left, right)
+        slot = jnp.where(turn % 2 == 1, low, high)
 
         @pl.when((slot >= 0) & (slot < depth))
         def _():
@@ -134,13 +152,15 @@
 
 def line_gather_end(x, send, recv, s, z, depth):
     def one(slot, _):
-        @pl.when((slot <= z) & (z < depth - 1))
-        def _():
-            line_push(x, send, recv, s, z, slot, 0).wait_send()
-
-        @pl.when((slot >= z) & (z > 0))
-        def _():
-            line_push(x, send, recv, s, z, slot, 1).wait_send()
+        for part in range(HALVES):
+
+            @pl.when((slot <= z) & (z < depth - 1))
+            def _():
+                line_copy(x, send, recv, s, z + 1, slot, part, 0).wait_send()
+
+            @pl.when((slot >= z) & (z > 0))
+            def _():
+                line_copy(x, send, recv, s, z - 1, slot, part, 1).wait_send()
 
         return 0
 
@@ -161,15 +181,26 @@
 
 
 def line_scatter(sbuf, rbuf, total, send, recv, s, z, depth, partial, own, hook=None):
-    def right(j):
-        return remote(sbuf.at[j], rbuf.at[j], send.at[j], recv.at[j], s, z + 1)
-
-    def left(j):
+    rows = total.shape[0]
+
+    def right(j, part):
+        at = part_of(rows, part)
+        return remote(
+            sbuf.at[j, at], rbuf.at[j, at], send.at[j, part], recv.at[j, part], s, z + 1
+        )
+
+    def left(j, part):
+        at = part_of(rows, part)
         slot = jnp.where(j == z - 1, depth, j)
-        return remote(sbuf.at[j], rbuf.at[slot], send.at[j], recv.at[slot], s, z - 1)
-
-    def arrived(slot, sender):
-        remote(sbuf.at[0], rbuf.at[slot], send.at[0], recv.at[slot], s, sender).wait_recv()
+        return remote(
+            sbuf.at[j, at], rbuf.at[slot, at], send.at[j, part], recv.at[slot, part], s, z - 1
+        )
+
+    def arrived(slot, part, sender):
+        at = part_of(rows, part)
+        remote(
+            sbuf.at[0, at], rbuf.at[slot, at], send.at[0, part], recv.at[slot, part], s, sender
+        ).wait_recv()
 
     def first(turn, _):
         up = depth - 1 + z - turn // 2
@@ -183,11 +214,13 @@
 
             @pl.when((z == 0) & (j > z))
             def _():
-                right(j).start()
+                for part in range(HALVES):
+                    right(j, part).start()
 
             @pl.when((z == depth - 1) & (j < z))
             def _():
-                left(j).start()
+                for part in range(HALVES):
+                    left(j, part).start()
 
         return 0
 
@@ -197,33 +230,35 @@
     def event(turn, _):
         up = depth - 1 + z - turn
         down = turn - (depth - 1) + z
-
-        @pl.when((z > 0) & (up >= z) & (up < depth))
-        def _():
-            arrived(up, z - 1)
-
-            @pl.when(up > z)
+        slot = jnp.where(down == z, depth, down)
+        for part in range(HALVES):
+            at = part_of(rows, part)
+
+            @pl.when((z > 0) & (up >= z) & (up < depth))
             def _():
-                add_rows(sbuf.at[up], rbuf.at[up])
-                right(up).start()
-
-            @pl.when(up == z)
+                arrived(up, part, z - 1)
+
+                @pl.when(up > z)
+                def _():
+                    add_rows(sbuf.at[up, at], rbuf.at[up, at])
+                    right(up, part).start()
+
+                @pl.when(up == z)
+                def _():
+                    add_rows(total.at[at], rbuf.at[up, at])
+
+            @pl.when((z < depth - 1) & (down >= 0) & (down <= z))
             def _():
-                add_rows(total, rbuf.at[up])
-
-        @pl.when((z < depth - 1) & (down >= 0) & (down <= z))
-        def _():
-            slot = jnp.where(down == z, depth, down)
-            arrived(slot, z + 1)
-
-            @pl.when(down < z)
-            def _():
-                add_rows(sbuf.at[down], rbuf.at[down])
-                left(down).start()
-
-            @pl.when(down == z)
-            def _():
-                add_rows(total, rbuf.at[depth])
+                arrived(slot, part, z + 1)
+
+                @pl.when(down < z)
+                def _():
+                    add_rows(sbuf.at[down, at], rbuf.at[down, at])
+                    left(down, part).start()
+
+                @pl.when(down == z)
+                def _():
+                    add_rows(total.at[at], rbuf.at[depth, at])
 
         if hook is not None:
             hook(turn)
@@ -232,13 +267,15 @@
     lax.fori_loop(0, depth, event, 0)
 
     def end(j, _):
-        @pl.when(j > z)
-        def _():
-            right(j).wait_send()
-
-        @pl.when(j < z)
-        def _():
-            left(j).wait_send()
+        for part in range(HALVES):
+
+            @pl.when(j > z)
+            def _():
+                right(j, part).wait_send()
+
+            @pl.when(j < z)
+            def _():
+                left(j, part).wait_send()
 
         return 0
 
@@ -365,7 +402,10 @@
         xg[z, part, :] = (unit * gain[...]).astype(bf16)
         return 0
 
-    lax.fori_loop(0, rows // 32, norm, 0)
+    def ready(part):
+        each = rows // 32 // HALVES
+        lax.fori_loop(part * each, (part + 1) * each, norm, 0)
+
     count = lax.axis_size("seq")
     across = flip(z, 2)
     greet(
@@ -398,14 +438,16 @@
             ),
         ]
 
-    mine.start()
-    near.start()
-
     @pl.when(place == 0)
     def _():
         state_in[...] = jnp.zeros_like(state_in)
 
     def after(turn):
+        @pl.when(turn == 0)
+        def _():
+            mine.start()
+            near.start()
+
         @pl.when(edge & (turn == 1))
         def _():
             swap.start()
@@ -455,7 +497,7 @@
             gp[at, wide] = dot(xg[j], wg[:, wide])
             weights[h, j] = (product_rt(q[at, cols], k[at, cols]) * mask[h]).astype(bf16)
 
-    line_gather(xg, g_send, g_recv, s, z, depth, use, after)
+    line_gather(xg, g_send, g_recv, s, z, depth, use, ready, after)
     def chain(h, to):
         return remote(state_to.at[h], state_in.at[h], c_send.at[h], c_recv.at[h], to, z)
 
@@ -516,33 +558,31 @@
         lax.fori_loop(0, count // 2, to_chip, 0)
 
     for h in range(heads):
-        cols = slice(h * DK, (h + 1) * DK)
-        wide = slice(h * DV, (h + 1) * DV)
         state[h] = state_in[h].astype(f32)
-
-        def cross(b, _):
-            at = block(rows, b)
+        for b in range(depth):
             entering[h, b] = state[h].astype(bf16)
-            state[h] = decay[h, 0] * state[h] + grown[h, b]
+            if b < depth - 1:
+                state[h] = decay[h, 0] * state[h] + grown[h, b]
+    saves[6].start()
+
+    def cross(b):
+        at = block(rows, b)
+        for h in range(heads):
+            cols = slice(h * DK, (h + 1) * DK)
+            wide = slice(h * DV, (h + 1) * DV)
             qd = (q[at, cols].astype(f32) * q_scale[h]).astype(bf16)
             tile[...] = dot(weights[h, b], v[at, wide]) + dot(qd, entering[h, b])
 
-            def norm(i, _):
-                here = block(32, i)
+            def norm(here, i):
                 there = pl.ds(pl.multiple_of(b * rows + i * 32, 32), 32)
                 unit, inverse = centred(tile[here, :])
                 gate = gp[there, wide]
                 gn[there, wide] = unit
                 gated[there, wide] = (unit * gate / (1.0 + jnp.exp(-gate))).astype(bf16)
                 inv[h, there, :] = jnp.broadcast_to(inverse, (32, inv.shape[2]))
-                return 0
-
-            lax.fori_loop(0, rows // 32, norm, 0)
-            return 0
-
-        lax.fori_loop(0, depth, cross, 0)
-    for copy in saves[6:]:
-        copy.start()
+
+            row_loop(rows, 32, norm)
+
     line_gather_end(xg, g_send, g_recv, s, z, depth)
 
     @pl.when(jnp.logical_not(edge))
@@ -569,10 +609,14 @@
             far.start()
 
     def partial(j):
+        cross(j)
         for n in range(0, total.shape[1], wide):
             xg[j, :, n : n + wide] = dot(gated[block(rows, j), :], wo[:, n : n + wide]).astype(bf16)
 
     def own():
+        cross(z)
+        for copy in saves[7:]:
+            copy.start()
         for n in range(0, total.shape[1], wide):
             total[:, n : n + wide] = tok[:, n : n + wide].astype(f32) + dot(
                 gated[block(rows, z), :], wo[:, n : n + wide]
@@ -682,10 +726,10 @@
             pltpu.VMEM(w_out.shape, bf16),
             dma((11,)),
             dma((10,)),
-            dma((2, depth)),
-            dma((depth,)),
-            dma((depth,)),
-            dma((depth + 1,)),
+            dma((2, depth, HALVES)),
+            dma((depth, HALVES)),
+            dma((depth, HALVES)),
+            dma((depth + 1, HALVES)),
             dma((heads,)),
             dma((heads,)),
             dma((4,)),
@@ -1123,7 +1167,10 @@
     def low(here, i):
         dx[z, here, :] = grad_hidden[here, :].astype(bf16)
 
-    row_loop(rows, 32, low)
+    def ready(part):
+        row_loop(rows // HALVES, 32, lambda here, i: low(
+            pl.ds(pl.multiple_of(part * (rows // HALVES) + i * 32, 32), 32), i))
+
     greet(
         [
             (z > 0, s, z - 1),
@@ -1199,7 +1246,7 @@
     def chain(h, to):
         return remote(state_to.at[h], state_in.at[h], c_send.at[h], c_recv.at[h], to, z)
 
-    line_gather(dx, g_send, g_recv, s, z, depth, use)
+    line_gather(dx, g_send, g_recv, s, z, depth, use, ready)
     swap = remote(y_send, y_got, y_sems.at[0], y_sems.at[1], s, pair)
     swap.start()
     def out_terms(m, _):
@@ -1337,8 +1384,8 @@
             dma((16,)),
             dma((1,)),
             dma((depth,)),
-            dma((2, depth)),
-            dma((depth,)),
+            dma((2, depth, HALVES)),
+            dma((depth, HALVES)),
             dma((heads,)),
             dma((heads,)),
             dma((2,)),
@@ -1772,8 +1819,8 @@
             dma((6,)),
             dma((depth,)),
             dma((depth,)),
-            dma((depth,)),
-            dma((depth + 1,)),
+            dma((depth, HALVES)),
+            dma((depth + 1, HALVES)),
             dma((6,)),
             dma((count,)),
             dma((count,)),

time: 485 us -> 468 us (0.965)
  Pallas kernels: 463 us -> 446 us
    pallas_call x1, Pallas kernels: 107 us -> 97.7 us  [retract(): pl.pallas_call(retract_kernel, out_shape=[jax.ShapeDtypeStruct((span, 2 *...]
    pallas_call x1, Pallas kernels: 174 us -> 168 us  [attend(): pl.pallas_call(attend_kernel, out_shape=[jax.ShapeDtypeStruct(*one) for o...]
  transfers between devices with their start and end apart: 2 -> 2, of which waited for: 1 -> 1; matrix products, arithmetic and copies ran while one was open for 0% -> 0% of each run, Pallas kernels for 40% -> 39%
where the time goes in v6:
time: 468 us
  Pallas kernels  446 us (95%)
  between operations  14.1 us (3%)
    pallas_call x1, Pallas kernels, attend(): pl.pallas_call(attend_kernel, out_shape=[jax.ShapeDtypeStruct(*one) for o...  168 us
    pallas_call x1, Pallas kernels, retract(): pl.pallas_call(retract_kernel, out_shape=[jax.ShapeDtypeStruct((span, 2 *...  97.7 us
    pallas_call x1, Pallas kernels, finish(): pl.pallas_call(finish_kernel, out_shape=[jax.ShapeDtypeStruct((rows, widt...  86 us
    pallas_call x1, Pallas kernels, feed(): pl.pallas_call(feed_kernel, out_shape=[jax.ShapeDtypeStruct((rows, width)...  57.4 us
    pallas_call x1, Pallas kernels, pair_sum(): pl.pallas_call(pair_kernel, out_shape=[jax.ShapeDtypeStruct((chips, high,...  31.3 us
  transfers between devices with their start and end apart: 2, of which 1 were waited for; matrix products, arithmetic and copies ran while one was open for 0% of the time, Pallas kernels for 39%

profile of v6, /device:TPU:0, one launch (start us, length us, event | category | flops | bytes accessed | tf_op | source)
XLA Modules:
  0.0 468.1 jit_solution(10120968737415232178)
XLA Ops:
  7.2 0.0 reduce-scatter.7.cloned.1.call-start
  7.2 168.2 %attend.1 = (bf16[4,256,2048]{2,1,0:T(8,128)(2,1)}, bf16[1024,512]{1,0:T(8,128)(2,1)}, bf16[1024,512]{1,0:T(8,128)(2,1)}, bf16[1024,1024]{1,0:T(8,128)(2,1)}, f3...) custom-call(bf16[256,2048]{1,0:T(8,128)(2,1)} %tok_in.1, ...), custom_call_target="tpu_custom_call" | custom-call | flops 190000005120 | bytes 60000000 | tf_op jit(solution)/shard_map/attend/pallas_call | solution.py:693
  175.4 57.4 %feed.1 = (f32[256,2048]{1,0:T(8,128)}, bf16[256,2048]{1,0:T(8,128)(2,1)}, f32[256,2048]{1,0:T(8,128)}, f32[1,2048]{1,0:T(1,128)}, bf16[4,2,512,1024]{3,2,1,0:T(8,128)(2,1)}) custom-call(f32[256,2048]{1,0:T(8,128)} %get-tuple-element.50.hidden, f32[1,2048]{1,0:T(1,128)} %bitcast.14, bf16[256,2048]{1,0:T(8,128)(2,1)} %cot.3, ...), custom_call_target="tpu_custom_call" | custom-call | flops 74999996416 | bytes 30000000 | tf_op jit(solution)/shard_map/feed/pallas_call | solution.py:1027
  232.8 0.0 reduce-scatter.7.cloned.1.call-update
  232.9 0.0 reduce-scatter.9.cloned.1.call-start
  232.9 97.7 %retract.1 = (bf16[1024,3072]{1,0:T(8,128)(2,1)}, bf16[1024,2048]{1,0:T(8,128)(2,1)}, bf16[256,2048]{1,0:T(8,128)(2,1)}) custom-call(f32[256,2048]{1,0:T(8,128)} %get-tuple-element.55.grad_hidden.grad_hidden_in, bf16[256,2048]{1,0:T(8,128)(2,1)} %get-tuple-element.56.y_send, bf16[1024,2048]{1,0:T(8,128)(2,1)} %w_out.3, ...), custom_call_target="tpu_custom_call" | custom-call | flops 120000004096 | bytes 40000000 | tf_op jit(solution)/shard_map/retract/pallas_call | solution.py:1346
  330.6 0.0 reduce-scatter.7.cloned.1.call-done
  330.6 31.3 %pair_sum.1 = (bf16[4,1024,1024]{2,1,0:T(8,128)(2,1)}, bf16[512,1024]{1,0:T(8,128)(2,1)}) custom-call(bf16[1024,2048]{1,0:T(8,128)(2,1)} %bitcast.17, bf16[1024,3072]{1,0:T(8,128)(2,1)} %get-tuple-element.72.d.d_in, bf16[4,2,128,2048]{3,2,1,0:T(8,128)(2,1)} %bitcast.18, bf16[2,512,1024]{2,1,0:T(8,128)(2,1)} %bitcast.12), custom_call_target="tpu_custom_call" | custom-call | flops 24999999488 | bytes 30000000 | tf_op jit(solution)/shard_map/pair_sum/pallas_call | solution.py:1528
  361.9 0.0 copy-start
  361.9 0.0 copy-start.1
  361.9 0.0 reduce-scatter.9.cloned.1.call-update
  361.9 1.5 copy-done
  363.5 0.3 copy-done.1
  363.7 1.3 add_convert_fusion
  365.0 86.0 %finish.1 = (bf16[256,2048]{1,0:T(8,128)(2,1)}, f32[8,2048]{1,0:T(8,128)}, f32[256,1024]{1,0:T(8,128)}, f32[128,2048]{1,0:T(8,128)}) custom-call(bf16[1024,3072]{1,0:T(8,128)(2,1)} %get-tuple-element.72.d.d_in, bf16[4,256,2048]{2,1,0:T(8,128)(2,1)} %get-tuple-element.67.x_in, bf16[256,2048]{1,0:T(8,128)(2,1)} %tok_in.1, f32[1,2048]{1,0:T(1,128)} %bitcast.16, ...), custom_call_target="tpu_custom_call" | custom-call | flops 109999996928 | bytes 30000000 | tf_op jit(solution)/shard_map/finish/pallas_call | solution.py:1793
  451.0 3.2 reduce-scatter.9.cloned.1.call-done
  454.3 1.5 fusion
  455.8 5.5 %unpack.1 = (f32[256,512]{1,0:T(8,128)}, f32[256,512]{1,0:T(8,128)}, f32[256,1024]{1,0:T(8,128)}, f32[256,1024]{1,0:T(8,128)}, f32[128,2048]{1,0:T(8,128)}, /*in...) custom-call(bf16[1024,1024]{1,0:T(8,128)(2,1)} %bitcast.9, ...), custom_call_target="tpu_custom_call" | custom-call | tf_op jit(solution)/shard_map/unpack/pallas_call | solution.py:1862
Async XLA Ops:
  7.2 323.4 %reduce-scatter.7.cloned.1.call-start = ((), (), s32[]{:S(2)}) async-start(), calls=%async_computation.2 | async-start | bytes 10485760
  232.9 221.4 %reduce-scatter.9.cloned.1.call-start = ((), (), s32[]{:S(2)}) async-start(), calls=%async_computation.3 | async-start | bytes 10485760
  361.9 1.6 copy-start
  361.9 1.8 copy-start.1
Sparse Core Ops, SparseCore 0:
  233.0 84.4 reduce-scatter.6
  362.0 92.1 reduce-scatter.8

commit v7 on v6

--- a/solution.py
+++ b/solution.py
@@ -1405,7 +1405,7 @@
 
 
 def pair_kernel(
-    x, d, wo_parts, far, out, far_got, stage, got, wo_mine, wo_got, result, save, send, recv, w_sems, f_sems
+    x_in, d_in, wo_parts, far, out, far_got, x, d, stage, got, wo_mine, wo_got, result, load, save, send, recv, w_sems, f_sems
 ):
     f32, bf16 = jnp.float32, jnp.bfloat16
     _, chips, rows, _ = stage.shape
@@ -1416,6 +1416,12 @@
     twin = flip(s, 1)
     across = flip(z, 2)
     edge = (z == 0) | (z == lax.axis_size("mp") - 1)
+    loads = [
+        pltpu.make_async_copy(d_in, d, load.at[0]),
+        pltpu.make_async_copy(x_in, x, load.at[1]),
+    ]
+    for copy in loads:
+        copy.start()
     greet([(z >= 0, twin, z), (z >= 0, s, across), (z >= 0, twin, across)])
     crossed = remote(far.at[0], far_got, f_sems.at[0], f_sems.at[1], twin, across)
     straight = remote(far.at[1], far_got, f_sems.at[2], f_sems.at[3], s, across)
@@ -1438,6 +1444,8 @@
     def keep(i):
         return pltpu.make_async_copy(result.at[i], out.at[i], save.at[i])
 
+    base = rows * (d.shape[1] // third)
+
     def take(i):
         give(i).wait_recv()
         for t in range(d.shape[1] // third):
@@ -1450,6 +1458,15 @@
                 ).astype(bf16)
 
             row_loop(rows, 32, add)
+        for t in range(wo_mine.shape[2] // third):
+            cols = slice(t * third, (t + 1) * third)
+            result[i, base + t * few : base + (t + 1) * few, :] = (
+                wo_mine[i, :, cols].astype(f32) + wo_got[i, :, cols].astype(f32)
+            ).astype(bf16)
+        keep(i).start()
+
+    for copy in loads:
+        copy.wait()
 
     def one(g, _):
         for c in range(span // 256):
@@ -1464,6 +1481,11 @@
         for e in range(each):
             give(g * each + e).start()
 
+        @pl.when(g == 1)
+        def _():
+            wo_load.wait()
+            wo_send.wait()
+
         @pl.when(g > 0)
         def _():
             for e in range(each):
@@ -1473,32 +1495,14 @@
 
     groups = chips // each
     lax.fori_loop(0, groups, one, 0)
-    wo_load.wait()
-    wo_send.wait()
-    base = rows * (d.shape[1] // third)
-
-    def wo_add(i, _):
-        for t in range(wo_mine.shape[2] // third):
-            cols = slice(t * third, (t + 1) * third)
-            result[i, base + t * few : base + (t + 1) * few, :] = (
-                wo_mine[i, :, cols].astype(f32) + wo_got[i, :, cols].astype(f32)
-            ).astype(bf16)
-        return 0
-
-    lax.fori_loop(0, chips, wo_add, 0)
     for e in range(each):
         take((groups - 1) * each + e)
-
-    def begin(i, _):
-        keep(i).start()
-        return 0
 
     def end(i, _):
         keep(i).wait()
         give(i).wait_send()
         return 0
 
-    lax.fori_loop(0, chips, begin, 0)
     lax.fori_loop(0, chips, end, 0)
 
     @pl.when(edge & (core == 1))
@@ -1523,7 +1527,6 @@
     wide, third = d.shape[1], d.shape[1] // 3
     high = 3 * rows + few * g_out.shape[1] // third
     any_ = pl.BlockSpec(memory_space=pl.ANY)
-    vmem = pl.BlockSpec(memory_space=pltpu.VMEM)
     dma = pltpu.SemaphoreType.DMA
     return pl.pallas_call(
         pair_kernel,
@@ -1531,14 +1534,17 @@
             jax.ShapeDtypeStruct((chips, high, third), bf16),
             jax.ShapeDtypeStruct(far.shape[1:], bf16),
         ],
-        in_specs=[vmem, vmem, any_, any_],
+        in_specs=[any_] * 4,
         out_specs=[any_, any_],
         scratch_shapes=[
+            pltpu.VMEM(x.shape, bf16),
+            pltpu.VMEM(d.shape, bf16),
             pltpu.VMEM((2, chips, rows, wide), bf16),
             pltpu.VMEM((chips, rows, wide), bf16),
             pltpu.VMEM((chips, few, g_out.shape[1]), bf16),
             pltpu.VMEM((chips, few, g_out.shape[1]), bf16),
             pltpu.VMEM((chips, high, third), bf16),
+            dma((2,)),
             dma((chips,)),
             dma((chips,)),
             dma((chips,)),

time: 468 us -> 464 us (level)
    pallas_call x1, Pallas kernels: 31.3 us -> 25.7 us  [pair_sum(): pl.pallas_call(pair_kernel, out_shape=[jax.ShapeDtypeStruct((chips, high,...]
  transfers between devices with their start and end apart: 2 -> 2, of which waited for: 1 -> 1; matrix products, arithmetic and copies ran while one was open for 0% -> 0% of each run, Pallas kernels for 39% -> 40%
where the time goes in v7:
time: 464 us
  Pallas kernels  443 us (95%)
  between operations  14.1 us (3%)
    pallas_call x1, Pallas kernels, attend(): pl.pallas_call(attend_kernel, out_shape=[jax.ShapeDtypeStruct(*one) for o...  168 us
    pallas_call x1, Pallas kernels, retract(): pl.pallas_call(retract_kernel, out_shape=[jax.ShapeDtypeStruct((span, 2 *...  97.7 us
    pallas_call x1, Pallas kernels, finish(): pl.pallas_call(finish_kernel, out_shape=[jax.ShapeDtypeStruct((rows, widt...  88.2 us
    pallas_call x1, Pallas kernels, feed(): pl.pallas_call(feed_kernel, out_shape=[jax.ShapeDtypeStruct((rows, width)...  57.4 us
    pallas_call x1, Pallas kernels, pair_sum(): pl.pallas_call(pair_kernel, out_shape=[jax.ShapeDtypeStruct((chips, high,...  25.7 us
  transfers between devices with their start and end apart: 2, of which 1 were waited for; matrix products, arithmetic and copies ran while one was open for 0% of the time, Pallas kernels for 40%

profile of v7, /device:TPU:0, one launch (start us, length us, event | category | flops | bytes accessed | tf_op | source)
XLA Modules:
  0.0 464.1 jit_solution(522296631580031237)
XLA Ops:
  7.2 0.0 reduce-scatter.7.cloned.1.call-start
  7.2 168.2 %attend.1 = (bf16[4,256,2048]{2,1,0:T(8,128)(2,1)}, bf16[1024,512]{1,0:T(8,128)(2,1)}, bf16[1024,512]{1,0:T(8,128)(2,1)}, bf16[1024,1024]{1,0:T(8,128)(2,1)}, f3...) custom-call(bf16[256,2048]{1,0:T(8,128)(2,1)} %tok_in.1, ...), custom_call_target="tpu_custom_call" | custom-call | flops 190000005120 | bytes 60000000 | tf_op jit(solution)/shard_map/attend/pallas_call | solution.py:693
  175.4 57.4 %feed.1 = (f32[256,2048]{1,0:T(8,128)}, bf16[256,2048]{1,0:T(8,128)(2,1)}, f32[256,2048]{1,0:T(8,128)}, f32[1,2048]{1,0:T(1,128)}, bf16[4,2,512,1024]{3,2,1,0:T(8,128)(2,1)}) custom-call(f32[256,2048]{1,0:T(8,128)} %get-tuple-element.50.hidden, f32[1,2048]{1,0:T(1,128)} %bitcast.14, bf16[256,2048]{1,0:T(8,128)(2,1)} %cot.3, ...), custom_call_target="tpu_custom_call" | custom-call | flops 74999996416 | bytes 30000000 | tf_op jit(solution)/shard_map/feed/pallas_call | solution.py:1027
  232.8 0.0 reduce-scatter.7.cloned.1.call-update
  232.9 0.0 reduce-scatter.9.cloned.1.call-start
  232.9 97.7 %retract.1 = (bf16[1024,3072]{1,0:T(8,128)(2,1)}, bf16[1024,2048]{1,0:T(8,128)(2,1)}, bf16[256,2048]{1,0:T(8,128)(2,1)}) custom-call(f32[256,2048]{1,0:T(8,128)} %get-tuple-element.55.grad_hidden.grad_hidden_in, bf16[256,2048]{1,0:T(8,128)(2,1)} %get-tuple-element.56.y_send, bf16[1024,2048]{1,0:T(8,128)(2,1)} %w_out.3, ...), custom_call_target="tpu_custom_call" | custom-call | flops 120000004096 | bytes 40000000 | tf_op jit(solution)/shard_map/retract/pallas_call | solution.py:1346
  330.6 0.0 reduce-scatter.7.cloned.1.call-done
  330.6 25.7 %pair_sum.1 = (bf16[4,1024,1024]{2,1,0:T(8,128)(2,1)}, bf16[512,1024]{1,0:T(8,128)(2,1)}) custom-call(bf16[1024,2048]{1,0:T(8,128)(2,1)} %bitcast.17, bf16[1024,3072]{1,0:T(8,128)(2,1)} %get-tuple-element.72.d_in, bf16[4,2,128,2048]{3,2,1,0:T(8,128)(2,1)} %bitcast.18, bf16[2,512,1024]{2,1,0:T(8,128)(2,1)} %bitcast.12), custom_call_target="tpu_custom_call" | custom-call | flops 24999999488 | bytes 30000000 | tf_op jit(solution)/shard_map/pair_sum/pallas_call | solution.py:1531
  356.3 0.0 copy-start
  356.3 0.0 copy-start.1
  356.4 0.0 reduce-scatter.9.cloned.1.call-update
  356.4 1.5 copy-done
  357.9 0.3 copy-done.1
  358.2 1.3 add_convert_fusion
  359.4 88.2 %finish.1 = (bf16[256,2048]{1,0:T(8,128)(2,1)}, f32[8,2048]{1,0:T(8,128)}, f32[256,1024]{1,0:T(8,128)}, f32[128,2048]{1,0:T(8,128)}) custom-call(bf16[1024,3072]{1,0:T(8,128)(2,1)} %get-tuple-element.72.d_in, bf16[4,256,2048]{2,1,0:T(8,128)(2,1)} %get-tuple-element.67.x_in, bf16[256,2048]{1,0:T(8,128)(2,1)} %tok_in.1, f32[1,2048]{1,0:T(1,128)} %bitcast.16, ...), custom_call_target="tpu_custom_call" | custom-call | flops 109999996928 | bytes 30000000 | tf_op jit(solution)/shard_map/finish/pallas_call | solution.py:1799
  447.7 2.5 reduce-scatter.9.cloned.1.call-done
  450.2 1.5 fusion
  451.8 5.5 %unpack.1 = (f32[256,512]{1,0:T(8,128)}, f32[256,512]{1,0:T(8,128)}, f32[256,1024]{1,0:T(8,128)}, f32[256,1024]{1,0:T(8,128)}, f32[128,2048]{1,0:T(8,128)}, /*in...) custom-call(bf16[1024,1024]{1,0:T(8,128)(2,1)} %bitcast.9, ...), custom_call_target="tpu_custom_call" | custom-call | tf_op jit(solution)/shard_map/unpack/pallas_call | solution.py:1868
Async XLA Ops:
  7.2 323.4 %reduce-scatter.7.cloned.1.call-start = ((), (), s32[]{:S(2)}) async-start(), calls=%async_computation.2 | async-start | bytes 10485760
  232.9 217.4 %reduce-scatter.9.cloned.1.call-start = ((), (), s32[]{:S(2)}) async-start(), calls=%async_computation.3 | async-start | bytes 10485760
  356.3 1.6 copy-start
  356.3 1.8 copy-start.1
Sparse Core Ops, SparseCore 0:
  233.0 84.4 reduce-scatter.6
  356.5 93.6 reduce-scatter.8

commit v8 on v7

--- a/solution.py
+++ b/solution.py
@@ -1843,7 +1843,9 @@
     )(d, x, tok, gain, gain_part, grad_hidden, w_query, w_key, w_value, w_gate, far, far_got)
 
 
-def unpack_kernel(summed, tok, up, down, query, key, value, gate, out, tok_out, up_out, down_out):
+def unpack_kernel(
+    summed, tok, up, down, y_keep, y_got, query, key, value, gate, out, tok_out, up_out, down_out, output
+):
     f32 = jnp.float32
     rows, wide = query.shape
     few, tall = out.shape[0], value.shape[1]
@@ -1857,9 +1859,10 @@
     tok_out[...] = tok[...]
     up_out[...] = up[...]
     down_out[...] = down[...]
-
-
-def unpack(summed, tok, up, down, wide):
+    output[...] = (y_keep[...] + y_got[...].astype(f32)).astype(output.dtype)
+
+
+def unpack(summed, tok, up, down, y_keep, y_got, wide):
     f32 = jnp.float32
     count = lax.axis_size("seq")
     width, tall = tok.shape[1], summed.shape[1]
@@ -1868,10 +1871,10 @@
     return pl.pallas_call(
         unpack_kernel,
         out_shape=[jax.ShapeDtypeStruct(one, f32) for one in shapes]
-        + [jax.ShapeDtypeStruct(a.shape, a.dtype) for a in (tok, up, down)],
+        + [jax.ShapeDtypeStruct(a.shape, a.dtype) for a in (tok, up, down, y_got)],
         compiler_params=pltpu.CompilerParams(vmem_limit_bytes=LIMIT),
         name="unpack",
-    )(summed, tok, up, down)
+    )(summed, tok, up, down, y_keep, y_got)
 
 
 def shards(
@@ -1909,7 +1912,6 @@
     grad_in, grad_out_w, y_got = retract(
         grad_hidden, y_send, w_out, q_all, k_all, v_all, gate, unit, gated, inverse, weights, entering, *trig
     )
-    output = (y_keep + y_got.astype(f32)).astype(bf16)
     pairs, far_got = pair_sum(x_rows.reshape(span_rows, -1), grad_in, grad_out_w, far)
     summed = lax.psum_scatter(
         pairs, "seq", scatter_dimension=0, tiled=False, axis_index_groups=same_core()
@@ -1929,7 +1931,8 @@
         grad_tokens,
         final_up,
         final_down,
-    ) = unpack(summed, grad_tokens, final_up, final_down, w_query.shape[1])
+        output,
+    ) = unpack(summed, grad_tokens, final_up, final_down, y_keep, y_got, w_query.shape[1])
     return (
         output,
         grad_tokens,

time: 464 us -> 466 us (level)
  no operation moved by 1% of the time
where the time goes in v8:
time: 466 us; the launch traced here: 465 us
  Pallas kernels  444 us (95%)
  between operations  14.1 us (3%)
  waiting for transfers between devices  5.91 us (1%)
    pallas_call x1, Pallas kernels, attend(): pl.pallas_call(attend_kernel, out_shape=[jax.ShapeDtypeStruct(*one) for o...  168 us
    pallas_call x1, Pallas kernels, retract(): pl.pallas_call(retract_kernel, out_shape=[jax.ShapeDtypeStruct((span, 2 *...  97.6 us
    pallas_call x1, Pallas kernels, finish(): pl.pallas_call(finish_kernel, out_shape=[jax.ShapeDtypeStruct((rows, widt...  88 us
    pallas_call x1, Pallas kernels, feed(): pl.pallas_call(feed_kernel, out_shape=[jax.ShapeDtypeStruct((rows, width)...  57.4 us
    pallas_call x1, Pallas kernels, pair_sum(): pl.pallas_call(pair_kernel, out_shape=[jax.ShapeDtypeStruct((chips, high,...  25.9 us
  transfers between devices with their start and end apart: 2, of which 1 were waited for; matrix products, arithmetic and copies ran while one was open for 0% of the time, Pallas kernels for 40%

profile of v8, /device:TPU:0, one launch (start us, length us, event | category | flops | bytes accessed | tf_op | source)
XLA Modules:
  0.0 465.4 jit_solution(7741118795594811642)
XLA Ops:
  7.2 0.0 reduce-scatter.7.cloned.1.call-start
  7.2 168.2 %attend.1 = (bf16[4,256,2048]{2,1,0:T(8,128)(2,1)}, bf16[1024,512]{1,0:T(8,128)(2,1)}, bf16[1024,512]{1,0:T(8,128)(2,1)}, bf16[1024,1024]{1,0:T(8,128)(2,1)}, f3...) custom-call(bf16[256,2048]{1,0:T(8,128)(2,1)} %tok_in.1, ...), custom_call_target="tpu_custom_call" | custom-call | flops 190000005120 | bytes 60000000 | tf_op jit(solution)/shard_map/attend/pallas_call | solution.py:693
  175.5 57.4 %feed.1 = (f32[256,2048]{1,0:T(8,128)}, bf16[256,2048]{1,0:T(8,128)(2,1)}, f32[256,2048]{1,0:T(8,128)}, f32[1,2048]{1,0:T(1,128)}, bf16[4,2,512,1024]{3,2,1,0:T(8,128)(2,1)}) custom-call(f32[256,2048]{1,0:T(8,128)} %get-tuple-element.52.hidden, f32[1,2048]{1,0:T(1,128)} %bitcast.14, bf16[256,2048]{1,0:T(8,128)(2,1)} %cot.3, ...), custom_call_target="tpu_custom_call" | custom-call | flops 74999996416 | bytes 30000000 | tf_op jit(solution)/shard_map/feed/pallas_call | solution.py:1027
  232.8 0.0 reduce-scatter.7.cloned.1.call-update
  232.9 0.0 reduce-scatter.9.cloned.1.call-start
  232.9 97.6 %retract.1 = (bf16[1024,3072]{1,0:T(8,128)(2,1)}, bf16[1024,2048]{1,0:T(8,128)(2,1)}, bf16[256,2048]{1,0:T(8,128)(2,1)}) custom-call(f32[256,2048]{1,0:T(8,128)} %get-tuple-element.56.grad_hidden.grad_hidden_in, bf16[256,2048]{1,0:T(8,128)(2,1)} %get-tuple-element.57.y_send, bf16[1024,2048]{1,0:T(8,128)(2,1)} %w_out.3, ...), custom_call_target="tpu_custom_call" | custom-call | flops 120000004096 | bytes 40000000 | tf_op jit(solution)/shard_map/retract/pallas_call | solution.py:1346
  330.6 0.0 reduce-scatter.7.cloned.1.call-done
  330.6 25.9 %pair_sum.1 = (bf16[4,1024,1024]{2,1,0:T(8,128)(2,1)}, bf16[512,1024]{1,0:T(8,128)(2,1)}) custom-call(bf16[1024,2048]{1,0:T(8,128)(2,1)} %bitcast.17, bf16[1024,3072]{1,0:T(8,128)(2,1)} %get-tuple-element.71.d_in, bf16[4,2,128,2048]{3,2,1,0:T(8,128)(2,1)} %bitcast.18, bf16[2,512,1024]{2,1,0:T(8,128)(2,1)} %bitcast.12), custom_call_target="tpu_custom_call" | custom-call | flops 24999999488 | bytes 30000000 | tf_op jit(solution)/shard_map/pair_sum/pallas_call | solution.py:1531
  356.5 0.0 reduce-scatter.9.cloned.1.call-update
  356.5 88.0 %finish.1 = (bf16[256,2048]{1,0:T(8,128)(2,1)}, f32[8,2048]{1,0:T(8,128)}, f32[256,1024]{1,0:T(8,128)}, f32[128,2048]{1,0:T(8,128)}) custom-call(bf16[1024,3072]{1,0:T(8,128)(2,1)} %get-tuple-element.71.d_in, bf16[4,256,2048]{2,1,0:T(8,128)(2,1)} %get-tuple-element.51.x_in, bf16[256,2048]{1,0:T(8,128)(2,1)} %tok_in.1, f32[1,2048]{1,0:T(1,128)} %bitcast.16, ...), custom_call_target="tpu_custom_call" | custom-call | flops 109999996928 | bytes 30000000 | tf_op jit(solution)/shard_map/finish/pallas_call | solution.py:1799
  444.5 5.9 %reduce-scatter.9.cloned.1.call-done = bf16[1,1024,1024]{2,1,0:T(8,128)(2,1)} async-done(((bf16[4,1024,1024]{2,1,0:T(8,128)(2,1)}), bf16[1,1024,1024]{2,1,0:T(8,128)(2,1)}) %reduce-scatter.9.cloned.1.call-update) | async-done | bytes 2097168
  450.3 1.5 fusion
  451.9 6.7 %unpack.1 = (f32[256,512]{1,0:T(8,128)}, f32[256,512]{1,0:T(8,128)}, f32[256,1024]{1,0:T(8,128)}, f32[256,1024]{1,0:T(8,128)}, f32[128,2048]{1,0:T(8,128)}, /*in...) custom-call(bf16[1024,1024]{1,0:T(8,128)(2,1)} %bitcast.9, ...), custom_call_target="tpu_custom_call" | custom-call | tf_op jit(solution)/shard_map/unpack/pallas_call | solution.py:1871
Async XLA Ops:
  7.2 323.4 %reduce-scatter.7.cloned.1.call-start = ((), (), s32[]{:S(2)}) async-start(), calls=%async_computation.2 | async-start | bytes 10485760
  232.9 217.5 %reduce-scatter.9.cloned.1.call-start = ((), (), s32[]{:S(2)}) async-start(), calls=%async_computation.3 | async-start | bytes 10485760
Sparse Core Ops, SparseCore 0:
  233.0 84.5 reduce-scatter.6
  356.6 93.6 reduce-scatter.8
